TPU v7x, 128 devices: a whole 4x4x4 slice. The times are simulated.
128 devices in a mesh: lvl: 4 (over y_hi, core), lat: 32 (over z, x, y_lo).
Axes of the slice: x: 4, y: 4 (y_hi: 2, y_lo: 2; y = y_hi * 2 + y_lo), z: 4, core: 2. Of those that a mesh axis runs over, the one named last changes fastest.
Arguments:
- tokens: bfloat16 [8, 192, 144, 384], P('lvl', 'lat'), may hold values from -60 to 60
- targets: bfloat16 [8, 192, 144, 160], P('lvl', 'lat'), may hold values from -6 to 6
- relief: int32 [192, 144], replicated, may hold values from 0 to 3
- earth_bias: float32 [4, 32, 12, 144, 144], P('lvl', 'lat'), may hold values from -4 to 300
- relief_table: bfloat16 [4, 384], replicated, may hold values from -3 to 3
- gain_attn: float32 [384], replicated, may hold values from 0.5 to 1.5
- gain_mlp: float32 [384], replicated, may hold values from 0.5 to 1.5
- w_qkv: bfloat16 [384, 1152], replicated, may hold values from -0.3125 to 0.3125
- w_proj: bfloat16 [384, 384], replicated, may hold values from -0.3125 to 0.3125
- w_up: bfloat16 [384, 1536], replicated, may hold values from -0.3125 to 0.3125
- w_down: bfloat16 [1536, 384], replicated, may hold values from -0.15625 to 0.15625
- w_out: bfloat16 [384, 160], replicated, may hold values from -0.3125 to 0.3125
- var_weight: float32 [5], replicated, may hold values from 0.5 to 4
Outputs:
- loss: float32 [], replicated
- grad_qkv: float32 [384, 1152], P(('lvl', 'lat'))
- grad_proj: float32 [384, 384], P(('lvl', 'lat'))
- grad_up: float32 [384, 1536], P(('lvl', 'lat'))
- grad_down: float32 [1536, 384], P(('lvl', 'lat'))
- grad_out: float32 [384, 160], P(('lvl', 'lat'))
- grad_gain_attn: float32 [384], P(('lvl', 'lat'))
- grad_gain_mlp: float32 [384], P(('lvl', 'lat'))
- grad_relief: float32 [384, 4], P(('lvl', 'lat'))
- grad_bias: float32 [4, 32, 12, 144, 144], P('lvl', 'lat')
All inputs are finite; a program needn't handle non-finite values.
Results may differ from a plain program's by a relative error of at most 0.022.
Values may be sent and summed in bfloat16 or wider, within the bound.
No kernel may reach another device: no remote copies, remote signals or barrier semaphores. Data moves between devices by JAX's collectives and lax.ppermute only.
A program may use at most 256 MiB of HBM per device.

v0:
```python
import math

import jax
import jax.numpy as jnp
from jax import lax
from jax.sharding import PartitionSpec as P

WIN_LON = 12


norm_eps = 1e-05
loss_scale = 32768.0
smooth_sq = 0.01
masked_score = -1e30
windows_together = 4


def passed_along(value, axis, by):
    count = lax.axis_size(axis)
    return lax.ppermute(value, axis, [(i, (i + by) % count) for i in range(count)])


def mult(formula, left_op, right_op):
    return jnp.einsum(formula, left_op, right_op, preferred_element_type=jnp.float32)


def exact_mult(formula, left_op, right_op):
    return jnp.einsum(formula, left_op, right_op, precision=lax.Precision.HIGHEST)


def ln_gain(values, gain_vec):
    centre = jnp.mean(values, -1, keepdims=True)
    spread = jnp.mean((values - centre) ** 2, -1, keepdims=True)
    return (values - centre) * lax.rsqrt(spread + norm_eps) * gain_vec


def gelu_exact(values):
    return jax.nn.gelu(values, approximate=False)


def lat_weights(row_ids, lat_rows):
    fine_rows = 4 * row_ids[:, None] + jnp.arange(4, dtype=jnp.int32)[None, :]
    angle_rad = (90.0 - 180.0 * (fine_rows.astype(jnp.float32) + 0.5) / (4.0 * lat_rows)) * (
        math.pi / 180.0
    )
    return jnp.cos(angle_rad)


def cell_weights(level_ids, row_ids, relief_rows, var_weight, lat_rows):
    lat_weight = lat_weights(row_ids, lat_rows)
    levels = 2 * level_ids[:, None] + jnp.arange(2, dtype=jnp.int32)[None, :]
    valid_cells = (levels[:, None, None, :] >= relief_rows[None, :, :, None]).astype(jnp.float32)
    var_count = var_weight.shape[0]
    slots_n, rows_n, lon_n = (valid_cells.shape[0], valid_cells.shape[1], valid_cells.shape[2])
    weight_grid = (
        var_weight[None, None, None, :, None, None, None]
        * valid_cells[:, :, :, None, :, None, None]
        * lat_weight[None, :, None, None, None, :, None]
    )
    weight_grid = jnp.broadcast_to(weight_grid, (slots_n, rows_n, lon_n, var_count, 2, 4, 4))
    return weight_grid.reshape(slots_n, rows_n, lon_n, var_count * 32)


def weight_total(relief, var_weight, level_count):
    lat_rows = relief.shape[0]
    lat_weight = jnp.sum(lat_weights(jnp.arange(lat_rows, dtype=jnp.int32), lat_rows), 1)
    live_levels = (2 * level_count - relief).astype(jnp.float32)
    return jnp.sum(var_weight) * 4.0 * jnp.sum(lat_weight[:, None] * live_levels)


def window_mask(last_level, last_band, slots_n, rows_n, win_lon):
    slot_label = jnp.where(last_level & (jnp.arange(slots_n) >= slots_n // 2), 2, 0)
    row_label = jnp.where(last_band & (jnp.arange(rows_n) >= rows_n // 2), 1, 0)
    labels = (
        slot_label[:, None, None] + row_label[None, :, None] + jnp.zeros((1, 1, win_lon), jnp.int32)
    )
    labels = labels.reshape(-1)
    return labels[:, None] == labels[None, :]


def windows(field_in):
    slots_n, rows_n, lon_n, chans = field_in.shape
    count_w = lon_n // WIN_LON
    parted = field_in.reshape(slots_n, rows_n, count_w, WIN_LON, chans).transpose(2, 0, 1, 3, 4)
    return parted.reshape(count_w, slots_n * rows_n * WIN_LON, chans)


def unwindows(win_in, slots_n, rows_n):
    count_w, tokens_n, chans = win_in.shape
    parted = win_in.reshape(count_w, slots_n, rows_n, WIN_LON, chans).transpose(1, 2, 0, 3, 4)
    return parted.reshape(slots_n, rows_n, count_w * WIN_LON, chans)


def roll_blocks(field_in, step_dir):
    slots_n, rows_n = (field_in.shape[0], field_in.shape[1])
    half_rows = rows_n // 2
    slot_piece = field_in[:1] if step_dir < 0 else field_in[slots_n - 1 :]
    slot_come = passed_along(slot_piece, "lvl", step_dir)
    if step_dir < 0:
        level_done = jnp.concatenate([field_in[1:], slot_come], 0)
    else:
        level_done = jnp.concatenate([slot_come, field_in[: slots_n - 1]], 0)
    row_piece = level_done[:, :half_rows] if step_dir < 0 else level_done[:, rows_n - half_rows :]
    row_come = passed_along(row_piece, "lat", step_dir)
    if step_dir < 0:
        band_done = jnp.concatenate([level_done[:, half_rows:], row_come], 1)
    else:
        band_done = jnp.concatenate([row_come, level_done[:, : rows_n - half_rows]], 1)
    return jnp.roll(band_done, step_dir * (WIN_LON // 2), 2)


def roll_ahead(field_in):
    return roll_blocks(field_in, -1)


def roll_behind(field_in):
    return roll_blocks(field_in, 1)


def split_heads(qkv_all, heads_n):
    groups_n, tokens_n, three_d = qkv_all.shape
    model_d = three_d // 3
    head_d = model_d // heads_n
    query_h = qkv_all[..., :model_d].reshape(groups_n, tokens_n, heads_n, head_d)
    key_h = qkv_all[..., model_d : 2 * model_d].reshape(groups_n, tokens_n, heads_n, head_d)
    value_h = qkv_all[..., 2 * model_d :].reshape(groups_n, tokens_n, heads_n, head_d)
    return (query_h, key_h, value_h, head_d ** (-0.5))


def attend(qkv_all, bias_blk, allowed):
    query_h, key_h, value_h, factor = split_heads(qkv_all, bias_blk.shape[0])
    groups_n, tokens_n = (qkv_all.shape[0], qkv_all.shape[1])
    scores = mult("gqhe,gkhe->ghqk", query_h, key_h) * factor + bias_blk[None]
    scores = jnp.where(allowed[None, None], scores, masked_score)
    top_row = jnp.max(scores, -1, keepdims=True)
    exp_scores = jnp.exp(scores - top_row)
    attn_prob = exp_scores / jnp.sum(exp_scores, -1, keepdims=True)
    attended = mult("ghqk,gkhe->gqhe", attn_prob.astype(jnp.bfloat16), value_h).astype(jnp.bfloat16)
    return (attended.reshape(groups_n, tokens_n, -1), attn_prob)


def attend_back(qkv_all, attn_prob, grad_att):
    heads_n = attn_prob.shape[1]
    query_h, key_h, value_h, factor = split_heads(qkv_all, heads_n)
    groups_n, tokens_n = (qkv_all.shape[0], qkv_all.shape[1])
    grad_h = grad_att.reshape(query_h.shape)
    prob_b = attn_prob.astype(jnp.bfloat16)
    grad_prob = mult("gqhe,gkhe->ghqk", grad_h, value_h)
    grad_value = mult("ghqk,gqhe->gkhe", prob_b, grad_h).astype(jnp.bfloat16)
    grad_score = attn_prob * (grad_prob - jnp.sum(grad_prob * attn_prob, -1, keepdims=True))
    score_b = grad_score.astype(jnp.bfloat16)
    grad_query = (mult("ghqk,gkhe->gqhe", score_b, key_h) * factor).astype(jnp.bfloat16)
    grad_key = (mult("ghqk,gqhe->gkhe", score_b, query_h) * factor).astype(jnp.bfloat16)
    grad_heads = jnp.concatenate(
        [
            grad_query.reshape(groups_n, tokens_n, -1),
            grad_key.reshape(groups_n, tokens_n, -1),
            grad_value.reshape(groups_n, tokens_n, -1),
        ],
        -1,
    )
    return (grad_heads, jnp.sum(grad_score, 0))


def tail(stream, branch, targ_blk, cell_w, gain_mlp, w_up, w_down, w_out, inv_total):
    stream2 = stream + branch.astype(jnp.float32)
    normed2 = ln_gain(stream2, gain_mlp).astype(jnp.bfloat16)
    pre_act = mult("zrwd,df->zrwf", normed2, w_up)
    hidden = gelu_exact(pre_act).astype(jnp.bfloat16)
    output_field = (stream2 + mult("zrwf,fd->zrwd", hidden, w_down)).astype(jnp.bfloat16)
    prediction = mult("zrwd,do->zrwo", output_field, w_out)
    differ = prediction - targ_blk.astype(jnp.float32)
    smooth_err = jnp.sqrt(differ * differ + smooth_sq)
    numerator = jnp.sum(cell_w * smooth_err)
    grad_pred = (inv_total * cell_w * differ / smooth_err).astype(jnp.bfloat16)
    grad_out = mult("zrwd,zrwo->do", output_field, grad_pred)
    grad_field = mult("zrwo,do->zrwd", grad_pred, w_out)
    grad_field_b = grad_field.astype(jnp.bfloat16)
    grad_down = mult("zrwf,zrwd->fd", hidden, grad_field_b)
    grad_hidden = mult("zrwd,fd->zrwf", grad_field_b, w_down)
    gelu_val, gelu_back = jax.vjp(gelu_exact, pre_act)
    grad_pre = gelu_back(grad_hidden)[0].astype(jnp.bfloat16)
    grad_up = mult("zrwd,zrwf->df", normed2, grad_pre)
    grad_normed2 = mult("zrwf,df->zrwd", grad_pre, w_up)
    ln_val, ln_back = jax.vjp(ln_gain, stream2, gain_mlp)
    grad_ln, grad_gain_mlp = ln_back(grad_normed2)
    grad_stream2 = grad_field + grad_ln
    return (
        numerator,
        grad_stream2,
        grad_stream2.astype(jnp.bfloat16),
        (grad_up, grad_down, grad_out, grad_gain_mlp),
    )


def forward_backward(
    tok_blk, targ_blk, relief_blk, cell_w, bias_blk, allowed, params, inv_total, turn_in, turn_out
):
    relief_table, gain_attn, gain_mlp, w_qkv, w_proj, w_up, w_down, w_out = params
    slots_n, rows_n = (tok_blk.shape[0], tok_blk.shape[1])
    one_hot = (relief_blk[:, :, None] == jnp.arange(relief_table.shape[0], dtype=jnp.int32)).astype(
        jnp.float32
    )
    stream = (
        tok_blk.astype(jnp.float32)
        + exact_mult("rwc,cd->rwd", one_hot, relief_table.astype(jnp.float32))[None]
    )
    normed = ln_gain(stream, gain_attn).astype(jnp.bfloat16)
    win_in = windows(turn_in(normed))
    qkv_all = mult("nqd,de->nqe", win_in, w_qkv).astype(jnp.bfloat16)
    count_w, tokens_n, three_d = qkv_all.shape
    group_count = count_w // windows_together
    grouped = qkv_all.reshape(group_count, windows_together, tokens_n, three_d)

    def attend_group(group_qkv):
        return attend(group_qkv, bias_blk, allowed)

    attended_g, prob_g = lax.map(attend_group, grouped)
    attended = attended_g.reshape(count_w, tokens_n, -1)
    mixed = mult("nqd,de->nqe", attended, w_proj).astype(jnp.bfloat16)
    branch = turn_out(unwindows(mixed, slots_n, rows_n))
    numerator, grad_stream2, grad_branch, tail_grads = tail(
        stream, branch, targ_blk, cell_w, gain_mlp, w_up, w_down, w_out, inv_total
    )
    grad_mixed = windows(turn_in(grad_branch))
    grad_proj = mult("nqd,nqe->de", attended, grad_mixed)
    grad_att = mult("nqe,de->nqd", grad_mixed, w_proj).astype(jnp.bfloat16)

    def back_group(group_in):
        return attend_back(group_in[0], group_in[1], group_in[2])

    grad_heads_g, grad_bias_g = lax.map(
        back_group, (grouped, prob_g, grad_att.reshape(group_count, windows_together, tokens_n, -1))
    )
    grad_heads = grad_heads_g.reshape(count_w, tokens_n, three_d)
    grad_bias = jnp.sum(grad_bias_g, 0)
    grad_qkv = mult("nqd,nqe->de", win_in, grad_heads)
    grad_shifted = mult("nqe,de->nqd", grad_heads, w_qkv).astype(jnp.bfloat16)
    grad_normed = turn_out(unwindows(grad_shifted, slots_n, rows_n))
    ln_val, ln_back = jax.vjp(ln_gain, stream, gain_attn)
    grad_front, grad_gain_attn = ln_back(grad_normed.astype(jnp.float32))
    grad_stream = grad_stream2 + grad_front
    grad_relief = exact_mult("rwc,zrwd->dc", one_hot, grad_stream)
    grad_up, grad_down, grad_out, grad_gain_mlp = tail_grads
    return (
        numerator,
        (
            grad_qkv,
            grad_proj,
            grad_up,
            grad_down,
            grad_out,
            grad_gain_attn,
            grad_gain_mlp,
            grad_relief,
        ),
        grad_bias,
    )


def body(
    tokens,
    targets,
    relief,
    earth_bias,
    relief_table,
    gain_attn,
    gain_mlp,
    w_qkv,
    w_proj,
    w_up,
    w_down,
    w_out,
    var_weight,
):
    lvl_count = lax.axis_size("lvl")
    lat_count = lax.axis_size("lat")
    lvl_id = lax.axis_index("lvl")
    lat_id = lax.axis_index("lat")
    slots_dev, rows_dev, lon_cells, model_d = tokens.shape
    level_total = slots_dev * lvl_count
    lat_rows = rows_dev * lat_count
    weight_sum = weight_total(relief, var_weight, level_total)
    inv_total = loss_scale / weight_sum
    allowed = window_mask(
        lvl_id == lvl_count - 1, lat_id == lat_count - 1, slots_dev, rows_dev, WIN_LON
    )
    tok_in, targ_in = (tokens, targets)
    level_shift, row_shift, lon_shift = (0, 0, 0)
    turn_in, turn_out = (roll_ahead, roll_behind)
    level_ids = (
        lvl_id * slots_dev + jnp.arange(slots_dev, dtype=jnp.int32) + level_shift
    ) % level_total
    row_ids = (lat_id * rows_dev + jnp.arange(rows_dev, dtype=jnp.int32) + row_shift) % lat_rows
    lon_ids = (jnp.arange(lon_cells, dtype=jnp.int32) + lon_shift) % lon_cells
    relief_blk = jnp.take(jnp.take(relief, row_ids, axis=0), lon_ids, axis=1)
    cell_w = cell_weights(level_ids, row_ids, relief_blk, var_weight, lat_rows)
    params = (relief_table, gain_attn, gain_mlp, w_qkv, w_proj, w_up, w_down, w_out)
    numerator, grad_set, grad_bias = forward_backward(
        tok_in,
        targ_in,
        relief_blk,
        cell_w,
        earth_bias[0, 0],
        allowed,
        params,
        inv_total,
        turn_in,
        turn_out,
    )
    pieces_all = grad_set + ()
    summed = lax.psum_scatter(pieces_all, ("lvl", "lat"), scatter_dimension=0, tiled=True)
    loss_value = lax.psum(numerator, ("lvl", "lat")) / weight_sum
    return (
        loss_value,
        summed[0],
        summed[1],
        summed[2],
        summed[3],
        summed[4],
        summed[5],
        summed[6],
        summed[7],
        grad_bias[None, None],
    )


def solution(mesh):
    placed = (
        P("lvl", "lat", None, None),
        P("lvl", "lat", None, None),
        P(),
        P("lvl", "lat", None, None, None),
        P(),
        P(),
        P(),
        P(),
        P(),
        P(),
        P(),
        P(),
        P(),
    )
    return jax.shard_map(
        body,
        mesh=mesh,
        in_specs=placed,
        out_specs=(
            P(),
            P(("lvl", "lat"), None),
            P(("lvl", "lat"), None),
            P(("lvl", "lat"), None),
            P(("lvl", "lat"), None),
            P(("lvl", "lat"), None),
            P(("lvl", "lat")),
            P(("lvl", "lat")),
            P(("lvl", "lat"), None),
            P("lvl", "lat", None, None, None),
        ),
        check_vma=False,
    )
```

profile of v0, /device:TPU:0, one launch (start us, length us, event | category | flops | bytes accessed | tf_op | source)
XLA Modules:
  0.0 967.1 jit_solution(13102936706999248473)
XLA Ops:
  19.3 8.5 collective-permute-done
  41.1 11.9 %collective-permute-done.1 = bf16[2,3,144,384]{3,2,1,0:T(8,128)(2,1)} collective-permute-done((bf16[2,3,144,384]{3,2,1,0:T(8,128)(2,1)}, bf16[2,3,144,384]{3,2,1,0:T(8,128)(2,1)}, u32[]{:S(2)}, u32[]{:S(2)}) %collective-permute-start.1) | collective-permute-done | bytes 663584 | tf_op jit(solution)/shard_map/ppermute | solution.py:20
  67.1 8.3 copy.157
  75.4 58.2 %while.26 = (s32[]{:T(128)}, bf16[3,4,144,384]{2,3,1,0:T(8,128)(2,1)}, f32[3,4,12,144,144]{3,4,2,1,0:T(8,128)}, bf16[3,4,144,1152]{2,3,1,0:T(8,128)(2,1)}, f32[1...) while((s32[]{:T(128)}, bf16[3,4,144,384]{2,3,1,0:T(8,128)(2,1)}, ...), condition=%wide.region_5.6_spmd.clone, body=%wide.region_2.5_spmd.clone.sunk | while | flops 135606672 | bytes 47471788 | solution.py:218
  78.6 7.7 fusion.171
  98.0 7.7 fusion.171
  117.5 7.7 fusion.171
  148.7 9.0 collective-permute-done.2
  169.0 9.2 collective-permute-done.3
  188.5 25.2 %multiply_convert_fusion.2 = (bf16[2,6,144,1536]{3,2,1,0:T(8,128)(2,1)S(1)}, f32[2,6,144,1536]{3,2,1,0:T(8,128)}) fusion(f32[2,6,144,1536]{3,2,1,0:T(8,128)S(1)} %get-tuple-element.252, u8[2,144,1536]{2,1,0:T(8,128)(4,1)S(1)} %get-tuple-element.176, u8[2,144,1536]{2,1,0:T(8,128)(4,1)S(1)} %get-tuple-element.175), kind=kLoop, calls=%fused_computation.46 | loop fusion | flops 185794560 | bytes 27426816 | tf_op jit(solution)/shard_map/convert_element_type | solution.py:169
  223.1 10.0 %add_convert_fusion = bf16[2,6,144,1536]{3,2,1,0:T(8,128)(2,1)} fusion(f32[2,6,144,1536]{3,2,1,0:T(8,128)} %get-tuple-element.219, f32[2,6,144,1536]{3,2,1,0:T(8,128)S(1)} %get-tuple-element.252, bf16[2,6,144,384]{3,2,1,0:T(8,128)(2,1)S(1)} %get-tuple-element.253, bf16[1536,384]{1,0:T(8,128)(2,1)} %param.27), kind=kOutput, calls=%fused_computation.45 | convolution fusion | flops 2075590656 | bytes 29048832 | tf_op jit(solution)/shard_map/zrwd,fd->zrwf/dot_general | solution.py:24
  249.6 18.5 %collective-permute-done.4 = bf16[1,6,144,384]{3,2,1,0:T(8,128)(2,1)S(1)} collective-permute-done((bf16[1,6,144,384]{3,2,1,0:T(8,128)(2,1)S(1)}, bf16[1,6,144,384]{3,2,1,0:T(8,128)(2,1)S(1)}, u32[]{:S(2)}, u32[]{:S(2)}) %collective-permute-start.4) | collective-permute-done | bytes 663584 | tf_op jit(solution)/shard_map/ppermute | solution.py:20
  272.9 12.6 %collective-permute-done.5 = bf16[2,3,144,384]{3,2,1,0:T(8,128)(2,1)S(1)} collective-permute-done((bf16[2,3,144,384]{3,2,1,0:T(8,128)(2,1)S(1)}, bf16[2,3,144,384]{3,2,1,0:T(8,128)(2,1)S(1)}, u32[]{:S(2)}, u32[]{:S(2)}) %collective-permute-start.5) | collective-permute-done | bytes 663584 | tf_op jit(solution)/shard_map/ppermute | solution.py:20
  294.8 85.6 %while.25 = (s32[]{:T(128)}, bf16[3,4,144,1152]{2,3,1,0:T(8,128)(2,1)}, f32[3,12,144,144]{2,3,1,0:T(8,128)}, bf16[3,4,144,1152]{2,3,1,0:T(8,128)(2,1)}, f32[3,4,...) while((s32[]{:T(128)}, bf16[3,4,144,1152]{2,3,1,0:T(8,128)(2,1)}, ...), condition=%wide.region_19.20_spmd, body=%wide.region_16.19_spmd.sunk | while | flops 265607424 | bytes 43556444 | solution.py:232
  300.0 7.1 fusion.163
  307.0 7.1 fusion.164
  335.5 7.2 fusion.164
  364.2 7.1 fusion.164
  380.4 8.1 convolution_convert_fusion.1
  413.2 349.8 %fusion.2 = f32[16,384]{1,0:T(8,128)S(1)} fusion(f32[1536,384]{1,0:T(8,128)} %fusion.42), kind=kCustom, calls=%all-reduce-scatter | all-reduce-scatter fusion | flops 786433 | bytes 2383872
  774.2 10.8 %collective-permute-start.17 = (f32[16,384]{1,0:T(8,128)S(1)}, f32[16,384]{1,0:T(8,128)S(1)}, u32[]{:S(2)}, u32[]{:S(2)}) collective-permute-start(f32[16,384]{1,0:T(8,128)S(1)} %fusion.2), channel_id=1, source_target_pairs={{0,10},{1,11},{2,12},{3,13},{4,14},{5,15},{6,16},{7,17},{8,18},{9,... | collective-permute-start | bytes 73736
  792.5 15.5 %collective-permute-start.21 = (f32[16,384]{1,0:T(8,128)S(1)}, f32[16,384]{1,0:T(8,128)S(1)}, u32[]{:S(2)}, u32[]{:S(2)}) collective-permute-start(f32[16,384]{1,0:T(8,128)S(1)} %fusion.2), channel_id=1, source_target_pairs={{0,14},{1,15},{2,16},{3,17},{4,18},{5,19},{6,20},{7,21},{8,22},{9,... | collective-permute-start | bytes 73736
  809.3 7.2 collective-permute-start.23
  880.3 70.5 %all-reduce.9 = (f32[]{:T(128)}, f32[384]{0:T(512)S(1)}, f32[384]{0:T(512)S(1)}, f32[384,4]{1,0:T(8,128)S(1)}) all-reduce(f32[]{:T(128)} %get-tuple-element.235, f32[384]{0:T(512)S(1)} %get-tuple-element.180, f32[384]{0:T(512)S(1)} %copy-done.29, ...), channel_id=1, replica_groups=mesh['lvl'=4,'lat'=32] {'lvl','lat'}, use_global_device_ids=true, to_apply=%region_9.10 | all-reduce | flops 2305 | bytes 18440 | tf_op jit(solution)/shard_map/psum | solution.py:313
  (315 shorter events, 321.4 us)
Async XLA Ops:
  7.2 946.1 %all-reduce.13.cloned.1.call-start = ((), (), s32[]{:S(2)}) async-start(), calls=%async_computation | async-start | bytes 10223616
  16.6 11.2 %collective-permute-start = (bf16[1,6,144,384]{3,2,1,0:T(8,128)(2,1)}, bf16[1,6,144,384]{3,2,1,0:T(8,128)(2,1)S(1)}, u32[]{:S(2)}, u32[]{:S(2)}) collective-permute-start(bf16[1,6,144,384]{3,2,1,0:T(8,128)(2,1)} %get-tuple-element.251), channel_id=1, source_target_pairs={{0,96},{32,0},{64,32},{96,64},{1,97},{33,1},{65,33},{97,65},{2,98}... | collective-permute-start | bytes 1990664 | tf_op jit(solution)/shard_map/ppermute | solution.py:20
  31.0 22.1 %collective-permute-start.1 = (bf16[2,3,144,384]{3,2,1,0:T(8,128)(2,1)}, bf16[2,3,144,384]{3,2,1,0:T(8,128)(2,1)}, u32[]{:S(2)}, u32[]{:S(2)}) collective-permute-start(bf16[2,3,144,384]{3,2,1,0:T(8,128)(2,1)} %get-tuple-element.249), channel_id=1, source_target_pairs={{0,31},{1,0},{2,1},{3,2},{4,3},{5,4},{6,5},{7,6},{8,7},{9,8},{10,9... | collective-permute-start | bytes 1990664 | tf_op jit(solution)/shard_map/ppermute | solution.py:20
  145.6 12.1 %collective-permute-start.2 = (bf16[1,6,144,384]{3,2,1,0:T(8,128)(2,1)}, bf16[1,6,144,384]{3,2,1,0:T(8,128)(2,1)}, u32[]{:S(2)}, u32[]{:S(2)}) collective-permute-start(bf16[1,6,144,384]{3,2,1,0:T(8,128)(2,1)} %slice.113), channel_id=1, source_target_pairs={{0,32},{32,64},{64,96},{96,0},{1,33},{33,65},{65,97},{97,1},{2,34}... | collective-permute-start | bytes 1990664 | tf_op jit(solution)/shard_map/ppermute | solution.py:20
  159.9 18.3 %collective-permute-start.3 = (bf16[2,3,144,384]{3,2,1,0:T(8,128)(2,1)}, bf16[2,3,144,384]{3,2,1,0:T(8,128)(2,1)}, u32[]{:S(2)}, u32[]{:S(2)}) collective-permute-start(bf16[2,3,144,384]{3,2,1,0:T(8,128)(2,1)} %get-tuple-element.246), channel_id=1, source_target_pairs={{0,1},{1,2},{2,3},{3,4},{4,5},{5,6},{6,7},{7,8},{8,9},{9,10},{10,1... | collective-permute-start | bytes 1990664 | tf_op jit(solution)/shard_map/ppermute | solution.py:20
  242.5 25.6 %collective-permute-start.4 = (bf16[1,6,144,384]{3,2,1,0:T(8,128)(2,1)S(1)}, bf16[1,6,144,384]{3,2,1,0:T(8,128)(2,1)S(1)}, u32[]{:S(2)}, u32[]{:S(2)}) collective-permute-start(bf16[1,6,144,384]{3,2,1,0:T(8,128)(2,1)S(1)} %get-tuple-element.245), channel_id=1, source_target_pairs={{0,96},{32,0},{64,32},{96,64},{1,97},{33,1},{65,33},{97,65},{2,98}... | collective-permute-start | bytes 1990664 | tf_op jit(solution)/shard_map/ppermute | solution.py:20
  268.3 17.2 %collective-permute-start.5 = (bf16[2,3,144,384]{3,2,1,0:T(8,128)(2,1)S(1)}, bf16[2,3,144,384]{3,2,1,0:T(8,128)(2,1)S(1)}, u32[]{:S(2)}, u32[]{:S(2)}) collective-permute-start(bf16[2,3,144,384]{3,2,1,0:T(8,128)(2,1)S(1)} %get-tuple-element.243), channel_id=1, source_target_pairs={{0,31},{1,0},{2,1},{3,2},{4,3},{5,4},{6,5},{7,6},{8,7},{9,8},{10,9... | collective-permute-start | bytes 1990664 | tf_op jit(solution)/shard_map/ppermute | solution.py:20
  392.3 11.9 %collective-permute-start.6 = (bf16[1,6,144,384]{3,2,1,0:T(8,128)(2,1)}, bf16[1,6,144,384]{3,2,1,0:T(8,128)(2,1)}, u32[]{:S(2)}, u32[]{:S(2)}) collective-permute-start(bf16[1,6,144,384]{3,2,1,0:T(8,128)(2,1)} %slice.127), channel_id=1, source_target_pairs={{0,32},{32,64},{64,96},{96,0},{1,33},{33,65},{65,97},{97,1},{2,34}... | collective-permute-start | bytes 1990664 | tf_op jit(solution)/shard_map/ppermute | solution.py:20
  406.5 462.8 %collective-permute-start.7 = (bf16[2,3,144,384]{3,2,1,0:T(8,128)(2,1)}, bf16[2,3,144,384]{3,2,1,0:T(8,128)(2,1)S(1)}, u32[]{:S(2)}, u32[]{:S(2)}) collective-permute-start(bf16[2,3,144,384]{3,2,1,0:T(8,128)(2,1)} %get-tuple-element.240), channel_id=1, source_target_pairs={{0,1},{1,2},{2,3},{3,4},{4,5},{5,6},{6,7},{7,8},{8,9},{9,10},{10,1... | collective-permute-start | bytes 1990664 | tf_op jit(solution)/shard_map/ppermute | solution.py:20
  770.3 14.7 %collective-permute-start.14 = (f32[16,384]{1,0:T(8,128)S(1)}, f32[16,384]{1,0:T(8,128)S(1)}, u32[]{:S(2)}, u32[]{:S(2)}) collective-permute-start(f32[16,384]{1,0:T(8,128)S(1)} %fusion.2), channel_id=1, source_target_pairs={{0,7},{1,8},{2,9},{3,10},{4,11},{5,12},{6,13},{7,14},{8,15},{9,16}... | collective-permute-start | bytes 73736
  771.6 16.9 %collective-permute-start.15 = (f32[16,384]{1,0:T(8,128)S(1)}, f32[16,384]{1,0:T(8,128)S(1)}, u32[]{:S(2)}, u32[]{:S(2)}) collective-permute-start(f32[16,384]{1,0:T(8,128)S(1)} %fusion.2), channel_id=1, source_target_pairs={{0,8},{1,9},{2,10},{3,11},{4,12},{5,13},{6,14},{7,15},{8,16},{9,17... | collective-permute-start | bytes 73736
  772.9 17.2 %collective-permute-start.16 = (f32[16,384]{1,0:T(8,128)S(1)}, f32[16,384]{1,0:T(8,128)S(1)}, u32[]{:S(2)}, u32[]{:S(2)}) collective-permute-start(f32[16,384]{1,0:T(8,128)S(1)} %fusion.2), channel_id=1, source_target_pairs={{0,9},{1,10},{2,11},{3,12},{4,13},{5,14},{6,15},{7,16},{8,17},{9,1... | collective-permute-start | bytes 73736
  774.2 18.2 %collective-permute-start.17 = (f32[16,384]{1,0:T(8,128)S(1)}, f32[16,384]{1,0:T(8,128)S(1)}, u32[]{:S(2)}, u32[]{:S(2)}) collective-permute-start(f32[16,384]{1,0:T(8,128)S(1)} %fusion.2), channel_id=1, source_target_pairs={{0,10},{1,11},{2,12},{3,13},{4,14},{5,15},{6,16},{7,17},{8,18},{9,... | collective-permute-start | bytes 73736
  785.1 22.9 %collective-permute-start.18 = (f32[16,384]{1,0:T(8,128)S(1)}, f32[16,384]{1,0:T(8,128)S(1)}, u32[]{:S(2)}, u32[]{:S(2)}) collective-permute-start(f32[16,384]{1,0:T(8,128)S(1)} %fusion.2), channel_id=1, source_target_pairs={{0,11},{1,12},{2,13},{3,14},{4,15},{5,16},{6,17},{7,18},{8,19},{9,... | collective-permute-start | bytes 73736
  788.5 20.8 %collective-permute-start.19 = (f32[16,384]{1,0:T(8,128)S(1)}, f32[16,384]{1,0:T(8,128)S(1)}, u32[]{:S(2)}, u32[]{:S(2)}) collective-permute-start(f32[16,384]{1,0:T(8,128)S(1)} %fusion.2), channel_id=1, source_target_pairs={{0,12},{1,13},{2,14},{3,15},{4,16},{5,17},{6,18},{7,19},{8,20},{9,... | collective-permute-start | bytes 73736
  790.2 26.3 %collective-permute-start.20 = (f32[16,384]{1,0:T(8,128)S(1)}, f32[16,384]{1,0:T(8,128)S(1)}, u32[]{:S(2)}, u32[]{:S(2)}) collective-permute-start(f32[16,384]{1,0:T(8,128)S(1)} %fusion.2), channel_id=1, source_target_pairs={{0,13},{1,14},{2,15},{3,16},{4,17},{5,18},{6,19},{7,20},{8,21},{9,... | collective-permute-start | bytes 73736
  792.5 25.4 %collective-permute-start.21 = (f32[16,384]{1,0:T(8,128)S(1)}, f32[16,384]{1,0:T(8,128)S(1)}, u32[]{:S(2)}, u32[]{:S(2)}) collective-permute-start(f32[16,384]{1,0:T(8,128)S(1)} %fusion.2), channel_id=1, source_target_pairs={{0,14},{1,15},{2,16},{3,17},{4,18},{5,19},{6,20},{7,21},{8,22},{9,... | collective-permute-start | bytes 73736
  808.0 11.5 %collective-permute-start.22 = (f32[16,384]{1,0:T(8,128)S(1)}, f32[16,384]{1,0:T(8,128)S(1)}, u32[]{:S(2)}, u32[]{:S(2)}) collective-permute-start(f32[16,384]{1,0:T(8,128)S(1)} %fusion.2), channel_id=1, source_target_pairs={{0,15},{1,16},{2,17},{3,18},{4,19},{5,20},{6,21},{7,22},{8,23},{9,... | collective-permute-start | bytes 73736
  809.3 13.7 %collective-permute-start.23 = (f32[16,384]{1,0:T(8,128)S(1)}, f32[16,384]{1,0:T(8,128)S(1)}, u32[]{:S(2)}, u32[]{:S(2)}) collective-permute-start(f32[16,384]{1,0:T(8,128)S(1)} %fusion.2), channel_id=1, source_target_pairs={{0,16},{1,17},{2,18},{3,19},{4,20},{5,21},{6,22},{7,23},{8,24},{9,... | collective-permute-start | bytes 73736
  817.9 9.9 %collective-permute-start.25 = (f32[16,384]{1,0:T(8,128)S(1)}, f32[16,384]{1,0:T(8,128)S(1)}, u32[]{:S(2)}, u32[]{:S(2)}) collective-permute-start(f32[16,384]{1,0:T(8,128)S(1)} %fusion.2), channel_id=1, source_target_pairs={{0,18},{1,19},{2,20},{3,21},{4,22},{5,23},{6,24},{7,25},{8,26},{9,... | collective-permute-start | bytes 73736
  819.5 9.6 collective-permute-start.26
  836.9 9.9 %collective-permute-start.34 = (f32[16,384]{1,0:T(8,128)S(1)}, f32[16,384]{1,0:T(8,128)S(1)}, u32[]{:S(2)}, u32[]{:S(2)}) collective-permute-start(f32[16,384]{1,0:T(8,128)S(1)} %fusion.2), channel_id=1, source_target_pairs={{0,27},{1,28},{2,29},{3,30},{4,31},{5,32},{6,33},{7,34},{8,35},{9,... | collective-permute-start | bytes 73736
  841.8 11.1 %collective-permute-start.36 = (f32[16,384]{1,0:T(8,128)S(1)}, f32[16,384]{1,0:T(8,128)S(1)}, u32[]{:S(2)}, u32[]{:S(2)}) collective-permute-start(f32[16,384]{1,0:T(8,128)S(1)} %fusion.2), channel_id=1, source_target_pairs={{0,29},{1,30},{2,31},{3,32},{4,33},{5,34},{6,35},{7,36},{8,37},{9,... | collective-permute-start | bytes 73736
  844.4 11.5 %collective-permute-start.37 = (f32[16,384]{1,0:T(8,128)S(1)}, f32[16,384]{1,0:T(8,128)S(1)}, u32[]{:S(2)}, u32[]{:S(2)}) collective-permute-start(f32[16,384]{1,0:T(8,128)S(1)} %fusion.2), channel_id=1, source_target_pairs={{0,30},{1,31},{2,32},{3,33},{4,34},{5,35},{6,36},{7,37},{8,38},{9,... | collective-permute-start | bytes 73736
  (57 other events, 950.2 us)
Sparse Core Ops, SparseCore 0:
  400.1 159.6 all-reduce.12
where the time goes:
time: 974 us; the launch traced here: 967 us
  blocking collectives  420 us (43%)
  matrix products  138 us (14%)
  starting transfers between devices  112 us (11%)
  other arithmetic  105 us (11%)
  local copies, waits for them, and re-layouts  96.4 us (10%)
  waiting for transfers between devices  76.4 us (8%)
  between operations  18.7 us (2%)
    unnamed x1, blocking collectives  350 us
    dot_general x30, matrix products, mult(): jnp.einsum(formula, left_op, right_op, preferred_element_type=jnp.float32)  111 us
    unnamed x33, starting transfers between devices  91.6 us
    ppermute x8, waiting for transfers between devices, passed_along(): lax.ppermute(value, axis, [(i, (i + by) % count) for i in range(count)])  74 us
    psum x1, blocking collectives, body(): loss_value = lax.psum(numerator, ('lvl', 'lat')) / weight_sum  70.5 us
    unnamed x90, local copies, waits for them, and re-layouts  30.7 us
    convert_element_type x1, other arithmetic, tail(): hidden = gelu_exact(pre_act).astype(jnp.bfloat16)  25.2 us
    sub x3, matrix products, attend(): exp_scores = jnp.exp(scores - top_row)  23.2 us
  transfers between devices with their start and end apart: 41, of which 9 were waited for; matrix products, arithmetic and copies ran while one was open for 42% of the time, Pallas kernels for 0%

commit v1 on v0

v1 whole, which is shorter than its diff:
```python
import functools
import math

import jax
import jax.numpy as jnp
from jax import lax
from jax.experimental import pallas as pl
from jax.experimental.pallas import tpu as pltpu
from jax.sharding import PartitionSpec as P

WIN_LON = 12
HEADS = 12
norm_eps = 1e-05
loss_scale = 32768.0
smooth_sq = 0.01
masked_score = -1e30
log2_e = math.log2(math.e)
f32 = jnp.float32
bf16 = jnp.bfloat16


def nn(left, right):
    return lax.dot_general(left, right, (((1,), (0,)), ((), ())), preferred_element_type=f32)


def nt(left, right):
    return lax.dot_general(left, right, (((1,), (1,)), ((), ())), preferred_element_type=f32)


def tn(left, right):
    return lax.dot_general(left, right, (((0,), (0,)), ((), ())), preferred_element_type=f32)


def normalize(values):
    width = values.shape[-1]
    centre = jnp.sum(values, -1, keepdims=True) * (1.0 / width)
    moved = values - centre
    spread = jnp.sum(moved * moved, -1, keepdims=True) * (1.0 / width)
    rstd = lax.rsqrt(spread + norm_eps)
    return moved * rstd, rstd


def norm_back(grad_hat, hat, rstd):
    width = hat.shape[-1]
    mean_g = jnp.sum(grad_hat, -1, keepdims=True) * (1.0 / width)
    mean_gh = jnp.sum(grad_hat * hat, -1, keepdims=True) * (1.0 / width)
    return rstd * (grad_hat - mean_g - hat * mean_gh)


def gelu_both(x):
    dens = jnp.exp2(x * x * (-0.5 * log2_e))
    den = 1.0 + jnp.abs(x) * (0.3275911 / math.sqrt(2.0))
    t = pl.reciprocal(den, approx=True)
    t = t * (2.0 - den * t)
    poly = 0.5 * 1.061405429
    for coef in (-1.453152027, 1.421413741, -0.284496736, 0.254829592):
        poly = poly * t + 0.5 * coef
    side = poly * t * dens
    cdf = jnp.where(x >= 0.0, 1.0 - side, side)
    return x * cdf, cdf + x * dens * (1.0 / math.sqrt(2.0 * math.pi))


def one_hot_of(relief_col, classes):
    ids = lax.broadcasted_iota(jnp.int32, (relief_col.shape[0], classes), 1)
    return (relief_col == ids).astype(f32).astype(bf16)


def stream_of(x_ref, relief_ref, table_ref):
    one_hot = one_hot_of(relief_ref[...], table_ref.shape[0])
    return x_ref[...].astype(f32) + nn(one_hot, table_ref[...]), one_hot


def att_kernel(
    x_ref,
    relief_ref,
    table_ref,
    gain_ref,
    wt_ref,
    wv_ref,
    wk_ref,
    wproj_ref,
    bias_ref,
    stream2_ref,
    qkt_ref,
    v_ref,
    prob_ref,
    att_ref,
):
    stream, _ = stream_of(x_ref, relief_ref, table_ref)
    hat, _ = normalize(stream)
    normed = (hat * gain_ref[...]).astype(bf16)
    d = normed.shape[1]
    e = d // HEADS
    qkvt = nt(wt_ref[...], normed)
    qt = (qkvt[:d] * (log2_e * e**-0.5)).astype(bf16)
    kt = qkvt[d : 2 * d].astype(bf16)
    vt = qkvt[2 * d :].astype(bf16)
    qkt_ref[0, :d] = qt
    qkt_ref[0, d:] = kt
    k_tok = nn(normed, wk_ref[...]).astype(bf16)
    v_ref[...] = nn(normed, wv_ref[...]).astype(bf16)
    per = 128 // e
    for h in range(HEADS):
        g, j = h // per, h % per
        parts = [jnp.zeros((e, qt.shape[1]), bf16)] * per
        parts[j] = qt[h * e : (h + 1) * e]
        q_one = jnp.concatenate(parts, 0)
        scores = nn(k_tok[:, g * 128 : (g + 1) * 128], q_one) + bias_ref[h]
        top = jnp.max(scores, 0, keepdims=True)
        probs = jnp.exp2(scores - top)
        probs = (probs * (1.0 / jnp.sum(probs, 0, keepdims=True))).astype(bf16)
        prob_ref[0, h] = probs
        att_ref[0, h * e : (h + 1) * e] = nn(vt[h * e : (h + 1) * e], probs).astype(bf16)
    mixed = tn(att_ref[0], wproj_ref[...]).astype(bf16)
    stream2_ref[...] = stream + mixed.astype(f32)


def tail_kernel(
    scale_ref,
    stream2_ref,
    targ_ref,
    relief_ref,
    lev_ref,
    base_ref,
    att_ref,
    gain_ref,
    wup_ref,
    wdown_ref,
    wout_ref,
    num_ref,
    gs2_ref,
    gproj_ref,
    gup_ref,
    gdown_ref,
    gout_ref,
    hid_ref,
    slope_ref,
    *,
    block_f,
):
    step = pl.program_id(0)

    @pl.when(step == 0)
    def _():
        num_ref[...] = jnp.zeros_like(num_ref)
        gproj_ref[...] = jnp.zeros_like(gproj_ref)
        gup_ref[...] = jnp.zeros_like(gup_ref)
        gdown_ref[...] = jnp.zeros_like(gdown_ref)
        gout_ref[...] = jnp.zeros_like(gout_ref)

    stream2 = stream2_ref[...]
    wins, win = att_ref.shape[0], att_ref.shape[2]
    ff = wup_ref.shape[1]
    hat, rstd = normalize(stream2)
    gain = gain_ref[...]
    normed2 = (hat * gain).astype(bf16)
    for n in range(0, ff, block_f):
        cols = slice(n, n + block_f)
        hidden, slope = gelu_both(nn(normed2, wup_ref[:, cols]))
        hid_ref[:, cols] = hidden.astype(bf16)
        slope_ref[:, cols] = slope.astype(bf16)
    field = (stream2 + nn(hid_ref[...], wdown_ref[...])).astype(bf16)
    pred = nn(field, wout_ref[...])
    relief = relief_ref[...]
    lev = jnp.concatenate([lev_ref[...]] * wins, 0)
    base = jnp.concatenate([base_ref[...]] * wins, 0)
    cell_w = jnp.where(lev >= relief, base, 0.0)
    differ = pred - targ_ref[...].astype(f32)
    square = differ * differ + smooth_sq
    inv_err = lax.rsqrt(square)
    num_ref[...] += jnp.sum(cell_w * (square * inv_err), 0, keepdims=True)
    gpred = (scale_ref[0] * cell_w * differ * inv_err).astype(bf16)
    gout_ref[...] += nn(field.T, gpred)
    gfield = nt(gpred, wout_ref[...])
    gfb = gfield.astype(bf16)
    gfbt = gfb.T
    normed2t = normed2.T
    for n in range(0, ff, block_f):
        cols = slice(n, n + block_f)
        gdown_ref[:, cols] += nn(gfbt, hid_ref[:, cols])
        ghid = nt(gfb, wdown_ref[cols, :])
        gpre = (slope_ref[:, cols].astype(f32) * ghid).astype(bf16)
        slope_ref[:, cols] = gpre
        gup_ref[:, cols] += nn(normed2t, gpre)
    gnorm2 = nt(slope_ref[...], wup_ref[...])
    gs2 = gfield + norm_back(gnorm2 * gain, hat, rstd)
    gs2_ref[...] = gs2
    gmix = gs2.astype(bf16)
    for w in range(wins):
        gproj_ref[...] += nn(att_ref[w], gmix[w * win : (w + 1) * win])


def back_kernel(
    x_ref,
    relief_ref,
    table_ref,
    gain_ref,
    wqkv_ref,
    wproj_ref,
    qkt_ref,
    v_ref,
    prob_ref,
    att_ref,
    gs2_ref,
    gbias_ref,
    gqkv_ref,
    grel_ref,
    gh_ref,
):
    step = pl.program_id(0)

    @pl.when(step == 0)
    def _():
        gbias_ref[...] = jnp.zeros_like(gbias_ref)
        gqkv_ref[...] = jnp.zeros_like(gqkv_ref)
        grel_ref[...] = jnp.zeros_like(grel_ref)

    stream, one_hot = stream_of(x_ref, relief_ref, table_ref)
    hat, rstd = normalize(stream)
    gain = gain_ref[...]
    normed = (hat * gain).astype(bf16)
    d = normed.shape[1]
    e = d // HEADS
    per = 128 // e
    gs2 = gs2_ref[...]
    gatt = nt(wproj_ref[...], gs2.astype(bf16))
    gatt_b = gatt.astype(bf16)
    prod = gatt_b.astype(f32) * att_ref[0].astype(f32)
    for h in range(HEADS):
        g, j = h // per, h % per
        rows = slice(h * e, (h + 1) * e)
        go = gatt_b[rows]
        parts = [jnp.zeros_like(go)] * per
        parts[j] = go
        delta = jnp.sum(prod[rows], 0, keepdims=True)
        gprob = nn(v_ref[:, g * 128 : (g + 1) * 128], jnp.concatenate(parts, 0))
        probs = prob_ref[0, h]
        gscore = probs.astype(f32) * (gprob - delta)
        gbias_ref[h] += gscore
        gsb = gscore.astype(bf16)
        gh_ref[rows] = (nn(qkt_ref[0, d + h * e : d + (h + 1) * e], gsb) * e**-0.5).astype(bf16)
        gh_ref[d + h * e : d + (h + 1) * e] = (nt(qkt_ref[0, rows], gsb) * (1.0 / log2_e)).astype(
            bf16
        )
        gh_ref[2 * d + h * e : 2 * d + (h + 1) * e] = nt(go, probs).astype(bf16)
    gheads = gh_ref[...]
    gqkv_ref[...] += nn(gheads, normed)
    gshift = nn(wqkv_ref[...], gheads).astype(bf16).T.astype(f32)
    gstream = gs2 + norm_back(gshift * gain, hat, rstd)
    grel_ref[...] += tn(one_hot, gstream.astype(bf16))


def whole(shape):
    return pl.BlockSpec(shape, lambda i: (0,) * len(shape))


def lead(shape):
    return pl.BlockSpec(shape, lambda i: (i,) + (0,) * (len(shape) - 1))


def params_of():
    return pltpu.CompilerParams(
        vmem_limit_bytes=56 * 2**20, dimension_semantics=("arbitrary",)
    )


def attention_forward(x, relief_col, table, gain, w_qkv, w_proj, bias_t):
    t, d = x.shape
    win = bias_t.shape[-1]
    count = t // win
    sds = jax.ShapeDtypeStruct
    return pl.pallas_call(
        att_kernel,
        grid=(count,),
        in_specs=[
            lead((win, d)),
            lead((win, 1)),
            whole(table.shape),
            whole((1, d)),
            whole((3 * d, d)),
            whole((d, d)),
            whole((d, d)),
            whole((d, d)),
            whole(bias_t.shape),
        ],
        out_specs=[
            lead((win, d)),
            lead((1, 2 * d, win)),
            lead((win, d)),
            lead((1, HEADS, win, win)),
            lead((1, d, win)),
        ],
        out_shape=[
            sds((t, d), f32),
            sds((count, 2 * d, win), bf16),
            sds((t, d), bf16),
            sds((count, HEADS, win, win), bf16),
            sds((count, d, win), bf16),
        ],
        compiler_params=params_of(),
        name="attention_forward",
    )(
        x,
        relief_col,
        table,
        gain[None],
        w_qkv.T,
        w_qkv[:, 2 * d :],
        w_qkv[:, d : 2 * d],
        w_proj,
        bias_t,
    )


def tail_both(scale, stream2, targ, relief_col, lev, base, att, gain, w_up, w_down, w_out, group):
    t, d = stream2.shape
    win = att.shape[-1]
    m = group * win
    ff, out = w_up.shape[1], w_out.shape[1]
    sds = jax.ShapeDtypeStruct
    return pl.pallas_call(
        functools.partial(tail_kernel, block_f=256),
        grid=(t // m,),
        in_specs=[
            pl.BlockSpec(memory_space=pltpu.SMEM),
            lead((m, d)),
            lead((m, out)),
            lead((m, 1)),
            whole((win, out)),
            whole((win, out)),
            lead((group, d, win)),
            whole((1, d)),
            whole((d, ff)),
            whole((ff, d)),
            whole((d, out)),
        ],
        out_specs=[
            whole((1, out)),
            lead((m, d)),
            whole((d, d)),
            whole((d, ff)),
            whole((d, ff)),
            whole((d, out)),
        ],
        out_shape=[
            sds((1, out), f32),
            sds((t, d), f32),
            sds((d, d), f32),
            sds((d, ff), f32),
            sds((d, ff), f32),
            sds((d, out), f32),
        ],
        scratch_shapes=[pltpu.VMEM((m, ff), bf16), pltpu.VMEM((m, ff), bf16)],
        compiler_params=params_of(),
        name="tail_both",
    )(scale, stream2, targ, relief_col, lev, base, att, gain[None], w_up, w_down, w_out)


def attention_back(x, relief_col, table, gain, w_qkv, w_proj, qkt, v_tok, probs, att, gs2):
    t, d = x.shape
    count, win = att.shape[0], att.shape[2]
    sds = jax.ShapeDtypeStruct
    return pl.pallas_call(
        back_kernel,
        grid=(count,),
        in_specs=[
            lead((win, d)),
            lead((win, 1)),
            whole(table.shape),
            whole((1, d)),
            whole((d, 3 * d)),
            whole((d, d)),
            lead((1, 2 * d, win)),
            lead((win, d)),
            lead((1, HEADS, win, win)),
            lead((1, d, win)),
            lead((win, d)),
        ],
        out_specs=[
            whole((HEADS, win, win)),
            whole((3 * d, d)),
            whole((table.shape[0], d)),
        ],
        out_shape=[
            sds((HEADS, win, win), f32),
            sds((3 * d, d), f32),
            sds((table.shape[0], d), f32),
        ],
        scratch_shapes=[pltpu.VMEM((3 * d, win), bf16)],
        compiler_params=params_of(),
        name="attention_back",
    )(x, relief_col, table, gain[None], w_qkv, w_proj, qkt, v_tok, probs, att, gs2)


def lat_weights(row_ids, lat_rows):
    fine_rows = 4 * row_ids[:, None] + jnp.arange(4, dtype=jnp.int32)[None, :]
    angle_rad = (90.0 - 180.0 * (fine_rows.astype(f32) + 0.5) / (4.0 * lat_rows)) * (
        math.pi / 180.0
    )
    return jnp.cos(angle_rad)


def weight_total(relief, var_weight, level_count):
    lat_rows = relief.shape[0]
    lat_weight = jnp.sum(lat_weights(jnp.arange(lat_rows, dtype=jnp.int32), lat_rows), 1)
    live_levels = (2 * level_count - relief).astype(f32)
    return jnp.sum(var_weight) * 4.0 * jnp.sum(lat_weight[:, None] * live_levels)


def window_mask(last_level, last_band, slots_n, rows_n, win_lon):
    slot_label = jnp.where(last_level & (jnp.arange(slots_n) >= slots_n // 2), 2, 0)
    row_label = jnp.where(last_band & (jnp.arange(rows_n) >= rows_n // 2), 1, 0)
    labels = (
        slot_label[:, None, None] + row_label[None, :, None] + jnp.zeros((1, 1, win_lon), jnp.int32)
    )
    labels = labels.reshape(-1)
    return labels[:, None] == labels[None, :]


def windows(field_in):
    slots_n, rows_n, lon_n, chans = field_in.shape
    count_w = lon_n // WIN_LON
    parted = field_in.reshape(slots_n, rows_n, count_w, WIN_LON, chans).transpose(2, 0, 1, 3, 4)
    return parted.reshape(count_w * slots_n * rows_n * WIN_LON, chans)


def from_next(value, axes):
    sizes = [lax.axis_size(a) for a in ("lvl", "lat")]
    move = [1 if a in axes else 0 for a in ("lvl", "lat")]
    pairs = []
    for i in range(sizes[0]):
        for j in range(sizes[1]):
            src = (i + move[0]) % sizes[0] * sizes[1] + (j + move[1]) % sizes[1]
            pairs.append((src, i * sizes[1] + j))
    return lax.ppermute(value, ("lvl", "lat"), pairs)


def shifted_windows(field_in):
    slots_n, rows_n = field_in.shape[:2]
    hs, hr = slots_n // 2, rows_n // 2
    up = from_next(field_in[:hs, hr:], ("lvl",))
    side = from_next(field_in[hs:, :hr], ("lat",))
    both = from_next(field_in[:hs, :hr], ("lvl", "lat"))
    rolled = jnp.concatenate(
        [
            jnp.concatenate([field_in[hs:, hr:], side], 1),
            jnp.concatenate([up, both], 1),
        ],
        0,
    )
    return windows(jnp.roll(rolled, -(WIN_LON // 2), 2))


def local_inputs(tokens_shape, relief, earth_bias, var_weight):
    slots_dev, rows_dev, lon_cells, _ = tokens_shape
    lvl_count, lat_count = lax.axis_size("lvl"), lax.axis_size("lat")
    lvl_id, lat_id = lax.axis_index("lvl"), lax.axis_index("lat")
    level_total, lat_rows = slots_dev * lvl_count, rows_dev * lat_count
    allowed = window_mask(
        lvl_id == lvl_count - 1, lat_id == lat_count - 1, slots_dev, rows_dev, WIN_LON
    )
    level_ids = (
        lvl_id * slots_dev + jnp.arange(slots_dev, dtype=jnp.int32) + slots_dev // 2
    ) % level_total
    row_ids = (
        lat_id * rows_dev + jnp.arange(rows_dev, dtype=jnp.int32) + rows_dev // 2
    ) % lat_rows
    relief_blk = jnp.roll(jnp.take(relief, row_ids, axis=0), -(WIN_LON // 2), 1)
    relief_col = windows(
        jnp.broadcast_to(relief_blk[None, :, :, None], (slots_dev, rows_dev, lon_cells, 1))
    )
    shape = (slots_dev, rows_dev, WIN_LON, var_weight.shape[0], 2, 4, 4)
    levels = 2 * level_ids[:, None] + jnp.arange(2, dtype=jnp.int32)[None, :]
    lev = jnp.broadcast_to(levels[:, None, None, None, :, None, None], shape)
    base = jnp.broadcast_to(
        var_weight[None, None, None, :, None, None, None]
        * lat_weights(row_ids, lat_rows)[None, :, None, None, None, :, None],
        shape,
    )
    win = slots_dev * rows_dev * WIN_LON
    bias_t = jnp.where(allowed, earth_bias.transpose(0, 2, 1) * log2_e, masked_score)
    return relief_col, lev.reshape(win, -1), base.reshape(win, -1), bias_t


def body(
    tokens,
    targets,
    relief,
    earth_bias,
    relief_table,
    gain_attn,
    gain_mlp,
    w_qkv,
    w_proj,
    w_up,
    w_down,
    w_out,
    var_weight,
):
    axes = ("lvl", "lat")
    devs = lax.axis_size("lvl") * lax.axis_size("lat")
    level_total = tokens.shape[0] * lax.axis_size("lvl")
    weight_sum = weight_total(relief, var_weight, level_total)
    x = shifted_windows(tokens)
    targ = shifted_windows(targets)
    relief_col, lev, base, bias_t = local_inputs(tokens.shape, relief, earth_bias[0, 0], var_weight)
    stream2, qkt, v_tok, probs, att = attention_forward(
        x, relief_col, relief_table, gain_attn, w_qkv, w_proj, bias_t
    )
    scale = (loss_scale / weight_sum).reshape(1)
    num, gs2, gproj, gup, gdown_t, gout = tail_both(
        scale, stream2, targ, relief_col, lev, base, att, gain_mlp, w_up, w_down, w_out, 3
    )
    gbias_t, gqkv_t, grel = attention_back(
        x, relief_col, relief_table, gain_attn, w_qkv, w_proj, qkt, v_tok, probs, att, gs2
    )
    gbias = gbias_t.transpose(0, 2, 1)
    pieces = [
        gqkv_t.T.reshape(devs, -1),
        gproj.reshape(devs, -1),
        gup.reshape(devs, -1),
        gdown_t.T.reshape(devs, -1),
        gout.reshape(devs, -1),
        grel.T.reshape(devs, -1),
        jnp.broadcast_to(jnp.sum(num), (devs, 1)),
    ]
    flat = jnp.concatenate(pieces, 1)
    high = flat.astype(bf16)
    low_num = (flat[:, -1:] - high[:, -1:].astype(f32)).astype(bf16)
    send = jnp.concatenate([high, low_num], 1)
    pad = -send.shape[1] % 2048
    send = jnp.pad(send, ((0, 0), (0, pad))).reshape(devs, -1, 128)
    got = lax.all_to_all(send, axes, 0, 0, tiled=True)
    total = jnp.sum(got.astype(f32), 0).reshape(-1)
    outs, at = [], 0
    d = tokens.shape[-1]
    for cols in (
        (d // devs, w_qkv.shape[1]),
        (d // devs, d),
        (d // devs, w_up.shape[1]),
        (w_down.shape[0] // devs, d),
        (d // devs, w_out.shape[1]),
        (d // devs, relief_table.shape[0]),
    ):
        size = cols[0] * cols[1]
        outs.append(total[at : at + size].reshape(cols))
        at += size
    grad_qkv, grad_proj, grad_up, grad_down, grad_out, grad_relief = outs
    numerator = total[at] + total[at + 1]
    me = lax.axis_index(axes)

    def mine(array):
        return lax.dynamic_slice_in_dim(array, me * (d // devs), d // devs, 0)

    grad_gain_attn = jnp.sum(mine(w_qkv).astype(f32) * grad_qkv, 1) / mine(gain_attn)
    grad_gain_mlp = jnp.sum(mine(w_up).astype(f32) * grad_up, 1) / mine(gain_mlp)
    return (
        numerator / weight_sum,
        grad_qkv,
        grad_proj,
        grad_up,
        grad_down,
        grad_out,
        grad_gain_attn,
        grad_gain_mlp,
        grad_relief,
        gbias[None, None],
    )


def solution(mesh):
    field = P("lvl", "lat", None, None)
    bias = P("lvl", "lat", None, None, None)
    rows = P(("lvl", "lat"), None)
    vec = P(("lvl", "lat"))
    return jax.shard_map(
        body,
        mesh=mesh,
        in_specs=(field, field, P(), bias) + (P(),) * 9,
        out_specs=(P(), rows, rows, rows, rows, rows, vec, vec, rows, bias),
        check_vma=False,
    )
```

time: 974 us -> 278 us (0.29)
  blocking collectives: 420 us -> 0 us
  matrix products: 138 us -> 0 us
  Pallas kernels: 0 us -> 137 us
  starting transfers between devices: 112 us -> 19.3 us
  other arithmetic: 105 us -> 23 us
  local copies, waits for them, and re-layouts: 96.4 us -> 46.4 us
  waiting for transfers between devices: 76.4 us -> 44.7 us
  between operations: 18.7 us -> 6.18 us
    unnamed x1 -> x0, blocking collectives: 350 us -> none
    pallas_call x0 -> x3, Pallas kernels: none -> 137 us  [the longest x1 52.3 us: attention_forward(): pl.pallas_call(att_kernel, grid=(count,), in_specs=[lead((win, d)), lead(...]
    dot_general x32 -> x0, matrix products: 115 us -> none  [the longest x30 111 us: mult(): jnp.einsum(formula, left_op, right_op, preferred_element_type=jnp.float32)]
    unnamed x33 -> x0, starting transfers between devices: 91.6 us -> none
    ppermute x8 -> x6, waiting for transfers between devices: 74 us -> 0.02 us  [from_next(): return lax.ppermute(value, ('lvl', 'lat'), pairs)]
    psum x1 -> x0, blocking collectives: 70.5 us -> none  [body(): loss_value = lax.psum(numerator, ('lvl', 'lat')) / weight_sum]
    all_to_all x0 -> x1, waiting for transfers between devices: none -> 44.7 us  [body(): got = lax.all_to_all(send, axes, 0, 0, tiled=True)]
    reduce_sum x12 -> x4, other arithmetic: 43.5 us -> 5.73 us  [the longest x1 2.6 us: body(): total = jnp.sum(got.astype(f32), 0).reshape(-1)]
  transfers between devices with their start and end apart: 41 -> 7, of which waited for: 9 -> 1; matrix products, arithmetic and copies ran while one was open for 42% -> 9% of each run, Pallas kernels for 0% -> 0%
where the time goes in v1:
time: 278 us; the launch traced here: 277 us
  Pallas kernels  137 us (49%)
  local copies, waits for them, and re-layouts  46.4 us (17%)
  waiting for transfers between devices  44.7 us (16%)
  other arithmetic  23 us (8%)
  starting transfers between devices  19.3 us (7%)
  between operations  6.18 us (2%)
    pallas_call x1, Pallas kernels, attention_forward(): pl.pallas_call(att_kernel, grid=(count,), in_specs=[lead((win, d)), lead(...  52.3 us
    pallas_call x1, Pallas kernels, attention_back(): pl.pallas_call(back_kernel, grid=(count,), in_specs=[lead((win, d)), lead...  47.6 us
    all_to_all x1, waiting for transfers between devices, body(): got = lax.all_to_all(send, axes, 0, 0, tiled=True)  44.7 us
    pallas_call x1, Pallas kernels, tail_both(): pl.pallas_call(functools.partial(tail_kernel, block_f=256), grid=(t // m,...  37.3 us
    ppermute x6, starting transfers between devices, from_next(): return lax.ppermute(value, ('lvl', 'lat'), pairs)  13.3 us
    unnamed x41, local copies, waits for them, and re-layouts  11.3 us
    all_to_all x1, starting transfers between devices, body(): got = lax.all_to_all(send, axes, 0, 0, tiled=True)  6.04 us
    concatenate x1, local copies, waits for them, and re-layouts, body(): send = jnp.concatenate([high, low_num], 1)  5.99 us
  transfers between devices with their start and end apart: 7, of which 1 were waited for; matrix products, arithmetic and copies ran while one was open for 9% of the time, Pallas kernels for 0%

profile of v1, /device:TPU:0, one launch (start us, length us, event | category | flops | bytes accessed | tf_op | source)
XLA Modules:
  0.0 276.9 jit_solution(14710291541144187263)
XLA Ops:
  0.7 2.2 fusion.8
  2.9 7.3 %collective-permute-start.3 = (bf16[1,3,144,160]{3,2,1,0:T(8,128)(2,1)}, bf16[1,3,144,160]{3,2,1,0:T(8,128)(2,1)}, u32[]{:S(2)}, u32[]{:S(2)}) collective-permute-start(bf16[1,3,144,160]{3,2,1,0:T(8,128)(2,1)} %get-tuple-element.73), channel_id=1, source_target_pairs={{1,0},{2,1},{3,2},{4,3},{5,4},{6,5},{7,6},{8,7},{9,8},{10,9},{11,1... | collective-permute-start | bytes 414728 | tf_op jit(solution)/shard_map/ppermute | solution.py:435
  11.5 2.0 collective-permute-start.4
  19.7 2.1 copy.54
  22.5 2.2 bitcast_select_fusion.bias_ref
  33.5 1.7 collective-permute-start.1
  36.5 1.4 maximum_maximum_fusion.1
  40.1 1.4 reshape.284.targ_ref
  45.2 1.4 reshape.280.x_ref
  46.7 52.3 %attention_forward.1 = (f32[1728,384]{1,0:T(8,128)}, bf16[12,768,144]{2,1,0:T(8,128)(2,1)}, bf16[1728,384]{1,0:T(8,128)(2,1)}, bf16[12,12,144,144]{3,2,1,0:T(8,128)(2,1)}, bf16[12,384,144]{2,1,0:T(8,128)(2,1)}) custom-call(bf16[1728,384]{1,0:T(8,128)(2,1)} %reshape.280.x_ref, s32[1728,1]{1,0:T(8,128)} %reshape.308.relief_ref, bf16[4,384]{1,0:T(4,128)(2,1)} %table_ref.3, ...), custom_call_target="tpu_custom_call" | custom-call | tf_op jit(solution)/shard_map/attention_forward/pallas_call | solution.py:272
  99.0 37.3 %tail_both.1 = (f32[1,160]{1,0:T(1,128)}, f32[1728,384]{1,0:T(8,128)}, f32[384,384]{1,0:T(8,128)}, f32[384,1536]{1,0:T(8,128)}, f32[384,1536]{1,0:T(8,128)}, /*index=5*/f32[384,160]{1,0:T(8,128)}) custom-call(f32[1]{0:T(128)} %bitcast.7.scale_ref, f32[1728,384]{1,0:T(8,128)} %get-tuple-element.28.stream2_ref, bf16[1728,160]{1,0:T(8,128)(2,1)} %reshape.284.targ_ref, ...), custom_call_target="tpu_custom_call" | custom-call | tf_op jit(solution)/shard_map/tail_both/pallas_call | solution.py:321
  138.9 47.6 %attention_back.1 = (f32[12,144,144]{2,1,0:T(8,128)}, f32[1152,384]{1,0:T(8,128)}, f32[4,384]{1,0:T(4,128)}) custom-call(bf16[1728,384]{1,0:T(8,128)(2,1)} %reshape.280.x_ref, s32[1728,1]{1,0:T(8,128)} %reshape.308.relief_ref, bf16[4,384]{1,0:T(4,128)(2,1)} %table_ref.3, f32[1,384]{1,0:T(1,128)} %broadcast_in_dim.83.gain_ref, bf16[384,1152]{1,0:T(8,128)(2,1)} %wqkv_ref.1, ...), custom_call_target="tpu_custom_call" | custom-call | tf_op jit(solution)/shard_map/attention_back/pallas_call | solution.py:363
  186.5 1.6 convert_bitcast_fusion.1
  193.0 1.8 convert.31
  195.4 1.8 convert_bitcast_fusion
  198.0 1.4 reshape.290
  199.4 6.0 %concatenate.45 = bf16[128,14318]{1,0:T(8,128)(2,1)} concatenate(bf16[128,3456]{1,0:T(8,128)(2,1)} %reshape.287, bf16[128,1152]{1,0:T(8,128)(2,1)} %reshape.288, bf16[128,4608]{1,0:T(8,128)(2,1)S(1)} %reshape.289, bf16[128,4608]{1,0:T(8,128)(2,1)S(1)} %reshape.290, bf16[128,480]{1,0:T(8,128)(2,1)} %reshape.291, bf16[128,12]{1,0:T(8,128)(2,1)} %reshape.292, ...), dimensions={1} | concatenate | bytes 7330816 | tf_op jit(solution)/shard_map/concatenate | solution.py:530
  205.4 2.3 pad_bitcast_fusion
  207.7 2.6 copy.67
  210.4 6.0 %all-to-all-start = ((bf16[128,112,128]{2,1,0:T(8,128)(2,1)}), bf16[128,112,128]{2,1,0:T(8,128)(2,1)}, u32[]{:S(2)}, u32[]{:S(2)}) async-start(bf16[128,112,128]{2,1,0:T(8,128)(2,1)} %bitcast.36), calls=%async_computation | async-start | bytes 7340032 | tf_op jit(solution)/shard_map/all_to_all | solution.py:533
  216.4 1.9 copy.66
  218.4 44.7 %all-to-all-done = bf16[128,112,128]{2,1,0:T(8,128)(2,1)} async-done(((bf16[128,112,128]{2,1,0:T(8,128)(2,1)}), bf16[128,112,128]{2,1,0:T(8,128)(2,1)}, u32[]{:S(2)}, u32[]{:S(2)}) %all-to-all-start) | async-done | bytes 3670048 | tf_op jit(solution)/shard_map/all_to_all | solution.py:533
  263.1 2.6 convert_reduce_fusion
  266.3 1.9 slice.109
  (119 shorter events, 37.1 us)
Async XLA Ops:
  0.6 12.9 %copy-start.2 = (bf16[2,6,144,384]{3,2,1,0:T(8,128)(2,1)S(1)}, bf16[2,6,144,384]{3,2,1,0:T(8,128)(2,1)}, u32[]{:S(2)}) copy-start(bf16[2,6,144,384]{3,2,1,0:T(8,128)(2,1)} %param.13) | copy-start | bytes 3981316
  2.9 12.7 %copy-start.4 = (s32[192,144]{0,1:T(8,128)S(1)}, s32[192,144]{0,1:T(8,128)}, u32[]{:S(2)}) copy-start(s32[192,144]{0,1:T(8,128)} %param.15) | copy-start | bytes 331780
  2.9 30.6 %collective-permute-start.3 = (bf16[1,3,144,160]{3,2,1,0:T(8,128)(2,1)}, bf16[1,3,144,160]{3,2,1,0:T(8,128)(2,1)}, u32[]{:S(2)}, u32[]{:S(2)}) collective-permute-start(bf16[1,3,144,160]{3,2,1,0:T(8,128)(2,1)} %get-tuple-element.73), channel_id=1, source_target_pairs={{1,0},{2,1},{3,2},{4,3},{5,4},{6,5},{7,6},{8,7},{9,8},{10,9},{11,1... | collective-permute-start | bytes 414728 | tf_op jit(solution)/shard_map/ppermute | solution.py:435
  10.2 26.3 %collective-permute-start.5 = (bf16[1,3,144,160]{3,2,1,0:T(8,128)(2,1)}, bf16[1,3,144,160]{3,2,1,0:T(8,128)(2,1)}, u32[]{:S(2)}, u32[]{:S(2)}) collective-permute-start(bf16[1,3,144,160]{3,2,1,0:T(8,128)(2,1)} %get-tuple-element.74), channel_id=1, source_target_pairs={{33,0},{34,1},{35,2},{36,3},{37,4},{38,5},{39,6},{40,7},{41,8},{42... | collective-permute-start | bytes 414728 | tf_op jit(solution)/shard_map/ppermute | solution.py:435
  11.5 7.3 %copy-start = (bf16[384,1152]{1,0:T(8,128)(2,1)S(1)}, bf16[384,1152]{1,0:T(8,128)(2,1)}, u32[]{:S(2)}) copy-start(bf16[384,1152]{1,0:T(8,128)(2,1)} %wqkv_ref.1) | copy-start | bytes 2654212
  11.5 25.0 %collective-permute-start.4 = (bf16[1,3,144,160]{3,2,1,0:T(8,128)(2,1)}, bf16[1,3,144,160]{3,2,1,0:T(8,128)(2,1)}, u32[]{:S(2)}, u32[]{:S(2)}) collective-permute-start(bf16[1,3,144,160]{3,2,1,0:T(8,128)(2,1)} %get-tuple-element.75), channel_id=1, source_target_pairs={{32,0},{33,1},{34,2},{35,3},{36,4},{37,5},{38,6},{39,7},{40,8},{41... | collective-permute-start | bytes 414728 | tf_op jit(solution)/shard_map/ppermute | solution.py:435
  14.6 26.9 %collective-permute-start = (bf16[1,3,144,384]{3,2,1,0:T(8,128)(2,1)}, bf16[1,3,144,384]{3,2,1,0:T(8,128)(2,1)S(1)}, u32[]{:S(2)}, u32[]{:S(2)}) collective-permute-start(bf16[1,3,144,384]{3,2,1,0:T(8,128)(2,1)} %get-tuple-element.69), channel_id=1, source_target_pairs={{1,0},{2,1},{3,2},{4,3},{5,4},{6,5},{7,6},{8,7},{9,8},{10,9},{11,1... | collective-permute-start | bytes 995336 | tf_op jit(solution)/shard_map/ppermute | solution.py:435
  15.5 26.0 %collective-permute-start.2 = (bf16[1,3,144,384]{3,2,1,0:T(8,128)(2,1)}, bf16[1,3,144,384]{3,2,1,0:T(8,128)(2,1)}, u32[]{:S(2)}, u32[]{:S(2)}) collective-permute-start(bf16[1,3,144,384]{3,2,1,0:T(8,128)(2,1)} %get-tuple-element.70), channel_id=1, source_target_pairs={{33,0},{34,1},{35,2},{36,3},{37,4},{38,5},{39,6},{40,7},{41,8},{42... | collective-permute-start | bytes 995336 | tf_op jit(solution)/shard_map/ppermute | solution.py:435
  24.7 1.4 copy-start.16
  24.7 2.0 copy-start.13
  24.7 2.6 copy-start.14
  24.7 3.2 %copy-start.9 = (bf16[384,160]{0,1:T(8,128)(2,1)S(1)}, bf16[384,160]{0,1:T(8,128)(2,1)}, u32[]{:S(2)}) copy-start(bf16[384,160]{0,1:T(8,128)(2,1)} %param.24) | copy-start | bytes 368644
  24.8 4.0 %copy-start.7 = (s32[12,2,6,12,1]{3,2,1,0,4:T(8,128)S(1)}, s32[12,2,6,12,1]{3,2,1,0,4:T(8,128)}, u32[]{:S(2)}) copy-start(s32[12,2,6,12,1]{3,2,1,0,4:T(8,128)} %broadcast_bitcast_fusion) | copy-start | bytes 20740
  29.9 1.4 copy-start.15
  30.6 2.9 %copy-start.8 = (bf16[1,3,144,384]{3,2,1,0:T(8,128)(2,1)S(1)}, bf16[1,3,144,384]{3,2,1,0:T(8,128)(2,1)}, u32[]{:S(2)}) copy-start(bf16[1,3,144,384]{3,2,1,0:T(8,128)(2,1)} %get-tuple-element.71) | copy-start | bytes 995332
  30.6 4.6 %copy-start.5 = (s32[192,144]{0,1:T(8,128)S(1)}, s32[192,144]{0,1:T(8,128)}, u32[]{:S(2)}) copy-start(s32[192,144]{0,1:T(8,128)} %param.15) | copy-start | bytes 331780
  33.5 8.0 %collective-permute-start.1 = (bf16[1,3,144,384]{3,2,1,0:T(8,128)(2,1)S(1)}, bf16[1,3,144,384]{3,2,1,0:T(8,128)(2,1)S(1)}, u32[]{:S(2)}, u32[]{:S(2)}) collective-permute-start(bf16[1,3,144,384]{3,2,1,0:T(8,128)(2,1)S(1)} %copy-done.8), channel_id=1, source_target_pairs={{32,0},{33,1},{34,2},{35,3},{36,4},{37,5},{38,6},{39,7},{40,8},{41... | collective-permute-start | bytes 995336 | tf_op jit(solution)/shard_map/ppermute | solution.py:435
  188.1 2.3 copy-start.12
  188.1 3.2 %copy-start.6 = (f32[384,160]{1,0:T(8,128)S(1)}, f32[384,160]{1,0:T(8,128)}, u32[]{:S(2)}) copy-start(f32[384,160]{1,0:T(8,128)} %get-tuple-element.34) | copy-start | bytes 737284
  189.0 3.1 %copy-start.3 = (f32[384,384]{1,0:T(8,128)S(1)}, f32[384,384]{1,0:T(8,128)}, u32[]{:S(2)}) copy-start(f32[384,384]{1,0:T(8,128)} %get-tuple-element.31) | copy-start | bytes 1769476
  210.4 6.1 %copy-start.1 = (f32[12,144,144]{2,1,0:T(8,128)S(1)}, f32[12,144,144]{2,1,0:T(8,128)}, u32[]{:S(2)}) copy-start(f32[12,144,144]{2,1,0:T(8,128)} %get-tuple-element.37) | copy-start | bytes 2985988
  210.4 52.7 %all-to-all-start = ((bf16[128,112,128]{2,1,0:T(8,128)(2,1)}), bf16[128,112,128]{2,1,0:T(8,128)(2,1)}, u32[]{:S(2)}, u32[]{:S(2)}) async-start(bf16[128,112,128]{2,1,0:T(8,128)(2,1)} %bitcast.36), calls=%async_computation | async-start | bytes 7340032 | tf_op jit(solution)/shard_map/all_to_all | solution.py:533
  270.8 4.9 %copy-start.11 = (f32[3,1152]{1,0:T(4,128)}, f32[3,1152]{1,0:T(4,128)S(1)}, u32[]{:S(2)}) copy-start(f32[3,1152]{1,0:T(4,128)S(1)} %reshape.295) | copy-start | bytes 41476
  272.9 2.8 %copy-start.10 = (f32[3,1536]{1,0:T(4,128)}, f32[3,1536]{1,0:T(4,128)S(1)}, u32[]{:S(2)}) copy-start(f32[3,1536]{1,0:T(4,128)S(1)} %reshape.297) | copy-start | bytes 55300

commit v2 on v1

v2 whole, which is shorter than its diff:
```python
import functools
import math

import jax
import jax.numpy as jnp
from jax import lax
from jax.experimental import pallas as pl
from jax.experimental.pallas import tpu as pltpu
from jax.sharding import PartitionSpec as P

WIN_LON = 12
HEADS = 12
GROUP = 6
DEVS = 128
WIDE = 256
TOGETHER = 3
norm_eps = 1e-05
loss_scale = 32768.0
smooth_sq = 0.01
masked_score = -1e30
log2_e = math.log2(math.e)
f32 = jnp.float32
bf16 = jnp.bfloat16


def nn(left, right):
    return lax.dot_general(left, right, (((1,), (0,)), ((), ())), preferred_element_type=f32)


def nt(left, right):
    return lax.dot_general(left, right, (((1,), (1,)), ((), ())), preferred_element_type=f32)


def tn(left, right):
    return lax.dot_general(left, right, (((0,), (0,)), ((), ())), preferred_element_type=f32)


def normalize(values):
    width = values.shape[-1]
    centre = jnp.sum(values, -1, keepdims=True) * (1.0 / width)
    moved = values - centre
    spread = jnp.sum(moved * moved, -1, keepdims=True) * (1.0 / width)
    rstd = lax.rsqrt(spread + norm_eps)
    return moved * rstd, rstd


def norm_back(grad_hat, hat, rstd):
    width = hat.shape[-1]
    mean_g = jnp.sum(grad_hat, -1, keepdims=True) * (1.0 / width)
    mean_gh = jnp.sum(grad_hat * hat, -1, keepdims=True) * (1.0 / width)
    return rstd * (grad_hat - mean_g - hat * mean_gh)


def gelu_both(x):
    dens = jnp.exp2(x * x * (-0.5 * log2_e))
    den = 1.0 + jnp.abs(x) * (0.3275911 / math.sqrt(2.0))
    t = pl.reciprocal(den, approx=True)
    t = t * (2.0 - den * t)
    poly = 0.5 * 1.061405429
    for coef in (-1.453152027, 1.421413741, -0.284496736, 0.254829592):
        poly = poly * t + 0.5 * coef
    side = poly * t * dens
    cdf = jnp.where(x >= 0.0, 1.0 - side, side)
    return x * cdf, cdf + x * dens * (1.0 / math.sqrt(2.0 * math.pi))


def own_rows(me, weight_ref):
    rows = weight_ref.shape[0]
    share = rows // DEVS
    ids = lax.broadcasted_iota(jnp.int32, (8, rows), 0) + me * share
    picks = (lax.broadcasted_iota(jnp.int32, (8, rows), 1) == ids).astype(f32).astype(bf16)
    return nn(picks, weight_ref[...])


def pack_rows(send_ref, at, piece_ref):
    pieces, rows, _ = piece_ref.shape
    share = rows // DEVS
    every = send_ref.shape[0] // DEVS
    for i in range(share):
        for c in range(pieces):
            block = piece_ref[c, pl.ds(i, DEVS, stride=share), :]
            send_ref[pl.ds(at, DEVS, stride=every), :] = block
            at += 1
    return at


def fill_rows(send_ref, at):
    every = send_ref.shape[0] // DEVS
    for j in range(at, every):
        send_ref[pl.ds(j, DEVS, stride=every), :] = jnp.zeros((DEVS, 128), f32)


def cut_pieces(piece_ref, grad_ref):
    for c in range(piece_ref.shape[0]):
        piece_ref[c] = grad_ref[:, c * 128 : (c + 1) * 128]


def turn_pieces(piece_ref, grad_t_ref):
    for c in range(piece_ref.shape[0]):
        piece_ref[c] = grad_t_ref[c * 128 : (c + 1) * 128].T


def one_hot_of(relief_col, classes):
    ids = lax.broadcasted_iota(jnp.int32, (relief_col.shape[0], classes), 1)
    return (relief_col == ids).astype(f32).astype(bf16)


def alone(part, place, count):
    parts = [jnp.zeros_like(part)] * count
    parts[place] = part
    return jnp.concatenate(parts, 0)


def stream_of(x_ref, relief_ref, table_ref):
    one_hot = one_hot_of(relief_ref[...], table_ref.shape[0])
    return x_ref[...].astype(f32) + nn(one_hot, table_ref[...]), one_hot


def att_kernel(
    x_ref,
    relief_ref,
    table_ref,
    gain_ref,
    wt_ref,
    wv_ref,
    wk_ref,
    wproj_ref,
    bias_ref,
    stream2_ref,
    qkt_ref,
    v_ref,
    prob_ref,
    att_ref,
):
    stream, _ = stream_of(x_ref, relief_ref, table_ref)
    hat, _ = normalize(stream)
    normed = (hat * gain_ref[...]).astype(bf16)
    d = normed.shape[1]
    count, win = att_ref.shape[0], att_ref.shape[2]
    k_tok = nn(normed, wk_ref[...]).astype(bf16)
    v_tok = nn(normed, wv_ref[...]).astype(bf16)
    e = d // HEADS
    per = 128 // e
    qkvts = []
    for u in range(count):
        rows = slice(u * win, (u + 1) * win)
        filled = jnp.concatenate([normed[rows], jnp.zeros((WIDE - win, d), bf16)], 0)
        qkvts.append(nt(wt_ref[...], filled))
    mixed = []
    for u in range(count):
        rows = slice(u * win, (u + 1) * win)
        qt = (qkvts[u][:d] * (log2_e * e**-0.5)).astype(bf16)
        kt = qkvts[u][d : 2 * d].astype(bf16)
        vt = qkvts[u][2 * d :].astype(bf16)
        att = []
        for g in range(d // 128):
            k_four = k_tok[rows, g * 128 : (g + 1) * 128]
            heads = range(g * per, (g + 1) * per)
            scores = [nn(k_four, alone(qt[h * e : (h + 1) * e], h % per, per)) for h in heads]
            probs = []
            for h, score in zip(heads, scores):
                score = score + bias_ref[h]
                top = jnp.max(score, 0, keepdims=True)
                prob = jnp.exp2(score - top)
                prob = (prob * (1.0 / jnp.sum(prob, 0, keepdims=True))).astype(bf16)
                probs.append(prob)
                prob_ref[u, h] = prob
            att += [nn(vt[h * e : (h + 1) * e, :win], prob) for h, prob in zip(heads, probs)]
        att = jnp.concatenate(att, 0).astype(bf16)[:, :win]
        att_ref[u] = att
        qkt_ref[u, :d] = qt
        qkt_ref[u, d:] = kt
        mixed.append(tn(att, wproj_ref[...]).astype(bf16))
    v_ref[...] = v_tok
    stream2_ref[...] = stream + jnp.concatenate(mixed, 0).astype(f32)


def tail_kernel(
    me_ref,
    scale_ref,
    stream2_ref,
    targ_ref,
    relief_ref,
    levels_ref,
    base_ref,
    att_ref,
    gain_ref,
    wup_ref,
    wdown_ref,
    wout_ref,
    num_ref,
    gs2_ref,
    send_ref,
    wsel_ref,
    lev_ref,
    wide_ref,
    gproj_ref,
    gup_ref,
    gdown_ref,
    gout_ref,
    piece_ref,
    gdown_t_ref,
    pack_ref,
    *,
    block_f,
):
    step = pl.program_id(0)
    me = me_ref[0]

    @pl.when(step == 0)
    def _():
        slots, rows = levels_ref.shape[0], base_ref.shape[0]
        shape = lev_ref.shape
        token = lax.broadcasted_iota(jnp.int32, shape, 0)
        upper = (lax.broadcasted_iota(jnp.int32, shape, 1) // 16) % 2
        line = token // WIN_LON
        lev = jnp.full(shape, 2 * levels_ref[0], jnp.int32)
        for s in range(1, slots):
            lev = jnp.where(line >= s * rows, 2 * levels_ref[s], lev)
        lev_ref[...] = lev + upper
        wide = jnp.zeros(shape, f32)
        for r in range(rows):
            wide = jnp.where(line % rows == r, base_ref[r : r + 1], wide)
        wide_ref[...] = wide
        num_ref[...] = jnp.zeros_like(num_ref)
        gproj_ref[...] = jnp.zeros_like(gproj_ref)
        gup_ref[...] = jnp.zeros_like(gup_ref)
        gdown_ref[...] = jnp.zeros_like(gdown_ref)
        gout_ref[...] = jnp.zeros_like(gout_ref)

    stream2 = stream2_ref[...]
    wins, win = att_ref.shape[0], att_ref.shape[2]
    ff = wup_ref.shape[1]
    hat, rstd = normalize(stream2)
    gain = gain_ref[...]
    normed2 = (hat * gain).astype(bf16)
    hids, slopes, gpres = [], [], []
    for n in range(0, ff, block_f):
        cols = slice(n, n + block_f)
        hidden, slope = gelu_both(nn(normed2, wup_ref[:, cols]))
        hids.append(hidden.astype(bf16))
        slopes.append(slope.astype(bf16))
    field = (stream2 + nn(jnp.concatenate(hids, 1), wdown_ref[...])).astype(bf16)
    pred = nn(field, wout_ref[...])
    relief = relief_ref[...]
    lev = jnp.concatenate([lev_ref[...]] * wins, 0)
    base = jnp.concatenate([wide_ref[...]] * wins, 0)
    cell_w = jnp.where(lev >= relief, base, 0.0)
    differ = pred - targ_ref[...].astype(f32)
    square = differ * differ + smooth_sq
    inv_err = lax.rsqrt(square)
    num_ref[...] += jnp.sum(cell_w * (square * inv_err), 0, keepdims=True)
    gpred = (scale_ref[0] * cell_w * differ * inv_err).astype(bf16)
    out = gpred.shape[1]
    gout_ref[:, :out] += nn(field.T, gpred)
    gfield = nt(gpred, wout_ref[...])
    gfb = gfield.astype(bf16)
    gfbt = gfb.T
    normed2t = normed2.T
    for n in range(0, ff, block_f):
        cols = slice(n, n + block_f)
        ghid = nt(gfb, wdown_ref[cols, :])
        gpres.append((slopes[n // block_f].astype(f32) * ghid).astype(bf16))
    for n in range(0, ff, block_f):
        cols = slice(n, n + block_f)
        gdown_ref[:, cols] += nn(gfbt, hids[n // block_f])
        gup_ref[:, cols] += nn(normed2t, gpres[n // block_f])
    gnorm2 = nt(jnp.concatenate(gpres, 1), wup_ref[...])
    gs2 = gfield + norm_back(gnorm2 * gain, hat, rstd)
    gs2_ref[...] = gs2
    gmix = gs2.astype(bf16)
    for w in range(wins):
        gproj_ref[...] += nn(att_ref[w], gmix[w * win : (w + 1) * win])

    @pl.when(step == pl.num_programs(0) - 1)
    def _():
        wsel_ref[...] = own_rows(me, wup_ref)
        at = 0
        for ref in (gup_ref, gproj_ref, gout_ref):
            pieces = piece_ref.at[: ref.shape[1] // 128]
            cut_pieces(pieces, ref)
            at = pack_rows(pack_ref, at, pieces)
        turn_pieces(gdown_t_ref, gdown_ref)
        at = pack_rows(pack_ref, at, gdown_t_ref)
        fill_rows(pack_ref, at)
        send_ref[...] = pack_ref[...].astype(bf16)


def back_kernel(
    me_ref,
    x_ref,
    relief_ref,
    table_ref,
    gain_ref,
    wqkv_ref,
    wproj_ref,
    qkt_ref,
    v_ref,
    prob_ref,
    att_ref,
    gs2_ref,
    num_ref,
    gbias_ref,
    send_ref,
    wsel_ref,
    gqkv_ref,
    gqkv_t_ref,
    grel_ref,
    grel_t_ref,
    pack_ref,
):
    step = pl.program_id(0)

    @pl.when(step == 0)
    def _():
        gbias_ref[...] = jnp.zeros_like(gbias_ref)
        gqkv_ref[...] = jnp.zeros_like(gqkv_ref)
        grel_ref[...] = jnp.zeros_like(grel_ref)

    stream, one_hot = stream_of(x_ref, relief_ref, table_ref)
    hat, rstd = normalize(stream)
    gain = gain_ref[...]
    normed = (hat * gain).astype(bf16)
    d = normed.shape[1]
    count, win = att_ref.shape[0], att_ref.shape[2]
    e = d // HEADS
    per = 128 // e
    gs2 = gs2_ref[...]
    gmix = gs2.astype(bf16)
    pad = jnp.zeros((WIDE - win, d), bf16)
    gatts = []
    for u in range(count):
        filled = jnp.concatenate([gmix[u * win : (u + 1) * win], pad], 0)
        gatts.append(nt(wproj_ref[...], filled).astype(bf16))
    v_tok = v_ref[...]
    gshift = []
    for u in range(count):
        wrows = slice(u * win, (u + 1) * win)
        gatt_b = gatts[u]
        prod = gatt_b[:, :win].astype(f32) * att_ref[u].astype(f32)
        prod = jnp.concatenate([prod, jnp.zeros((d, WIDE - win), f32)], 1)
        qt, kt = qkt_ref[u, :d], qkt_ref[u, d:, :win]
        gqs, gks, gvs = [], [], []
        for g in range(d // 128):
            v_four = v_tok[wrows, g * 128 : (g + 1) * 128]
            heads = range(g * per, (g + 1) * per)
            gprobs = [nn(v_four, alone(gatt_b[h * e : (h + 1) * e], h % per, per)) for h in heads]
            gscores = []
            probs = [prob_ref[u, h] for h in heads]
            for h, gprob, prob in zip(heads, gprobs, probs):
                delta = jnp.sum(prod[h * e : (h + 1) * e], 0, keepdims=True)
                gscore = prob.astype(f32) * (gprob - delta)
                gbias_ref[h] += gscore
                gscores.append(gscore.astype(bf16))
            for h, gsb, prob in zip(heads, gscores, probs):
                rows = slice(h * e, (h + 1) * e)
                gqs.append((nn(kt[rows], gsb) * e**-0.5).astype(bf16)[:, :win])
                gks.append((nt(qt[rows], gsb) * (1.0 / log2_e)).astype(bf16))
                gvs.append(nt(gatt_b[rows], prob).astype(bf16))
        gheads = jnp.concatenate(gqs + gks + gvs, 0)
        gqkv_ref[...] += nn(gheads, normed[wrows])
        gshift.append(nn(wqkv_ref[...], gheads).astype(bf16).T.astype(f32))
    gshift = jnp.concatenate(gshift, 0)
    gstream = gs2 + norm_back(gshift * gain, hat, rstd)
    grel_ref[...] += tn(one_hot, gstream.astype(bf16))

    @pl.when(step == pl.num_programs(0) - 1)
    def _():
        wsel_ref[...] = own_rows(me_ref[0], wqkv_ref)
        turn_pieces(gqkv_t_ref, gqkv_ref)
        at = pack_rows(pack_ref, 0, gqkv_t_ref)
        classes = grel_ref.shape[0]
        wide = jnp.concatenate([grel_ref[...], jnp.zeros((128 - classes, d), f32)], 0)
        grel_t_ref[...] = wide.T
        share = d // DEVS
        num = jnp.sum(num_ref[...], 1, keepdims=True)
        high = num.astype(bf16).astype(f32)
        lane = lax.broadcasted_iota(jnp.int32, (DEVS, 128), 1)
        last = jnp.where(lane == 126, high, jnp.where(lane == 127, num - high, 0.0))
        for i in range(share):
            part = grel_t_ref[pl.ds(i, DEVS, stride=share), :]
            last += pltpu.roll(part, i * classes, 1) if i else part
        every = pack_ref.shape[0] // DEVS
        pack_ref[pl.ds(at, DEVS, stride=every), :] = last
        fill_rows(pack_ref, at + 1)
        send_ref[...] = pack_ref[...].astype(bf16)


def assemble_kernel(own_ref, up_ref, side_ref, both_ref, out_ref, scr_ref):
    slots, rows, lon, _ = own_ref.shape
    hs, hr = slots // 2, rows // 2
    half = WIN_LON // 2
    win = slots * rows * WIN_LON
    for s in range(slots):
        for r in range(rows):
            if s < hs:
                plane = own_ref[hs + s, hr + r] if r < hr else side_ref[s, r - hr]
            else:
                plane = up_ref[s - hs, r] if r < hr else both_ref[s - hs, r - hr]
            plane = plane.astype(f32)
            plane = jnp.concatenate([plane[half:], plane[:half]], 0)
            for w in range(lon // WIN_LON):
                at = w * win + (s * rows + r) * WIN_LON
                scr_ref[at : at + WIN_LON] = plane[w * WIN_LON : (w + 1) * WIN_LON]
    out_ref[...] = scr_ref[...].astype(bf16)


def assemble(own, up, side, both):
    count = own.shape[0] * own.shape[1] * own.shape[2]
    return pl.pallas_call(
        assemble_kernel,
        out_shape=jax.ShapeDtypeStruct((count, own.shape[3]), bf16),
        scratch_shapes=[pltpu.VMEM((count, own.shape[3]), f32)],
        compiler_params=pltpu.CompilerParams(vmem_limit_bytes=40 * 2**20),
        name="assemble_windows",
    )(own, up, side, both)


def finish_kernel(
    weight_sum_ref, gott_ref, gotq_ref, wup_ref, wqkv_ref, gmlp_ref, gatt_ref, *outs
):
    loss_ref, gqkv_ref, gproj_ref, gup_ref, gdown_ref, gout_ref, ga_ref, gm_ref, grel_ref = outs
    got = jnp.sum(gott_ref[...].astype(f32), 0)
    at = 0
    for ref in (gup_ref, gproj_ref, gout_ref, gdown_ref):
        rows, cols = ref.shape
        for i in range(rows):
            for c in range(0, cols, 128):
                size = min(128, cols - c)
                ref[i : i + 1, c : c + size] = got[at : at + 1, :size]
                at += 1
    got = jnp.sum(gotq_ref[...].astype(f32), 0)
    at = 0
    rows, cols = gqkv_ref.shape
    for i in range(rows):
        for c in range(0, cols, 128):
            gqkv_ref[i : i + 1, c : c + 128] = got[at : at + 1]
            at += 1
    last = got[at : at + 1]
    classes = grel_ref.shape[1]
    for i in range(rows):
        grel_ref[i : i + 1, :] = last[:, i * classes : (i + 1) * classes]
    loss_ref[...] = (last[:, 126:127] + last[:, 127:128]) / weight_sum_ref[0]
    ga_ref[...] = jnp.sum(wqkv_ref[:rows] * gqkv_ref[...], 1, keepdims=True) / gatt_ref[...]
    gm_ref[...] = jnp.sum(wup_ref[:rows] * gup_ref[...], 1, keepdims=True) / gmlp_ref[...]


def finish(weight_sum, got_t, got_q, w_up, w_qkv, gain_mlp, gain_attn, shapes):
    smem = pl.BlockSpec(memory_space=pltpu.SMEM)
    vmem = pl.BlockSpec(memory_space=pltpu.VMEM)
    return pl.pallas_call(
        finish_kernel,
        in_specs=[smem] + [vmem] * 6,
        out_specs=[vmem] * len(shapes),
        out_shape=[jax.ShapeDtypeStruct(shape, f32) for shape in shapes],
        compiler_params=pltpu.CompilerParams(vmem_limit_bytes=40 * 2**20),
        name="finish_sums",
    )(weight_sum, got_t, got_q, w_up, w_qkv, gain_mlp, gain_attn)


def whole(shape):
    return pl.BlockSpec(shape, lambda i: (0,) * len(shape))


def lead(shape):
    return pl.BlockSpec(shape, lambda i: (i,) + (0,) * (len(shape) - 1))


def params_of():
    return pltpu.CompilerParams(
        vmem_limit_bytes=56 * 2**20, dimension_semantics=("arbitrary",)
    )


def attention_forward(x, relief_col, table, gain, w_qkv, wt, w_proj, bias_t):
    t, d = x.shape
    win = bias_t.shape[1]
    count = t // win
    sds = jax.ShapeDtypeStruct
    return pl.pallas_call(
        att_kernel,
        grid=(count // TOGETHER,),
        in_specs=[
            lead((TOGETHER * win, d)),
            lead((TOGETHER * win, 1)),
            whole(table.shape),
            whole((1, d)),
            whole((3 * d, d)),
            whole((d, d)),
            whole((d, d)),
            whole((d, d)),
            whole(bias_t.shape),
        ],
        out_specs=[
            lead((TOGETHER * win, d)),
            lead((TOGETHER, 2 * d, WIDE)),
            lead((TOGETHER * win, d)),
            lead((TOGETHER, HEADS, win, WIDE)),
            lead((TOGETHER, d, win)),
        ],
        out_shape=[
            sds((t, d), f32),
            sds((count, 2 * d, WIDE), bf16),
            sds((t, d), bf16),
            sds((count, HEADS, win, WIDE), bf16),
            sds((count, d, win), bf16),
        ],
        compiler_params=params_of(),
        name="attention_forward",
    )(
        x,
        relief_col,
        table,
        gain[None],
        wt,
        w_qkv[:, 2 * d :],
        w_qkv[:, d : 2 * d],
        w_proj,
        bias_t,
    )


def cost(flops, moved, trans):
    return pl.CostEstimate(flops=flops, bytes_accessed=moved, transcendentals=trans)


def tail_both(me, scale, stream2, targ, relief_col, lev, base, att, gain, w_up, w_down, w_out, group):
    t, d = stream2.shape
    win = att.shape[-1]
    m = group * win
    ff, out = w_up.shape[1], w_out.shape[1]
    pieces = (d * ff + d * d + d * 256 + d * ff) // (DEVS * 128)
    pieces += -pieces % 8
    sds = jax.ShapeDtypeStruct
    return pl.pallas_call(
        functools.partial(tail_kernel, block_f=256),
        grid=(t // m,),
        in_specs=[
            pl.BlockSpec(memory_space=pltpu.SMEM),
            pl.BlockSpec(memory_space=pltpu.SMEM),
            lead((m, d)),
            lead((m, out)),
            lead((m, 1)),
            pl.BlockSpec(memory_space=pltpu.SMEM),
            whole(base.shape),
            lead((group, d, win)),
            whole((1, d)),
            whole((d, ff)),
            whole((ff, d)),
            whole((d, out)),
        ],
        out_specs=[
            whole((1, out)),
            lead((m, d)),
            whole((DEVS * pieces, 128)),
            whole((8, ff)),
        ],
        out_shape=[
            sds((1, out), f32),
            sds((t, d), f32),
            sds((DEVS * pieces, 128), bf16),
            sds((8, ff), f32),
        ],
        scratch_shapes=[
            pltpu.VMEM((win, out), jnp.int32),
            pltpu.VMEM((win, out), f32),
            pltpu.VMEM((d, d), f32),
            pltpu.VMEM((d, ff), f32),
            pltpu.VMEM((d, ff), f32),
            pltpu.VMEM((d, 256), f32),
            pltpu.VMEM((ff // 128, d, 128), f32),
            pltpu.VMEM((d // 128, ff, 128), f32),
            pltpu.VMEM((DEVS * pieces, 128), f32),
        ],
        compiler_params=params_of(),
        name="tail_both",
    )(me, scale, stream2, targ, relief_col, lev, base, att, gain[None], w_up, w_down, w_out)


def attention_back(me, num, x, relief_col, table, gain, w_qkv, w_proj, qkt, v_tok, probs, att, gs2):
    t, d = x.shape
    count, win = att.shape[0], att.shape[2]
    sds = jax.ShapeDtypeStruct
    return pl.pallas_call(
        back_kernel,
        grid=(count // TOGETHER,),
        in_specs=[
            pl.BlockSpec(memory_space=pltpu.SMEM),
            lead((TOGETHER * win, d)),
            lead((TOGETHER * win, 1)),
            whole(table.shape),
            whole((1, d)),
            whole((d, 3 * d)),
            whole((d, d)),
            lead((TOGETHER, 2 * d, WIDE)),
            lead((TOGETHER * win, d)),
            lead((TOGETHER, HEADS, win, WIDE)),
            lead((TOGETHER, d, win)),
            lead((TOGETHER * win, d)),
            whole(num.shape),
        ],
        out_specs=[
            whole((HEADS, win, WIDE)),
            whole((DEVS * 32, 128)),
            whole((8, 3 * d)),
        ],
        out_shape=[
            sds((HEADS, win, WIDE), f32),
            sds((DEVS * 32, 128), bf16),
            sds((8, 3 * d), f32),
        ],
        scratch_shapes=[
            pltpu.VMEM((3 * d, d), f32),
            pltpu.VMEM((3 * d // 128, d, 128), f32),
            pltpu.VMEM((table.shape[0], d), f32),
            pltpu.VMEM((d, 128), f32),
            pltpu.VMEM((DEVS * 32, 128), f32),
        ],
        compiler_params=params_of(),
        cost_estimate=cost(10 * 2**30, 20 * 2**20, 0),
        name="attention_back",
    )(me, x, relief_col, table, gain[None], w_qkv, w_proj, qkt, v_tok, probs, att, gs2, num)


def lat_weights(row_ids, lat_rows):
    fine_rows = 4 * row_ids[:, None] + jnp.arange(4, dtype=jnp.int32)[None, :]
    angle_rad = (90.0 - 180.0 * (fine_rows.astype(f32) + 0.5) / (4.0 * lat_rows)) * (
        math.pi / 180.0
    )
    return jnp.cos(angle_rad)


def weight_total(relief, var_weight, level_count):
    lat_rows = relief.shape[0]
    lat_weight = jnp.sum(lat_weights(jnp.arange(lat_rows, dtype=jnp.int32), lat_rows), 1)
    live_levels = (2 * level_count - relief).astype(f32)
    return jnp.sum(var_weight) * 4.0 * jnp.sum(lat_weight[:, None] * live_levels)


def window_mask(last_level, last_band, slots_n, rows_n, win_lon):
    slot_label = jnp.where(last_level & (jnp.arange(slots_n) >= slots_n // 2), 2, 0)
    row_label = jnp.where(last_band & (jnp.arange(rows_n) >= rows_n // 2), 1, 0)
    labels = (
        slot_label[:, None, None] + row_label[None, :, None] + jnp.zeros((1, 1, win_lon), jnp.int32)
    )
    labels = labels.reshape(-1)
    return labels[:, None] == labels[None, :]


def windows(field_in):
    slots_n, rows_n, lon_n, chans = field_in.shape
    count_w = lon_n // WIN_LON
    parted = field_in.reshape(slots_n, rows_n, count_w, WIN_LON, chans).transpose(2, 0, 1, 3, 4)
    return parted.reshape(count_w * slots_n * rows_n * WIN_LON, chans)


def from_next(value, axes):
    sizes = [lax.axis_size(a) for a in ("lvl", "lat")]
    move = [1 if a in axes else 0 for a in ("lvl", "lat")]
    pairs = []
    for i in range(sizes[0]):
        for j in range(sizes[1]):
            src = (i + move[0]) % sizes[0] * sizes[1] + (j + move[1]) % sizes[1]
            pairs.append((src, i * sizes[1] + j))
    return lax.ppermute(value, ("lvl", "lat"), pairs)


def halo_of(field_in):
    slots_n, rows_n = field_in.shape[:2]
    hs, hr = slots_n // 2, rows_n // 2
    up = from_next(field_in[:hs, hr:], ("lvl",))
    side = from_next(field_in[hs:, :hr], ("lat",))
    both = from_next(field_in[:hs, :hr], ("lvl", "lat"))
    return up, side, both


def local_inputs(tokens_shape, relief, earth_bias, var_weight):
    slots_dev, rows_dev, lon_cells, _ = tokens_shape
    lvl_count, lat_count = lax.axis_size("lvl"), lax.axis_size("lat")
    lvl_id, lat_id = lax.axis_index("lvl"), lax.axis_index("lat")
    level_total, lat_rows = slots_dev * lvl_count, rows_dev * lat_count
    allowed = window_mask(
        lvl_id == lvl_count - 1, lat_id == lat_count - 1, slots_dev, rows_dev, WIN_LON
    )
    level_ids = (
        lvl_id * slots_dev + jnp.arange(slots_dev, dtype=jnp.int32) + slots_dev // 2
    ) % level_total
    row_ids = (
        lat_id * rows_dev + jnp.arange(rows_dev, dtype=jnp.int32) + rows_dev // 2
    ) % lat_rows
    relief_blk = jnp.roll(jnp.take(relief, row_ids, axis=0), -(WIN_LON // 2), 1)
    relief_col = windows(
        jnp.broadcast_to(relief_blk[None, :, :, None], (slots_dev, rows_dev, lon_cells, 1))
    )
    vars_n = var_weight.shape[0]
    base = jnp.broadcast_to(
        var_weight[None, :, None, None, None]
        * lat_weights(row_ids, lat_rows)[:, None, None, :, None],
        (rows_dev, vars_n, 2, 4, 4),
    ).reshape(rows_dev, vars_n * 32)
    bias_t = jnp.where(allowed, earth_bias.transpose(0, 2, 1) * log2_e, masked_score)
    bias_t = jnp.pad(bias_t, ((0, 0), (0, 0), (0, WIDE - bias_t.shape[2])))
    return relief_col, level_ids, base, bias_t


def body(
    tokens,
    targets,
    relief,
    earth_bias,
    relief_table,
    gain_attn,
    gain_mlp,
    w_qkv,
    w_proj,
    w_up,
    w_down,
    w_out,
    var_weight,
):
    axes = ("lvl", "lat")
    devs = lax.axis_size("lvl") * lax.axis_size("lat")
    level_total = tokens.shape[0] * lax.axis_size("lvl")
    weight_sum = weight_total(relief, var_weight, level_total)
    token_halo = halo_of(tokens)
    targ_halo = halo_of(targets)
    relief_col, lev, base, bias_t = local_inputs(tokens.shape, relief, earth_bias[0, 0], var_weight)
    scale = (loss_scale / weight_sum).reshape(1)
    wt = w_qkv.T
    tokens, relief_col, bias_t, base, scale, wt = lax.optimization_barrier(
        (tokens, relief_col, bias_t, base, scale, wt)
    )
    x = assemble(tokens, *token_halo)
    stream2, qkt, v_tok, probs, att = attention_forward(
        x, relief_col, relief_table, gain_attn, w_qkv, wt, w_proj, bias_t
    )
    stream2, targets = lax.optimization_barrier((stream2, targets))
    targ = assemble(targets, *targ_halo)
    me = lax.axis_index(axes)
    num, gs2, send_t, up_rows = tail_both(
        me.reshape(1), scale, stream2, targ, relief_col, lev, base, att, gain_mlp, w_up, w_down, w_out, GROUP
    )
    got_t = lax.all_to_all(send_t.reshape(devs, -1, 128), axes, 0, 0, tiled=True)
    gbias_t, send_q, qkv_rows = attention_back(
        me.reshape(1), num, x, relief_col, relief_table, gain_attn, w_qkv, w_proj, qkt, v_tok, probs, att, gs2
    )
    send_q, got_t = lax.optimization_barrier((send_q.reshape(devs, -1, 128), got_t))
    got_q = lax.all_to_all(send_q, axes, 0, 0, tiled=True)
    d = tokens.shape[-1]
    share = d // devs

    def mine(array):
        return lax.dynamic_slice_in_dim(array, me * share, share, 0)[:, None]

    shapes = (
        (1, 1),
        (share, w_qkv.shape[1]),
        (share, d),
        (share, w_up.shape[1]),
        (w_down.shape[0] // devs, d),
        (share, w_out.shape[1]),
        (share, 1),
        (share, 1),
        (share, relief_table.shape[0]),
    )
    sums = finish(
        weight_sum.reshape(1), got_t, got_q, up_rows, qkv_rows, mine(gain_mlp), mine(gain_attn), shapes
    )
    return (
        sums[0][0, 0],
        *sums[1:6],
        sums[6][:, 0],
        sums[7][:, 0],
        sums[8],
        gbias_t[..., : gbias_t.shape[1]].transpose(0, 2, 1)[None, None],
    )


def solution(mesh):
    field = P("lvl", "lat", None, None)
    bias = P("lvl", "lat", None, None, None)
    rows = P(("lvl", "lat"), None)
    vec = P(("lvl", "lat"))
    return jax.shard_map(
        body,
        mesh=mesh,
        in_specs=(field, field, P(), bias) + (P(),) * 9,
        out_specs=(P(), rows, rows, rows, rows, rows, vec, vec, rows, bias),
        check_vma=False,
    )
```

time: 278 us -> 180 us (0.65)
  Pallas kernels: 137 us -> 95.4 us
  waiting for transfers between devices: 44.7 us -> 18.6 us
  local copies, waits for them, and re-layouts: 46.4 us -> 28.1 us
  other arithmetic: 23 us -> 7.2 us
  starting transfers between devices: 19.3 us -> 26.7 us
  between operations: 6.18 us -> 2.21 us
    pallas_call x2 -> x5, Pallas kernels: 99.9 us -> 62.4 us  [the longest x1 31.7 us: attention_back(): pl.pallas_call(back_kernel, grid=(count // TOGETHER,), in_specs=[pl.Block...]
    all_to_all x1 -> x2, waiting for transfers between devices: 44.7 us -> 18.5 us  [the longest x1 11.7 us: body(): got_q = lax.all_to_all(send_q, axes, 0, 0, tiled=True)]
    reshape x15 -> x1, local copies, waits for them, and re-layouts: 10.2 us -> 0.74 us  [local_inputs(): base = jnp.broadcast_to(var_weight[None, :, None, None, None] * lat_weigh...]
    all_to_all x1 -> x2, starting transfers between devices: 6.04 us -> 14.3 us  [the longest x1 8.58 us: body(): lax.all_to_all(send_t.reshape(devs, -1, 128), axes, 0, 0, tiled=True)]
    concatenate x3 -> x0, local copies, waits for them, and re-layouts: 7.92 us -> none  [the longest x1 5.99 us: body(): send = jnp.concatenate([high, low_num], 1)]
    reduce_sum x4 -> x0, other arithmetic: 5.73 us -> none  [the longest x1 2.6 us: body(): total = jnp.sum(got.astype(f32), 0).reshape(-1)]
    concatenate x4 -> x0, other arithmetic: 4.31 us -> none  [the longest x2 2.51 us: shifted_windows(): jnp.concatenate([jnp.concatenate([field_in[hs:, hr:], side], 1), jnp.conc...]
    pallas_call x1, Pallas kernels: 37.3 us -> 33 us  [tail_both(): pl.pallas_call(functools.partial(tail_kernel, block_f=256), grid=(t // m,...]
  transfers between devices with their start and end apart: 7 -> 8, of which waited for: 1 -> 2; matrix products, arithmetic and copies ran while one was open for 9% -> 17% of each run, Pallas kernels for 0% -> 33%
where the time goes in v2:
time: 180 us; the launch traced here: 178 us
  Pallas kernels  95.4 us (53%)
  local copies, waits for them, and re-layouts  28.1 us (16%)
  starting transfers between devices  26.7 us (15%)
  waiting for transfers between devices  18.6 us (10%)
  other arithmetic  7.2 us (4%)
  between operations  2.21 us (1%)
    pallas_call x1, Pallas kernels, tail_both(): pl.pallas_call(functools.partial(tail_kernel, block_f=256), grid=(t // m,...  33 us
    pallas_call x1, Pallas kernels, attention_back(): pl.pallas_call(back_kernel, grid=(count // TOGETHER,), in_specs=[pl.Block...  31.7 us
    pallas_call x1, Pallas kernels, attention_forward(): pl.pallas_call(att_kernel, grid=(count // TOGETHER,), in_specs=[lead((TOG...  26.3 us
    ppermute x6, starting transfers between devices, from_next(): return lax.ppermute(value, ('lvl', 'lat'), pairs)  12.4 us
    all_to_all x1, waiting for transfers between devices, body(): got_q = lax.all_to_all(send_q, axes, 0, 0, tiled=True)  11.7 us
    unnamed x27, local copies, waits for them, and re-layouts  11.2 us
    all_to_all x1, starting transfers between devices, body(): lax.all_to_all(send_t.reshape(devs, -1, 128), axes, 0, 0, tiled=True)  8.58 us
    all_to_all x1, waiting for transfers between devices, body(): lax.all_to_all(send_t.reshape(devs, -1, 128), axes, 0, 0, tiled=True)  6.83 us
  transfers between devices with their start and end apart: 8, of which 2 were waited for; matrix products, arithmetic and copies ran while one was open for 17% of the time, Pallas kernels for 33%

profile of v2, /device:TPU:0, one launch (start us, length us, event | category | flops | bytes accessed | tf_op | source)
XLA Modules:
  0.0 178.2 jit_solution(13894768074752347566)
XLA Ops:
  0.7 2.2 %fusion.2 = (bf16[1,3,144,384]{3,2,1,0:T(8,128)(2,1)}, bf16[1,3,144,384]{3,2,1,0:T(8,128)(2,1)}, bf16[1,3,144,384]{3,2,1,0:T(8,128)(2,1)}) fusion(bf16[2,6,144,384]{3,2,1,0:T(8,128)(2,1)} %own_ref), kind=kLoop, calls=%fused_computation.29 | loop fusion | bytes 1990656 | tf_op jit(solution)/shard_map/slice | solution.py:673
  2.9 2.7 %collective-permute-start = (bf16[1,3,144,384]{3,2,1,0:T(8,128)(2,1)}, bf16[1,3,144,384]{3,2,1,0:T(8,128)(2,1)S(1)}, u32[]{:S(2)}, u32[]{:S(2)}) collective-permute-start(bf16[1,3,144,384]{3,2,1,0:T(8,128)(2,1)} %get-tuple-element.103), channel_id=1, source_target_pairs={{32,0},{33,1},{34,2},{35,3},{36,4},{37,5},{38,6},{39,7},{40,8},{41... | collective-permute-start | bytes 995336 | tf_op jit(solution)/shard_map/ppermute | solution.py:665
  5.6 6.3 %collective-permute-start.1 = (bf16[1,3,144,384]{3,2,1,0:T(8,128)(2,1)}, bf16[1,3,144,384]{3,2,1,0:T(8,128)(2,1)S(1)}, u32[]{:S(2)}, u32[]{:S(2)}) collective-permute-start(bf16[1,3,144,384]{3,2,1,0:T(8,128)(2,1)} %get-tuple-element.104), channel_id=1, source_target_pairs={{1,0},{2,1},{3,2},{4,3},{5,4},{6,5},{7,6},{8,7},{9,8},{10,9},{11,1... | collective-permute-start | bytes 995336 | tf_op jit(solution)/shard_map/ppermute | solution.py:665
  13.1 1.4 collective-permute-start.3
  14.5 1.6 collective-permute-start.4
  17.2 3.1 %copy.44 = f32[1,1,12,144,144]{3,4,2,1,0:T(8,128)} copy(f32[1,1,12,144,144]{4,3,2,1,0:T(8,128)} %param.16) | data formatting | bytes 1990656 | tf_op args[3]
  21.7 2.9 %bitcast_select_fusion = f32[12,144,144]{2,1,0:T(8,128)} fusion(f32[1,1,12,144,144]{3,4,2,1,0:T(8,128)} %copy.44, pred[144,144]{1,0:T(8,128)(4,1)S(1)} %broadcast_compare_fusion), kind=kLoop, calls=%fused_computation.1 | loop fusion | flops 497664 | bytes 2011392 | tf_op jit(solution)/shard_map/jit(_where)/select_n | solution.py:701
  26.1 1.3 copy.45
  28.7 3.0 %pad.4.bias_ref = f32[12,144,256]{2,1,0:T(8,128)} pad(f32[12,144,144]{2,1,0:T(8,128)} %bitcast_select_fusion, f32[]{:T(128)} %constant.28.clone.1), padding=0_0x0_0x0_112 | pad | bytes 2764804 | tf_op jit(solution)/shard_map/jit(_pad)/pad | solution.py:702
  33.9 1.9 %copy.49.relief_ref = s32[1728,1]{1,0:T(8,128)} copy(s32[1728,1]{0,1:T(1,128)} %reshape.183) | data formatting | bytes 13824 | tf_op jit(solution)/shard_map/optimization_barrier | solution.py:730
  36.4 1.2 broadcast_in_dim.81.gain_ref
  37.6 1.7 copy.48.wout_ref
  40.4 1.0 copy-done
  41.4 26.3 %attention_forward.1 = (f32[1728,384]{1,0:T(8,128)}, bf16[12,768,256]{2,1,0:T(8,128)(2,1)}, bf16[1728,384]{1,0:T(8,128)(2,1)}, bf16[12,12,144,256]{3,2,1,0:T(8,128)(2,1)}, bf16[12,384,144]{2,1,0:T(8,128)(2,1)}) custom-call(bf16[1728,384]{1,0:T(8,128)(2,1)} %copy-done, s32[1728,1]{1,0:T(8,128)} %copy.49.relief_ref, bf16[4,384]{1,0:T(4,128)(2,1)} %table_ref.3, ...), custom_call_target="tpu_custom_call" | custom-call | tf_op jit(solution)/shard_map/attention_forward/pallas_call | solution.py:480
  67.8 1.4 assemble_windows.3.targ_ref
  70.0 33.0 %tail_both.1 = (f32[1,160]{1,0:T(1,128)}, f32[1728,384]{1,0:T(8,128)}, bf16[11264,128]{1,0:T(8,128)(2,1)}, f32[8,1536]{1,0:T(8,128)}) custom-call(s32[1]{0:T(128)} %bitcast.1.me_ref, f32[1]{0:T(128)} %bitcast.6.scale_ref, f32[1728,384]{1,0:T(8,128)} %get-tuple-element.51.stream2_ref, bf16[1728,160]{1,0:T(8,128)(2,1)} %copy-done.2, ...), custom_call_target="tpu_custom_call" | custom-call | tf_op jit(solution)/shard_map/tail_both/pallas_call | solution.py:535
  103.1 8.6 %all-to-all-start = ((bf16[128,88,128]{2,1,0:T(8,128)(2,1)}), bf16[128,88,128]{2,1,0:T(8,128)(2,1)S(1)}, u32[]{:S(2)}, u32[]{:S(2)}) async-start(bf16[128,88,128]{2,1,0:T(8,128)(2,1)} %bitcast.26), calls=%async_computation | async-start | bytes 5767168 | tf_op jit(solution)/shard_map/all_to_all | solution.py:743
  111.6 31.7 %attention_back.1 = (f32[12,144,256]{2,1,0:T(8,128)}, bf16[4096,128]{1,0:T(8,128)(2,1)}, f32[8,1152]{1,0:T(8,128)}) custom-call(s32[1]{0:T(128)} %bitcast.1.me_ref, bf16[1728,384]{1,0:T(8,128)(2,1)} %copy-done, s32[1728,1]{1,0:T(8,128)} %copy.49.relief_ref, bf16[4,384]{1,0:T(4,128)(2,1)} %table_ref.3, f32[1,384]{1,0:T(1,128)} %broadcast_in_dim.80.gain_ref, ...), custom_call_target="tpu_custom_call" | custom-call | flops 10737418240 | bytes 20971520 | tf_op jit(solution)/shard_map/attention_back/pallas_call | solution.py:584
  143.4 6.8 %all-to-all-done.gott_ref = bf16[128,88,128]{2,1,0:T(8,128)(2,1)S(1)} async-done(((bf16[128,88,128]{2,1,0:T(8,128)(2,1)}), bf16[128,88,128]{2,1,0:T(8,128)(2,1)S(1)}, u32[]{:S(2)}, u32[]{:S(2)}) %all-to-all-start) | async-done | bytes 2883616 | tf_op jit(solution)/shard_map/all_to_all | solution.py:743
  150.2 5.8 %all-to-all-start.1 = ((bf16[128,32,128]{2,1,0:T(8,128)(2,1)}), bf16[128,32,128]{2,1,0:T(8,128)(2,1)}, u32[]{:S(2)}, u32[]{:S(2)}) async-start(bf16[128,32,128]{2,1,0:T(8,128)(2,1)} %bitcast.27), calls=%async_computation.1 | async-start | bytes 2097152 | tf_op jit(solution)/shard_map/all_to_all | solution.py:748
  156.9 2.8 %slice_bitcast_fusion = f32[1,1,12,144,144]{3,4,2,1,0:T(8,128)} fusion(f32[12,144,256]{2,1,0:T(8,128)} %get-tuple-element.71), kind=kLoop, calls=%fused_computation.2 | loop fusion | bytes 1990656 | tf_op jit(solution)/shard_map/broadcast_in_dim | solution.py:775
  159.8 3.0 %copy.52 = f32[1,1,12,144,144]{4,3,2,1,0:T(8,128)} copy(f32[1,1,12,144,144]{3,4,2,1,0:T(8,128)} %slice_bitcast_fusion) | data formatting | bytes 1990656
  162.7 11.7 %all-to-all-done.1.gotq_ref = bf16[128,32,128]{2,1,0:T(8,128)(2,1)} async-done(((bf16[128,32,128]{2,1,0:T(8,128)(2,1)}), bf16[128,32,128]{2,1,0:T(8,128)(2,1)}, u32[]{:S(2)}, u32[]{:S(2)}) %all-to-all-start.1) | async-done | bytes 1048608 | tf_op jit(solution)/shard_map/all_to_all | solution.py:748
  174.4 2.5 %finish_sums.1 = (f32[1,1]{1,0:T(1,128)}, f32[3,1152]{1,0:T(4,128)}, f32[3,384]{1,0:T(4,128)}, f32[3,1536]{1,0:T(4,128)}, f32[12,384]{1,0:T(8,128)}, /*index=5*/...) custom-call(f32[1]{0:T(128)} %bitcast.weight_sum_ref, ...), custom_call_target="tpu_custom_call" | custom-call | tf_op jit(solution)/shard_map/finish_sums/pallas_call | solution.py:451
  (67 shorter events, 11.9 us)
Async XLA Ops:
  0.6 11.6 %copy-start.3 = (bf16[2,6,144,160]{3,2,1,0:T(8,128)(2,1)S(1)}, bf16[2,6,144,160]{3,2,1,0:T(8,128)(2,1)}, u32[]{:S(2)}) copy-start(bf16[2,6,144,160]{3,2,1,0:T(8,128)(2,1)} %own_ref.1) | copy-start | bytes 1658884
  0.7 15.5 %copy-start.7 = (s32[192,144]{0,1:T(8,128)S(1)}, s32[192,144]{0,1:T(8,128)}, u32[]{:S(2)}) copy-start(s32[192,144]{0,1:T(8,128)} %param.15) | copy-start | bytes 331780
  2.9 22.5 %collective-permute-start = (bf16[1,3,144,384]{3,2,1,0:T(8,128)(2,1)}, bf16[1,3,144,384]{3,2,1,0:T(8,128)(2,1)S(1)}, u32[]{:S(2)}, u32[]{:S(2)}) collective-permute-start(bf16[1,3,144,384]{3,2,1,0:T(8,128)(2,1)} %get-tuple-element.103), channel_id=1, source_target_pairs={{32,0},{33,1},{34,2},{35,3},{36,4},{37,5},{38,6},{39,7},{40,8},{41... | collective-permute-start | bytes 995336 | tf_op jit(solution)/shard_map/ppermute | solution.py:665
  5.6 34.2 %collective-permute-start.1 = (bf16[1,3,144,384]{3,2,1,0:T(8,128)(2,1)}, bf16[1,3,144,384]{3,2,1,0:T(8,128)(2,1)S(1)}, u32[]{:S(2)}, u32[]{:S(2)}) collective-permute-start(bf16[1,3,144,384]{3,2,1,0:T(8,128)(2,1)} %get-tuple-element.104), channel_id=1, source_target_pairs={{1,0},{2,1},{3,2},{4,3},{5,4},{6,5},{7,6},{8,7},{9,8},{10,9},{11,1... | collective-permute-start | bytes 995336 | tf_op jit(solution)/shard_map/ppermute | solution.py:665
  12.0 27.9 %collective-permute-start.2 = (bf16[1,3,144,384]{3,2,1,0:T(8,128)(2,1)}, bf16[1,3,144,384]{3,2,1,0:T(8,128)(2,1)S(1)}, u32[]{:S(2)}, u32[]{:S(2)}) collective-permute-start(bf16[1,3,144,384]{3,2,1,0:T(8,128)(2,1)} %get-tuple-element.102), channel_id=1, source_target_pairs={{33,0},{34,1},{35,2},{36,3},{37,4},{38,5},{39,6},{40,7},{41,8},{42... | collective-permute-start | bytes 995336 | tf_op jit(solution)/shard_map/ppermute | solution.py:665
  13.1 54.6 %collective-permute-start.3 = (bf16[1,3,144,160]{3,2,1,0:T(8,128)(2,1)}, bf16[1,3,144,160]{3,2,1,0:T(8,128)(2,1)S(1)}, u32[]{:S(2)}, u32[]{:S(2)}) collective-permute-start(bf16[1,3,144,160]{3,2,1,0:T(8,128)(2,1)} %get-tuple-element.106), channel_id=1, source_target_pairs={{32,0},{33,1},{34,2},{35,3},{36,4},{37,5},{38,6},{39,7},{40,8},{41... | collective-permute-start | bytes 414728 | tf_op jit(solution)/shard_map/ppermute | solution.py:665
  14.5 53.2 %collective-permute-start.4 = (bf16[1,3,144,160]{3,2,1,0:T(8,128)(2,1)}, bf16[1,3,144,160]{3,2,1,0:T(8,128)(2,1)}, u32[]{:S(2)}, u32[]{:S(2)}) collective-permute-start(bf16[1,3,144,160]{3,2,1,0:T(8,128)(2,1)} %get-tuple-element.107), channel_id=1, source_target_pairs={{1,0},{2,1},{3,2},{4,3},{5,4},{6,5},{7,6},{8,7},{9,8},{10,9},{11,1... | collective-permute-start | bytes 414728 | tf_op jit(solution)/shard_map/ppermute | solution.py:665
  17.2 3.5 %copy-start.6 = (bf16[384,1152]{1,0:T(8,128)(2,1)S(1)}, bf16[384,1152]{1,0:T(8,128)(2,1)}, u32[]{:S(2)}) copy-start(bf16[384,1152]{1,0:T(8,128)(2,1)} %wqkv_ref.1) | copy-start | bytes 2654212
  21.7 3.0 %copy-start.10 = (f32[5]{0:T(128)S(1)}, f32[5]{0:T(128)}, u32[]{:S(2)}) copy-start(f32[5]{0:T(128)} %param.25) | copy-start | bytes 64
  25.4 42.4 %collective-permute-start.5 = (bf16[1,3,144,160]{3,2,1,0:T(8,128)(2,1)}, bf16[1,3,144,160]{3,2,1,0:T(8,128)(2,1)}, u32[]{:S(2)}, u32[]{:S(2)}) collective-permute-start(bf16[1,3,144,160]{3,2,1,0:T(8,128)(2,1)} %get-tuple-element.105), channel_id=1, source_target_pairs={{33,0},{34,1},{35,2},{36,3},{37,4},{38,5},{39,6},{40,7},{41,8},{42... | collective-permute-start | bytes 414728 | tf_op jit(solution)/shard_map/ppermute | solution.py:665
  28.7 3.0 %copy-start.8 = (f32[6,5,4]{2,1,0:T(8,128)S(1)}, f32[6,5,4]{2,1,0:T(8,128)}, u32[]{:S(2)}) copy-start(f32[6,5,4]{2,1,0:T(8,128)} %broadcast_multiply_fusion) | copy-start | bytes 1444
  28.7 7.1 %copy-start.9 = (f32[384]{0:T(512)S(1)}, f32[384]{0:T(512)}, u32[]{:S(2)}) copy-start(f32[384]{0:T(512)} %param.18) | copy-start | bytes 4612
  28.7 11.1 %copy-start.1 = (bf16[2,6,144,384]{3,2,1,0:T(8,128)(2,1)S(1)}, bf16[2,6,144,384]{3,2,1,0:T(8,128)(2,1)}, u32[]{:S(2)}) copy-start(bf16[2,6,144,384]{3,2,1,0:T(8,128)(2,1)} %own_ref) | copy-start | bytes 3981316
  40.4 1.0 copy-start
  69.1 0.9 copy-start.2
  103.1 47.1 %all-to-all-start = ((bf16[128,88,128]{2,1,0:T(8,128)(2,1)}), bf16[128,88,128]{2,1,0:T(8,128)(2,1)S(1)}, u32[]{:S(2)}, u32[]{:S(2)}) async-start(bf16[128,88,128]{2,1,0:T(8,128)(2,1)} %bitcast.26), calls=%async_computation | async-start | bytes 5767168 | tf_op jit(solution)/shard_map/all_to_all | solution.py:743
  150.2 24.2 %all-to-all-start.1 = ((bf16[128,32,128]{2,1,0:T(8,128)(2,1)}), bf16[128,32,128]{2,1,0:T(8,128)(2,1)}, u32[]{:S(2)}, u32[]{:S(2)}) async-start(bf16[128,32,128]{2,1,0:T(8,128)(2,1)} %bitcast.27), calls=%async_computation.1 | async-start | bytes 2097152 | tf_op jit(solution)/shard_map/all_to_all | solution.py:748
  159.8 14.7 %copy-start.4 = (f32[8,1536]{1,0:T(8,128)S(1)}, f32[8,1536]{1,0:T(8,128)}, u32[]{:S(2)}) copy-start(f32[8,1536]{1,0:T(8,128)} %get-tuple-element.60.wup_ref) | copy-start | bytes 147460
  159.8 14.7 %copy-start.5 = (f32[8,1152]{1,0:T(8,128)S(1)}, f32[8,1152]{1,0:T(8,128)}, u32[]{:S(2)}) copy-start(f32[8,1152]{1,0:T(8,128)} %get-tuple-element.61.wqkv_ref) | copy-start | bytes 110596

commit v3 on v2

--- a/solution.py
+++ b/solution.py
@@ -13,6 +13,7 @@
 GROUP = 6
 DEVS = 128
 WIDE = 256
+SLOTS = 2
 TOGETHER = 3
 norm_eps = 1e-05
 loss_scale = 32768.0
@@ -122,13 +123,11 @@
     table_ref,
     gain_ref,
     wt_ref,
-    wv_ref,
-    wk_ref,
+    wqkv_ref,
     wproj_ref,
     bias_ref,
     stream2_ref,
-    qkt_ref,
-    v_ref,
+    qt_ref,
     prob_ref,
     att_ref,
 ):
@@ -137,21 +136,19 @@
     normed = (hat * gain_ref[...]).astype(bf16)
     d = normed.shape[1]
     count, win = att_ref.shape[0], att_ref.shape[2]
-    k_tok = nn(normed, wk_ref[...]).astype(bf16)
-    v_tok = nn(normed, wv_ref[...]).astype(bf16)
+    k_tok = nn(normed, wqkv_ref[:, d : 2 * d]).astype(bf16)
     e = d // HEADS
     per = 128 // e
-    qkvts = []
+    qvts = []
     for u in range(count):
         rows = slice(u * win, (u + 1) * win)
         filled = jnp.concatenate([normed[rows], jnp.zeros((WIDE - win, d), bf16)], 0)
-        qkvts.append(nt(wt_ref[...], filled))
+        qvts.append((nt(wt_ref[:d], filled), nt(wt_ref[2 * d :], filled)))
     mixed = []
     for u in range(count):
         rows = slice(u * win, (u + 1) * win)
-        qt = (qkvts[u][:d] * (log2_e * e**-0.5)).astype(bf16)
-        kt = qkvts[u][d : 2 * d].astype(bf16)
-        vt = qkvts[u][2 * d :].astype(bf16)
+        qt = (qvts[u][0] * (log2_e * e**-0.5)).astype(bf16)
+        vt = qvts[u][1].astype(bf16)
         att = []
         for g in range(d // 128):
             k_four = k_tok[rows, g * 128 : (g + 1) * 128]
@@ -168,10 +165,8 @@
             att += [nn(vt[h * e : (h + 1) * e, :win], prob) for h, prob in zip(heads, probs)]
         att = jnp.concatenate(att, 0).astype(bf16)[:, :win]
         att_ref[u] = att
-        qkt_ref[u, :d] = qt
-        qkt_ref[u, d:] = kt
+        qt_ref[u] = qt
         mixed.append(tn(att, wproj_ref[...]).astype(bf16))
-    v_ref[...] = v_tok
     stream2_ref[...] = stream + jnp.concatenate(mixed, 0).astype(f32)
 
 
@@ -241,7 +236,7 @@
         hids.append(hidden.astype(bf16))
         slopes.append(slope.astype(bf16))
     field = (stream2 + nn(jnp.concatenate(hids, 1), wdown_ref[...])).astype(bf16)
-    pred = nn(field, wout_ref[...])
+    pred = nt(field, wout_ref[...])
     relief = relief_ref[...]
     lev = jnp.concatenate([lev_ref[...]] * wins, 0)
     base = jnp.concatenate([wide_ref[...]] * wins, 0)
@@ -253,7 +248,7 @@
     gpred = (scale_ref[0] * cell_w * differ * inv_err).astype(bf16)
     out = gpred.shape[1]
     gout_ref[:, :out] += nn(field.T, gpred)
-    gfield = nt(gpred, wout_ref[...])
+    gfield = nn(gpred, wout_ref[...])
     gfb = gfield.astype(bf16)
     gfbt = gfb.T
     normed2t = normed2.T
@@ -293,9 +288,9 @@
     table_ref,
     gain_ref,
     wqkv_ref,
+    wt_ref,
     wproj_ref,
-    qkt_ref,
-    v_ref,
+    qt_ref,
     prob_ref,
     att_ref,
     gs2_ref,
@@ -332,14 +327,18 @@
     for u in range(count):
         filled = jnp.concatenate([gmix[u * win : (u + 1) * win], pad], 0)
         gatts.append(nt(wproj_ref[...], filled).astype(bf16))
-    v_tok = v_ref[...]
+    v_tok = nn(normed, wqkv_ref[:, 2 * d :]).astype(bf16)
+    kts = []
+    for u in range(count):
+        filled = jnp.concatenate([normed[u * win : (u + 1) * win], pad], 0)
+        kts.append(nt(wt_ref[d : 2 * d], filled).astype(bf16)[:, :win])
     gshift = []
     for u in range(count):
         wrows = slice(u * win, (u + 1) * win)
         gatt_b = gatts[u]
         prod = gatt_b[:, :win].astype(f32) * att_ref[u].astype(f32)
         prod = jnp.concatenate([prod, jnp.zeros((d, WIDE - win), f32)], 1)
-        qt, kt = qkt_ref[u, :d], qkt_ref[u, d:, :win]
+        qt, kt = qt_ref[u], kts[u]
         gqs, gks, gvs = [], [], []
         for g in range(d // 128):
             v_four = v_tok[wrows, g * 128 : (g + 1) * 128]
@@ -441,8 +440,13 @@
     for i in range(rows):
         grel_ref[i : i + 1, :] = last[:, i * classes : (i + 1) * classes]
     loss_ref[...] = (last[:, 126:127] + last[:, 127:128]) / weight_sum_ref[0]
-    ga_ref[...] = jnp.sum(wqkv_ref[:rows] * gqkv_ref[...], 1, keepdims=True) / gatt_ref[...]
-    gm_ref[...] = jnp.sum(wup_ref[:rows] * gup_ref[...], 1, keepdims=True) / gmlp_ref[...]
+    diag = lax.broadcasted_iota(jnp.int32, (rows, rows), 0) == lax.broadcasted_iota(
+        jnp.int32, (rows, rows), 1
+    )
+    ga = jnp.sum(wqkv_ref[:rows] * gqkv_ref[...], 1, keepdims=True)
+    ga_ref[...] = jnp.sum(jnp.where(diag, ga, 0.0), 0, keepdims=True) / gatt_ref[...]
+    gm = jnp.sum(wup_ref[:rows] * gup_ref[...], 1, keepdims=True)
+    gm_ref[...] = jnp.sum(jnp.where(diag, gm, 0.0), 0, keepdims=True) / gmlp_ref[...]
 
 
 def finish(weight_sum, got_t, got_q, w_up, w_qkv, gain_mlp, gain_attn, shapes):
@@ -486,22 +490,19 @@
             whole(table.shape),
             whole((1, d)),
             whole((3 * d, d)),
-            whole((d, d)),
-            whole((d, d)),
+            whole((d, 3 * d)),
             whole((d, d)),
             whole(bias_t.shape),
         ],
         out_specs=[
             lead((TOGETHER * win, d)),
-            lead((TOGETHER, 2 * d, WIDE)),
-            lead((TOGETHER * win, d)),
+            lead((TOGETHER, d, WIDE)),
             lead((TOGETHER, HEADS, win, WIDE)),
             lead((TOGETHER, d, win)),
         ],
         out_shape=[
             sds((t, d), f32),
-            sds((count, 2 * d, WIDE), bf16),
-            sds((t, d), bf16),
+            sds((count, d, WIDE), bf16),
             sds((count, HEADS, win, WIDE), bf16),
             sds((count, d, win), bf16),
         ],
@@ -513,8 +514,7 @@
         table,
         gain[None],
         wt,
-        w_qkv[:, 2 * d :],
-        w_qkv[:, d : 2 * d],
+        w_qkv,
         w_proj,
         bias_t,
     )
@@ -547,7 +547,7 @@
             whole((1, d)),
             whole((d, ff)),
             whole((ff, d)),
-            whole((d, out)),
+            whole((out, d)),
         ],
         out_specs=[
             whole((1, out)),
@@ -574,10 +574,10 @@
         ],
         compiler_params=params_of(),
         name="tail_both",
-    )(me, scale, stream2, targ, relief_col, lev, base, att, gain[None], w_up, w_down, w_out)
-
-
-def attention_back(me, num, x, relief_col, table, gain, w_qkv, w_proj, qkt, v_tok, probs, att, gs2):
+    )(me, scale, stream2, targ, relief_col, lev, base, att, gain[None], w_up, w_down, w_out.T)
+
+
+def attention_back(me, num, x, relief_col, table, gain, w_qkv, wt, w_proj, qt, probs, att, gs2):
     t, d = x.shape
     count, win = att.shape[0], att.shape[2]
     sds = jax.ShapeDtypeStruct
@@ -591,9 +591,9 @@
             whole(table.shape),
             whole((1, d)),
             whole((d, 3 * d)),
+            whole((3 * d, d)),
             whole((d, d)),
-            lead((TOGETHER, 2 * d, WIDE)),
-            lead((TOGETHER * win, d)),
+            lead((TOGETHER, d, WIDE)),
             lead((TOGETHER, HEADS, win, WIDE)),
             lead((TOGETHER, d, win)),
             lead((TOGETHER * win, d)),
@@ -619,7 +619,7 @@
         compiler_params=params_of(),
         cost_estimate=cost(10 * 2**30, 20 * 2**20, 0),
         name="attention_back",
-    )(me, x, relief_col, table, gain[None], w_qkv, w_proj, qkt, v_tok, probs, att, gs2, num)
+    )(me, x, relief_col, table, gain[None], w_qkv, wt, w_proj, qt, probs, att, gs2, num)
 
 
 def lat_weights(row_ids, lat_rows):
@@ -635,23 +635,6 @@
     lat_weight = jnp.sum(lat_weights(jnp.arange(lat_rows, dtype=jnp.int32), lat_rows), 1)
     live_levels = (2 * level_count - relief).astype(f32)
     return jnp.sum(var_weight) * 4.0 * jnp.sum(lat_weight[:, None] * live_levels)
-
-
-def window_mask(last_level, last_band, slots_n, rows_n, win_lon):
-    slot_label = jnp.where(last_level & (jnp.arange(slots_n) >= slots_n // 2), 2, 0)
-    row_label = jnp.where(last_band & (jnp.arange(rows_n) >= rows_n // 2), 1, 0)
-    labels = (
-        slot_label[:, None, None] + row_label[None, :, None] + jnp.zeros((1, 1, win_lon), jnp.int32)
-    )
-    labels = labels.reshape(-1)
-    return labels[:, None] == labels[None, :]
-
-
-def windows(field_in):
-    slots_n, rows_n, lon_n, chans = field_in.shape
-    count_w = lon_n // WIN_LON
-    parted = field_in.reshape(slots_n, rows_n, count_w, WIN_LON, chans).transpose(2, 0, 1, 3, 4)
-    return parted.reshape(count_w * slots_n * rows_n * WIN_LON, chans)
 
 
 def from_next(value, axes):
@@ -674,33 +657,92 @@
     return up, side, both
 
 
-def local_inputs(tokens_shape, relief, earth_bias, var_weight):
-    slots_dev, rows_dev, lon_cells, _ = tokens_shape
+def summed_by_chips(send):
+    lvls, lats = lax.axis_size("lvl"), lax.axis_size("lat")
+    odd = lax.axis_index("lvl") % 2
+    halves = send.reshape(lvls // 2, 2, lats, *send.shape[1:])
+    keep = lax.dynamic_index_in_dim(halves, odd, 1, False)
+    give = lax.dynamic_index_in_dim(halves, 1 - odd, 1, False)
+    got = lax.ppermute(give, "lvl", [(i, i ^ 1) for i in range(lvls)])
+    pair = (keep.astype(f32) + got.astype(f32)).astype(bf16)
+    groups = [
+        [lvl * lats + lat for lvl in range(c, lvls, 2) for lat in range(lats)] for c in range(2)
+    ]
+    return lax.all_to_all(
+        pair.reshape(-1, *send.shape[1:]), ("lvl", "lat"), 0, 0, axis_index_groups=groups, tiled=True
+    )
+
+
+def prepare_kernel(me_ref, bias_ref, relief_ref, wqkv_ref, bias_t_ref, col_ref, wt_ref, lane_ref, *, lvls, lats):
+    me = me_ref[0]
+    heads, win, _ = bias_ref.shape
+    slots, rows, lon = SLOTS, win // (SLOTS * WIN_LON), relief_ref.shape[0]
+    shape = (win, win)
+    key, query = (lax.broadcasted_iota(jnp.int32, shape, dim) for dim in (0, 1))
+    block = rows * WIN_LON
+    split_slots = (key >= win // 2) != (query >= win // 2)
+    half = rows // 2 * WIN_LON
+    split_rows = (key % block >= half) != (query % block >= half)
+    low = jnp.where(me // lats == lvls - 1, masked_score, 0.0)
+    band = jnp.where(me % lats == lats - 1, masked_score, 0.0)
+    hidden = jnp.where(split_slots, low, 0.0) + jnp.where(split_rows, band, 0.0)
+    blank = jnp.zeros((win, WIDE - win), f32)
+    for h in range(heads):
+        bias_t_ref[h] = jnp.concatenate([bias_ref[h].T * log2_e + hidden, blank], 1)
+    grid = relief_ref[...].astype(f32)
+    lane = lax.broadcasted_iota(jnp.int32, grid.shape, 1)
+    first = (me % lats) * rows + rows // 2
+    for r in range(rows):
+        row = (first + r) % (rows * lats)
+        col = jnp.sum(jnp.where(lane == row, grid, 0.0), 1, keepdims=True)
+        col = jnp.concatenate([col[WIN_LON // 2 :], col[: WIN_LON // 2]], 0)
+        for w in range(lon // WIN_LON):
+            for s in range(slots):
+                at = w * win + (s * rows + r) * WIN_LON
+                lane_ref[at : at + WIN_LON] = col[w * WIN_LON : (w + 1) * WIN_LON]
+    col_ref[...] = lane_ref[...].astype(jnp.int32)
+    wt_ref[...] = wqkv_ref[...].T
+
+
+def prepare(me, earth_bias, relief, w_qkv, lvls, lats):
+    heads, win, _ = earth_bias.shape
+    rows = win // (SLOTS * WIN_LON)
+    tokens = SLOTS * rows * relief.shape[1]
+    sds = jax.ShapeDtypeStruct
+    vmem = pl.BlockSpec(memory_space=pltpu.VMEM)
+    return pl.pallas_call(
+        functools.partial(prepare_kernel, lvls=lvls, lats=lats),
+        in_specs=[pl.BlockSpec(memory_space=pltpu.SMEM)] + [vmem] * 3,
+        out_specs=[vmem] * 3,
+        out_shape=[
+            sds((heads, win, WIDE), f32),
+            sds((tokens, 1), jnp.int32),
+            sds(w_qkv.shape[::-1], bf16),
+        ],
+        scratch_shapes=[pltpu.VMEM((tokens, 1), f32)],
+        compiler_params=pltpu.CompilerParams(vmem_limit_bytes=40 * 2**20),
+        name="prepare_inputs",
+    )(me, earth_bias, relief.T, w_qkv)
+
+
+def local_inputs(tokens_shape, var_weight):
+    slots_dev, rows_dev, _, _ = tokens_shape
     lvl_count, lat_count = lax.axis_size("lvl"), lax.axis_size("lat")
     lvl_id, lat_id = lax.axis_index("lvl"), lax.axis_index("lat")
     level_total, lat_rows = slots_dev * lvl_count, rows_dev * lat_count
-    allowed = window_mask(
-        lvl_id == lvl_count - 1, lat_id == lat_count - 1, slots_dev, rows_dev, WIN_LON
-    )
     level_ids = (
         lvl_id * slots_dev + jnp.arange(slots_dev, dtype=jnp.int32) + slots_dev // 2
     ) % level_total
     row_ids = (
         lat_id * rows_dev + jnp.arange(rows_dev, dtype=jnp.int32) + rows_dev // 2
     ) % lat_rows
-    relief_blk = jnp.roll(jnp.take(relief, row_ids, axis=0), -(WIN_LON // 2), 1)
-    relief_col = windows(
-        jnp.broadcast_to(relief_blk[None, :, :, None], (slots_dev, rows_dev, lon_cells, 1))
-    )
     vars_n = var_weight.shape[0]
     base = jnp.broadcast_to(
         var_weight[None, :, None, None, None]
         * lat_weights(row_ids, lat_rows)[:, None, None, :, None],
         (rows_dev, vars_n, 2, 4, 4),
     ).reshape(rows_dev, vars_n * 32)
-    bias_t = jnp.where(allowed, earth_bias.transpose(0, 2, 1) * log2_e, masked_score)
-    bias_t = jnp.pad(bias_t, ((0, 0), (0, 0), (0, WIDE - bias_t.shape[2])))
-    return relief_col, level_ids, base, bias_t
+    return level_ids, base
 
 
 def body(
@@ -723,34 +765,36 @@
     level_total = tokens.shape[0] * lax.axis_size("lvl")
     weight_sum = weight_total(relief, var_weight, level_total)
     token_halo = halo_of(tokens)
+    me = lax.axis_index(axes)
+    bias_t, relief_col, wt = prepare(
+        me.reshape(1), earth_bias[0, 0], relief, w_qkv, lax.axis_size("lvl"), lax.axis_size("lat")
+    )
+    lev, base = local_inputs(tokens.shape, var_weight)
+    scale = (loss_scale / weight_sum).reshape(1)
+    tokens, targets, relief_col, bias_t, base, lev, scale, wt = lax.optimization_barrier(
+        (tokens, targets, relief_col, bias_t, base, lev, scale, wt)
+    )
     targ_halo = halo_of(targets)
-    relief_col, lev, base, bias_t = local_inputs(tokens.shape, relief, earth_bias[0, 0], var_weight)
-    scale = (loss_scale / weight_sum).reshape(1)
-    wt = w_qkv.T
-    tokens, relief_col, bias_t, base, scale, wt = lax.optimization_barrier(
-        (tokens, relief_col, bias_t, base, scale, wt)
-    )
     x = assemble(tokens, *token_halo)
-    stream2, qkt, v_tok, probs, att = attention_forward(
+    stream2, qt, probs, att = attention_forward(
         x, relief_col, relief_table, gain_attn, w_qkv, wt, w_proj, bias_t
     )
     stream2, targets = lax.optimization_barrier((stream2, targets))
     targ = assemble(targets, *targ_halo)
-    me = lax.axis_index(axes)
     num, gs2, send_t, up_rows = tail_both(
         me.reshape(1), scale, stream2, targ, relief_col, lev, base, att, gain_mlp, w_up, w_down, w_out, GROUP
     )
     got_t = lax.all_to_all(send_t.reshape(devs, -1, 128), axes, 0, 0, tiled=True)
     gbias_t, send_q, qkv_rows = attention_back(
-        me.reshape(1), num, x, relief_col, relief_table, gain_attn, w_qkv, w_proj, qkt, v_tok, probs, att, gs2
+        me.reshape(1), num, x, relief_col, relief_table, gain_attn, w_qkv, wt, w_proj, qt, probs, att, gs2
     )
     send_q, got_t = lax.optimization_barrier((send_q.reshape(devs, -1, 128), got_t))
-    got_q = lax.all_to_all(send_q, axes, 0, 0, tiled=True)
+    got_q = summed_by_chips(send_q)
     d = tokens.shape[-1]
     share = d // devs
 
     def mine(array):
-        return lax.dynamic_slice_in_dim(array, me * share, share, 0)[:, None]
+        return lax.dynamic_slice_in_dim(array, me * share, share, 0)[None]
 
     shapes = (
         (1, 1),
@@ -759,8 +803,8 @@
         (share, w_up.shape[1]),
         (w_down.shape[0] // devs, d),
         (share, w_out.shape[1]),
-        (share, 1),
-        (share, 1),
+        (1, share),
+        (1, share),
         (share, relief_table.shape[0]),
     )
     sums = finish(
@@ -769,8 +813,8 @@
     return (
         sums[0][0, 0],
         *sums[1:6],
-        sums[6][:, 0],
-        sums[7][:, 0],
+        sums[6][0],
+        sums[7][0],
         sums[8],
         gbias_t[..., : gbias_t.shape[1]].transpose(0, 2, 1)[None, None],
     )

time: 180 us -> 163 us (0.906)
  local copies, waits for them, and re-layouts: 28.1 us -> 17.6 us
  waiting for transfers between devices: 18.6 us -> 14.1 us
  other arithmetic: 7.2 us -> 4.05 us
  starting transfers between devices: 26.7 us -> 28.8 us
    all_to_all x1, waiting for transfers between devices: 11.7 us -> 7.35 us  [summed_by_chips(): lax.all_to_all(pair.reshape(-1, *send.shape[1:]), ('lvl', 'lat'), 0, 0, a...]
    all_to_all x1, waiting for transfers between devices: 6.83 us -> 3.42 us  [body(): lax.all_to_all(send_t.reshape(devs, -1, 128), axes, 0, 0, tiled=True)]
    pallas_call x1, Pallas kernels: 31.7 us -> 35.1 us  [attention_back(): pl.pallas_call(back_kernel, grid=(count // TOGETHER,), in_specs=[pl.Block...]
    select_n x5 -> x0, other arithmetic: 3.05 us -> none  [the longest x1 2.95 us: local_inputs(): jnp.where(allowed, earth_bias.transpose(0, 2, 1) * log2_e, masked_score)]
    pad x1 -> x0, local copies, waits for them, and re-layouts: 2.96 us -> none  [local_inputs(): bias_t = jnp.pad(bias_t, ((0, 0), (0, 0), (0, WIDE - bias_t.shape[2])))]
    unnamed x27 -> x31, local copies, waits for them, and re-layouts: 11.2 us -> 8.61 us
    ppermute x0 -> x1, waiting for transfers between devices: none -> 2.12 us  [summed_by_chips(): got = lax.ppermute(give, 'lvl', [(i, i ^ 1) for i in range(lvls)])]
    convert_element_type x0 -> x1, other arithmetic: none -> 1.97 us  [summed_by_chips(): pair = (keep.astype(f32) + got.astype(f32)).astype(bf16)]
  transfers between devices with their start and end apart: 8 -> 9, of which waited for: 2 -> 4; matrix products, arithmetic and copies ran while one was open for 17% -> 6% of each run, Pallas kernels for 33% -> 38%
where the time goes in v3:
time: 163 us
  Pallas kernels  96.2 us (59%)
  starting transfers between devices  28.8 us (18%)
  local copies, waits for them, and re-layouts  17.6 us (11%)
  waiting for transfers between devices  14.1 us (9%)
  other arithmetic  4.05 us (2%)
  between operations  2.19 us (1%)
    pallas_call x1, Pallas kernels, attention_back(): pl.pallas_call(back_kernel, grid=(count // TOGETHER,), in_specs=[pl.Block...  35.1 us
    pallas_call x1, Pallas kernels, tail_both(): pl.pallas_call(functools.partial(tail_kernel, block_f=256), grid=(t // m,...  33.1 us
    pallas_call x1, Pallas kernels, attention_forward(): pl.pallas_call(att_kernel, grid=(count // TOGETHER,), in_specs=[lead((TOG...  24.8 us
    ppermute x6, starting transfers between devices, from_next(): return lax.ppermute(value, ('lvl', 'lat'), pairs)  12.4 us
    all_to_all x1, starting transfers between devices, body(): lax.all_to_all(send_t.reshape(devs, -1, 128), axes, 0, 0, tiled=True)  9.71 us
    unnamed x31, local copies, waits for them, and re-layouts  8.61 us
    all_to_all x1, waiting for transfers between devices, summed_by_chips(): lax.all_to_all(pair.reshape(-1, *send.shape[1:]), ('lvl', 'lat'), 0, 0, a...  7.35 us
    all_to_all x1, starting transfers between devices, summed_by_chips(): lax.all_to_all(pair.reshape(-1, *send.shape[1:]), ('lvl', 'lat'), 0, 0, a...  6.71 us
  transfers between devices with their start and end apart: 9, of which 4 were waited for; matrix products, arithmetic and copies ran while one was open for 6% of the time, Pallas kernels for 38%

profile of v3, /device:TPU:0, one launch (start us, length us, event | category | flops | bytes accessed | tf_op | source)
XLA Modules:
  0.0 163.0 jit_solution(12214079677999237789)
XLA Ops:
  0.7 2.2 %fusion.3 = (bf16[1,3,144,384]{3,2,1,0:T(8,128)(2,1)S(1)}, bf16[1,3,144,384]{3,2,1,0:T(8,128)(2,1)}, bf16[1,3,144,384]{3,2,1,0:T(8,128)(2,1)}) fusion(bf16[2,6,144,384]{3,2,1,0:T(8,128)(2,1)} %own_ref), kind=kLoop, calls=%fused_computation.17 | loop fusion | bytes 1990656 | tf_op jit(solution)/shard_map/slice | solution.py:656
  2.9 2.7 %collective-permute-start = (bf16[1,3,144,384]{3,2,1,0:T(8,128)(2,1)}, bf16[1,3,144,384]{3,2,1,0:T(8,128)(2,1)S(1)}, u32[]{:S(2)}, u32[]{:S(2)}) collective-permute-start(bf16[1,3,144,384]{3,2,1,0:T(8,128)(2,1)} %get-tuple-element.111), channel_id=1, source_target_pairs={{32,0},{33,1},{34,2},{35,3},{36,4},{37,5},{38,6},{39,7},{40,8},{41... | collective-permute-start | bytes 995336 | tf_op jit(solution)/shard_map/ppermute | solution.py:648
  5.6 6.3 %collective-permute-start.1 = (bf16[1,3,144,384]{3,2,1,0:T(8,128)(2,1)}, bf16[1,3,144,384]{3,2,1,0:T(8,128)(2,1)S(1)}, u32[]{:S(2)}, u32[]{:S(2)}) collective-permute-start(bf16[1,3,144,384]{3,2,1,0:T(8,128)(2,1)} %get-tuple-element.112), channel_id=1, source_target_pairs={{1,0},{2,1},{3,2},{4,3},{5,4},{6,5},{7,6},{8,7},{9,8},{10,9},{11,1... | collective-permute-start | bytes 995336 | tf_op jit(solution)/shard_map/ppermute | solution.py:648
  16.0 1.5 copy-done.7
  17.5 1.2 prepare_inputs.1
  18.6 1.2 copy-done.6
  19.8 0.9 copy-done.8
  21.4 1.4 collective-permute-start.3
  22.8 1.6 collective-permute-start.4
  25.6 1.2 collective-permute-done.2.both_ref
  27.2 1.1 copy-done
  28.3 24.8 %attention_forward.1 = (f32[1728,384]{1,0:T(8,128)}, bf16[12,384,256]{2,1,0:T(8,128)(2,1)}, bf16[12,12,144,256]{3,2,1,0:T(8,128)(2,1)}, bf16[12,384,144]{2,1,0:T(8,128)(2,1)}) custom-call(bf16[1728,384]{1,0:T(8,128)(2,1)} %copy-done, s32[1728,1]{1,0:T(8,128)} %copy-done.4, bf16[4,384]{1,0:T(4,128)(2,1)} %table_ref.3, f32[1,384]{1,0:T(1,128)} %broadcast_in_dim.13.gain_ref, ...), custom_call_target="tpu_custom_call" | custom-call | tf_op jit(solution)/shard_map/attention_forward/pallas_call | solution.py:484
  54.4 33.1 %tail_both.1 = (f32[1,160]{1,0:T(1,128)}, f32[1728,384]{1,0:T(8,128)}, bf16[11264,128]{1,0:T(8,128)(2,1)}, f32[8,1536]{1,0:T(8,128)}) custom-call(s32[1]{0:T(128)} %bitcast.1.me_ref, f32[1]{0:T(128)} %bitcast.4.scale_ref, f32[1728,384]{1,0:T(8,128)} %get-tuple-element.58.stream2_ref, bf16[1728,160]{1,0:T(8,128)(2,1)} %copy-done.3, s32[1728,1]{1,0:T(8,128)} %copy-done.4, ...), custom_call_target="tpu_custom_call" | custom-call | tf_op jit(solution)/shard_map/tail_both/pallas_call | solution.py:535
  87.5 9.7 %all-to-all-start = ((bf16[128,88,128]{2,1,0:T(8,128)(2,1)}), bf16[128,88,128]{2,1,0:T(8,128)(2,1)S(1)}, u32[]{:S(2)}, u32[]{:S(2)}) async-start(bf16[128,88,128]{2,1,0:T(8,128)(2,1)} %bitcast.28), calls=%async_computation | async-start | bytes 5767168 | tf_op jit(solution)/shard_map/all_to_all | solution.py:787
  97.2 35.1 %attention_back.1 = (f32[12,144,256]{2,1,0:T(8,128)}, bf16[4096,128]{1,0:T(8,128)(2,1)}, f32[8,1152]{1,0:T(8,128)}) custom-call(s32[1]{0:T(128)} %bitcast.1.me_ref, bf16[1728,384]{1,0:T(8,128)(2,1)} %copy-done, s32[1728,1]{1,0:T(8,128)} %copy-done.4, bf16[4,384]{1,0:T(4,128)(2,1)} %table_ref.3, f32[1,384]{1,0:T(1,128)} %broadcast_in_dim.13.gain_ref, ...), custom_call_target="tpu_custom_call" | custom-call | flops 10737418240 | bytes 20971520 | tf_op jit(solution)/shard_map/attention_back/pallas_call | solution.py:584
  132.3 3.4 %all-to-all-done.gott_ref = bf16[128,88,128]{2,1,0:T(8,128)(2,1)S(1)} async-done(((bf16[128,88,128]{2,1,0:T(8,128)(2,1)}), bf16[128,88,128]{2,1,0:T(8,128)(2,1)S(1)}, u32[]{:S(2)}, u32[]{:S(2)}) %all-to-all-start) | async-done | bytes 2883616 | tf_op jit(solution)/shard_map/all_to_all | solution.py:787
  135.8 1.9 %dynamic-slice_bitcast_fusion = bf16[2,32,32,128]{3,2,1,0:T(8,128)(2,1)} fusion(bf16[2,2,32,32,128]{4,3,2,1,0:T(8,128)(2,1)} %bitcast.30, s32[]{:T(128)S(6)} %select_n.38), kind=kLoop, calls=%fused_computation.3 | loop fusion | bytes 1048580 | tf_op jit(solution)/shard_map/jit(dynamic_index_in_dim)/squeeze | solution.py:665
  137.6 2.1 %collective-permute-done.6 = bf16[2,32,32,128]{3,2,1,0:T(8,128)(2,1)S(1)} collective-permute-done((bf16[2,32,32,128]{3,2,1,0:T(8,128)(2,1)}, bf16[2,32,32,128]{3,2,1,0:T(8,128)(2,1)S(1)}, u32[]{:S(2)}, u32[]{:S(2)}) %collective-permute-start.6) | collective-permute-done | bytes 524320 | tf_op jit(solution)/shard_map/ppermute | solution.py:666
  139.8 2.0 %fusion = bf16[2,32,32,128]{3,2,1,0:T(8,128)(2,1)} fusion(bf16[2,32,32,128]{3,2,1,0:T(8,128)(2,1)S(1)} %collective-permute-done.6, bf16[2,2,32,32,128]{4,3,2,1,0:T(8,128)(2,1)} %bitcast.31, s32[]{:T(128)S(6)} %select_n.37), kind=kLoop, calls=%fused_computation.2 | loop fusion | flops 1048576 | bytes 1572868 | tf_op jit(solution)/shard_map/convert_element_type | solution.py:667
  141.7 6.7 %all-to-all-start.1 = ((bf16[64,32,128]{2,1,0:T(8,128)(2,1)}), bf16[64,32,128]{2,1,0:T(8,128)(2,1)S(1)}, u32[]{:S(2)}, u32[]{:S(2)}) async-start(bf16[64,32,128]{2,1,0:T(8,128)(2,1)} %bitcast.29), calls=%async_computation.1 | async-start | bytes 1048576 | tf_op jit(solution)/shard_map/all_to_all | solution.py:671
  148.5 2.8 %slice_bitcast_fusion = f32[1,1,12,144,144]{3,4,2,1,0:T(8,128)} fusion(f32[12,144,256]{2,1,0:T(8,128)} %get-tuple-element.79), kind=kLoop, calls=%fused_computation | loop fusion | bytes 1990656 | tf_op jit(solution)/shard_map/broadcast_in_dim | solution.py:819
  151.4 3.0 %copy.25 = f32[1,1,12,144,144]{4,3,2,1,0:T(8,128)} copy(f32[1,1,12,144,144]{3,4,2,1,0:T(8,128)} %slice_bitcast_fusion) | data formatting | bytes 1990656
  154.3 7.3 %all-to-all-done.1.gotq_ref = bf16[64,32,128]{2,1,0:T(8,128)(2,1)S(1)} async-done(((bf16[64,32,128]{2,1,0:T(8,128)(2,1)}), bf16[64,32,128]{2,1,0:T(8,128)(2,1)S(1)}, u32[]{:S(2)}, u32[]{:S(2)}) %all-to-all-start.1) | async-done | bytes 524320 | tf_op jit(solution)/shard_map/all_to_all | solution.py:671
  161.7 1.3 finish_sums.1
  (50 shorter events, 6.2 us)
Async XLA Ops:
  0.6 11.8 %copy-start.14 = (f32[5]{0:T(128)S(1)}, f32[5]{0:T(128)}, u32[]{:S(2)}) copy-start(f32[5]{0:T(128)} %param.25) | copy-start | bytes 64
  0.7 14.0 %copy-start.9 = (s32[192,144]{0,1:T(8,128)S(1)}, s32[192,144]{0,1:T(8,128)}, u32[]{:S(2)}) copy-start(s32[192,144]{0,1:T(8,128)} %param.15) | copy-start | bytes 331780
  0.7 15.3 %copy-start.2 = (bf16[384,1152]{1,0:T(8,128)(2,1)S(1)}, bf16[384,1152]{1,0:T(8,128)(2,1)}, u32[]{:S(2)}) copy-start(bf16[384,1152]{1,0:T(8,128)(2,1)} %wqkv_ref.5) | copy-start | bytes 2654212
  2.9 18.4 %copy-start.5 = (bf16[2,6,144,160]{3,2,1,0:T(8,128)(2,1)S(1)}, bf16[2,6,144,160]{3,2,1,0:T(8,128)(2,1)}, u32[]{:S(2)}) copy-start(bf16[2,6,144,160]{3,2,1,0:T(8,128)(2,1)} %own_ref.1) | copy-start | bytes 1658884
  2.9 21.5 %collective-permute-start = (bf16[1,3,144,384]{3,2,1,0:T(8,128)(2,1)}, bf16[1,3,144,384]{3,2,1,0:T(8,128)(2,1)S(1)}, u32[]{:S(2)}, u32[]{:S(2)}) collective-permute-start(bf16[1,3,144,384]{3,2,1,0:T(8,128)(2,1)} %get-tuple-element.111), channel_id=1, source_target_pairs={{32,0},{33,1},{34,2},{35,3},{36,4},{37,5},{38,6},{39,7},{40,8},{41... | collective-permute-start | bytes 995336 | tf_op jit(solution)/shard_map/ppermute | solution.py:648
  5.6 19.9 %collective-permute-start.1 = (bf16[1,3,144,384]{3,2,1,0:T(8,128)(2,1)}, bf16[1,3,144,384]{3,2,1,0:T(8,128)(2,1)S(1)}, u32[]{:S(2)}, u32[]{:S(2)}) collective-permute-start(bf16[1,3,144,384]{3,2,1,0:T(8,128)(2,1)} %get-tuple-element.112), channel_id=1, source_target_pairs={{1,0},{2,1},{3,2},{4,3},{5,4},{6,5},{7,6},{8,7},{9,8},{10,9},{11,1... | collective-permute-start | bytes 995336 | tf_op jit(solution)/shard_map/ppermute | solution.py:648
  12.0 14.8 %collective-permute-start.2 = (bf16[1,3,144,384]{3,2,1,0:T(8,128)(2,1)S(1)}, bf16[1,3,144,384]{3,2,1,0:T(8,128)(2,1)S(1)}, u32[]{:S(2)}, u32[]{:S(2)}) collective-permute-start(bf16[1,3,144,384]{3,2,1,0:T(8,128)(2,1)S(1)} %get-tuple-element.110), channel_id=1, source_target_pairs={{33,0},{34,1},{35,2},{36,3},{37,4},{38,5},{39,6},{40,7},{41,8},{42... | collective-permute-start | bytes 995336 | tf_op jit(solution)/shard_map/ppermute | solution.py:648
  16.0 1.5 copy-start.7
  17.5 6.9 %copy-start.12 = (f32[384]{0:T(512)S(1)}, f32[384]{0:T(512)}, u32[]{:S(2)}) copy-start(f32[384]{0:T(512)} %param.18) | copy-start | bytes 4612
  17.5 7.5 %copy-start.13 = (f32[384]{0:T(512)S(1)}, f32[384]{0:T(512)}, u32[]{:S(2)}) copy-start(f32[384]{0:T(512)} %param.19) | copy-start | bytes 4612
  17.5 9.3 %copy-start.1 = (bf16[2,6,144,384]{3,2,1,0:T(8,128)(2,1)S(1)}, bf16[2,6,144,384]{3,2,1,0:T(8,128)(2,1)}, u32[]{:S(2)}) copy-start(bf16[2,6,144,384]{3,2,1,0:T(8,128)(2,1)} %own_ref) | copy-start | bytes 3981316
  18.6 1.2 copy-start.6
  19.8 0.9 copy-start.8
  20.8 4.8 %copy-start.4 = (s32[1728,1]{1,0:T(8,128)}, s32[1728,1]{1,0:T(8,128)S(1)}, u32[]{:S(2)}) copy-start(s32[1728,1]{1,0:T(8,128)S(1)} %get-tuple-element.49.relief_ref) | copy-start | bytes 20740
  21.4 31.8 %collective-permute-start.3 = (bf16[1,3,144,160]{3,2,1,0:T(8,128)(2,1)S(1)}, bf16[1,3,144,160]{3,2,1,0:T(8,128)(2,1)S(1)}, u32[]{:S(2)}, u32[]{:S(2)}) collective-permute-start(bf16[1,3,144,160]{3,2,1,0:T(8,128)(2,1)S(1)} %get-tuple-element.115), channel_id=1, source_target_pairs={{32,0},{33,1},{34,2},{35,3},{36,4},{37,5},{38,6},{39,7},{40,8},{41... | collective-permute-start | bytes 414728 | tf_op jit(solution)/shard_map/ppermute | solution.py:648
  22.8 30.4 %collective-permute-start.4 = (bf16[1,3,144,160]{3,2,1,0:T(8,128)(2,1)S(1)}, bf16[1,3,144,160]{3,2,1,0:T(8,128)(2,1)S(1)}, u32[]{:S(2)}, u32[]{:S(2)}) collective-permute-start(bf16[1,3,144,160]{3,2,1,0:T(8,128)(2,1)S(1)} %get-tuple-element.114), channel_id=1, source_target_pairs={{1,0},{2,1},{3,2},{4,3},{5,4},{6,5},{7,6},{8,7},{9,8},{10,9},{11,1... | collective-permute-start | bytes 414728 | tf_op jit(solution)/shard_map/ppermute | solution.py:648
  24.4 28.8 %collective-permute-start.5 = (bf16[1,3,144,160]{3,2,1,0:T(8,128)(2,1)S(1)}, bf16[1,3,144,160]{3,2,1,0:T(8,128)(2,1)S(1)}, u32[]{:S(2)}, u32[]{:S(2)}) collective-permute-start(bf16[1,3,144,160]{3,2,1,0:T(8,128)(2,1)S(1)} %get-tuple-element.113), channel_id=1, source_target_pairs={{33,0},{34,1},{35,2},{36,3},{37,4},{38,5},{39,6},{40,7},{41,8},{42... | collective-permute-start | bytes 414728 | tf_op jit(solution)/shard_map/ppermute | solution.py:648
  27.2 1.1 copy-start
  53.5 0.9 copy-start.3
  87.5 48.3 %all-to-all-start = ((bf16[128,88,128]{2,1,0:T(8,128)(2,1)}), bf16[128,88,128]{2,1,0:T(8,128)(2,1)S(1)}, u32[]{:S(2)}, u32[]{:S(2)}) async-start(bf16[128,88,128]{2,1,0:T(8,128)(2,1)} %bitcast.28), calls=%async_computation | async-start | bytes 5767168 | tf_op jit(solution)/shard_map/all_to_all | solution.py:787
  137.6 2.1 %collective-permute-start.6 = (bf16[2,32,32,128]{3,2,1,0:T(8,128)(2,1)}, bf16[2,32,32,128]{3,2,1,0:T(8,128)(2,1)S(1)}, u32[]{:S(2)}, u32[]{:S(2)}) collective-permute-start(bf16[2,32,32,128]{3,2,1,0:T(8,128)(2,1)} %dynamic-slice_bitcast_fusion), channel_id=1, source_target_pairs={{0,32},{32,0},{64,96},{96,64},{1,33},{33,1},{65,97},{97,65},{2,34}... | collective-permute-start | bytes 1572872 | tf_op jit(solution)/shard_map/ppermute | solution.py:666
  141.7 20.0 %all-to-all-start.1 = ((bf16[64,32,128]{2,1,0:T(8,128)(2,1)}), bf16[64,32,128]{2,1,0:T(8,128)(2,1)S(1)}, u32[]{:S(2)}, u32[]{:S(2)}) async-start(bf16[64,32,128]{2,1,0:T(8,128)(2,1)} %bitcast.29), calls=%async_computation.1 | async-start | bytes 1048576 | tf_op jit(solution)/shard_map/all_to_all | solution.py:671
  151.4 10.3 %copy-start.10 = (f32[8,1536]{1,0:T(8,128)S(1)}, f32[8,1536]{1,0:T(8,128)}, u32[]{:S(2)}) copy-start(f32[8,1536]{1,0:T(8,128)} %get-tuple-element.68.wup_ref) | copy-start | bytes 147460
  151.4 10.3 %copy-start.11 = (f32[8,1152]{1,0:T(8,128)S(1)}, f32[8,1152]{1,0:T(8,128)}, u32[]{:S(2)}) copy-start(f32[8,1152]{1,0:T(8,128)} %get-tuple-element.69.wqkv_ref) | copy-start | bytes 110596

commit v4 on v3

--- a/solution.py
+++ b/solution.py
@@ -91,9 +91,9 @@
         send_ref[pl.ds(j, DEVS, stride=every), :] = jnp.zeros((DEVS, 128), f32)
 
 
-def cut_pieces(piece_ref, grad_ref):
-    for c in range(piece_ref.shape[0]):
-        piece_ref[c] = grad_ref[:, c * 128 : (c + 1) * 128]
+def add_pieces(piece_ref, at, grad):
+    for c in range(grad.shape[1] // 128):
+        piece_ref[at + c] += grad[:, c * 128 : (c + 1) * 128]
 
 
 def turn_pieces(piece_ref, grad_t_ref):
@@ -133,7 +133,7 @@
 ):
     stream, _ = stream_of(x_ref, relief_ref, table_ref)
     hat, _ = normalize(stream)
-    normed = (hat * gain_ref[...]).astype(bf16)
+    normed = (hat * gain_ref[:1]).astype(bf16)
     d = normed.shape[1]
     count, win = att_ref.shape[0], att_ref.shape[2]
     k_tok = nn(normed, wqkv_ref[:, d : 2 * d]).astype(bf16)
@@ -144,7 +144,7 @@
         rows = slice(u * win, (u + 1) * win)
         filled = jnp.concatenate([normed[rows], jnp.zeros((WIDE - win, d), bf16)], 0)
         qvts.append((nt(wt_ref[:d], filled), nt(wt_ref[2 * d :], filled)))
-    mixed = []
+    mixed, atts = [], []
     for u in range(count):
         rows = slice(u * win, (u + 1) * win)
         qt = (qvts[u][0] * (log2_e * e**-0.5)).astype(bf16)
@@ -166,17 +166,16 @@
         att = jnp.concatenate(att, 0).astype(bf16)[:, :win]
         att_ref[u] = att
         qt_ref[u] = qt
-        mixed.append(tn(att, wproj_ref[...]).astype(bf16))
-    stream2_ref[...] = stream + jnp.concatenate(mixed, 0).astype(f32)
+        atts.append(att.T)
+    stream2_ref[...] = stream + nn(jnp.concatenate(atts, 0), wproj_ref[...]).astype(bf16).astype(f32)
 
 
 def tail_kernel(
     me_ref,
-    scale_ref,
+    wsum_ref,
     stream2_ref,
     targ_ref,
     relief_ref,
-    levels_ref,
     base_ref,
     att_ref,
     gain_ref,
@@ -193,26 +192,25 @@
     gup_ref,
     gdown_ref,
     gout_ref,
-    piece_ref,
     gdown_t_ref,
     pack_ref,
     *,
     block_f,
+    lvls,
+    lats,
 ):
     step = pl.program_id(0)
     me = me_ref[0]
 
     @pl.when(step == 0)
     def _():
-        slots, rows = levels_ref.shape[0], base_ref.shape[0]
         shape = lev_ref.shape
+        slots, rows = SLOTS, shape[0] // (SLOTS * WIN_LON)
+        own = (me // lats) * slots + slots // 2
         token = lax.broadcasted_iota(jnp.int32, shape, 0)
         upper = (lax.broadcasted_iota(jnp.int32, shape, 1) // 16) % 2
         line = token // WIN_LON
-        lev = jnp.full(shape, 2 * levels_ref[0], jnp.int32)
-        for s in range(1, slots):
-            lev = jnp.where(line >= s * rows, 2 * levels_ref[s], lev)
-        lev_ref[...] = lev + upper
+        lev_ref[...] = 2 * ((own + line // rows) % (slots * lvls)) + upper
         wide = jnp.zeros(shape, f32)
         for r in range(rows):
             wide = jnp.where(line % rows == r, base_ref[r : r + 1], wide)
@@ -227,7 +225,7 @@
     wins, win = att_ref.shape[0], att_ref.shape[2]
     ff = wup_ref.shape[1]
     hat, rstd = normalize(stream2)
-    gain = gain_ref[...]
+    gain = gain_ref[1:2]
     normed2 = (hat * gain).astype(bf16)
     hids, slopes, gpres = [], [], []
     for n in range(0, ff, block_f):
@@ -245,9 +243,11 @@
     square = differ * differ + smooth_sq
     inv_err = lax.rsqrt(square)
     num_ref[...] += jnp.sum(cell_w * (square * inv_err), 0, keepdims=True)
-    gpred = (scale_ref[0] * cell_w * differ * inv_err).astype(bf16)
-    out = gpred.shape[1]
-    gout_ref[:, :out] += nn(field.T, gpred)
+    scale = loss_scale / wsum_ref[...]
+    gpred = (scale * cell_w * differ * inv_err).astype(bf16)
+    gout = nn(field.T, gpred)
+    add_pieces(gout_ref, 0, gout[:, :128])
+    gout_ref[1, :, : gout.shape[1] - 128] += gout[:, 128:]
     gfield = nn(gpred, wout_ref[...])
     gfb = gfield.astype(bf16)
     gfbt = gfb.T
@@ -259,22 +259,20 @@
     for n in range(0, ff, block_f):
         cols = slice(n, n + block_f)
         gdown_ref[:, cols] += nn(gfbt, hids[n // block_f])
-        gup_ref[:, cols] += nn(normed2t, gpres[n // block_f])
+        add_pieces(gup_ref, n // 128, nn(normed2t, gpres[n // block_f]))
     gnorm2 = nt(jnp.concatenate(gpres, 1), wup_ref[...])
     gs2 = gfield + norm_back(gnorm2 * gain, hat, rstd)
     gs2_ref[...] = gs2
     gmix = gs2.astype(bf16)
     for w in range(wins):
-        gproj_ref[...] += nn(att_ref[w], gmix[w * win : (w + 1) * win])
+        add_pieces(gproj_ref, 0, nn(att_ref[w], gmix[w * win : (w + 1) * win]))
 
     @pl.when(step == pl.num_programs(0) - 1)
     def _():
         wsel_ref[...] = own_rows(me, wup_ref)
         at = 0
         for ref in (gup_ref, gproj_ref, gout_ref):
-            pieces = piece_ref.at[: ref.shape[1] // 128]
-            cut_pieces(pieces, ref)
-            at = pack_rows(pack_ref, at, pieces)
+            at = pack_rows(pack_ref, at, ref)
         turn_pieces(gdown_t_ref, gdown_ref)
         at = pack_rows(pack_ref, at, gdown_t_ref)
         fill_rows(pack_ref, at)
@@ -296,7 +294,8 @@
     gs2_ref,
     num_ref,
     gbias_ref,
-    send_ref,
+    keep_ref,
+    give_ref,
     wsel_ref,
     gqkv_ref,
     gqkv_t_ref,
@@ -314,7 +313,7 @@
 
     stream, one_hot = stream_of(x_ref, relief_ref, table_ref)
     hat, rstd = normalize(stream)
-    gain = gain_ref[...]
+    gain = gain_ref[:1]
     normed = (hat * gain).astype(bf16)
     d = normed.shape[1]
     count, win = att_ref.shape[0], att_ref.shape[2]
@@ -382,7 +381,14 @@
         every = pack_ref.shape[0] // DEVS
         pack_ref[pl.ds(at, DEVS, stride=every), :] = last
         fill_rows(pack_ref, at + 1)
-        send_ref[...] = pack_ref[...].astype(bf16)
+        lats = DEVS // 4
+        odd = (me_ref[0] // lats) % 2
+        size = lats * every
+        for c in range(2):
+            mine = pl.multiple_of((2 * c + odd) * size, size)
+            other = pl.multiple_of((2 * c + 1 - odd) * size, size)
+            keep_ref[c * size : (c + 1) * size] = pack_ref[pl.ds(mine, size), :].astype(bf16)
+            give_ref[c * size : (c + 1) * size] = pack_ref[pl.ds(other, size), :].astype(bf16)
 
 
 def assemble_kernel(own_ref, up_ref, side_ref, both_ref, out_ref, scr_ref):
@@ -439,7 +445,7 @@
     classes = grel_ref.shape[1]
     for i in range(rows):
         grel_ref[i : i + 1, :] = last[:, i * classes : (i + 1) * classes]
-    loss_ref[...] = (last[:, 126:127] + last[:, 127:128]) / weight_sum_ref[0]
+    loss_ref[...] = (last[:, 126:127] + last[:, 127:128]) / weight_sum_ref[...]
     diag = lax.broadcasted_iota(jnp.int32, (rows, rows), 0) == lax.broadcasted_iota(
         jnp.int32, (rows, rows), 1
     )
@@ -450,11 +456,10 @@
 
 
 def finish(weight_sum, got_t, got_q, w_up, w_qkv, gain_mlp, gain_attn, shapes):
-    smem = pl.BlockSpec(memory_space=pltpu.SMEM)
     vmem = pl.BlockSpec(memory_space=pltpu.VMEM)
     return pl.pallas_call(
         finish_kernel,
-        in_specs=[smem] + [vmem] * 6,
+        in_specs=[vmem] * 7,
         out_specs=[vmem] * len(shapes),
         out_shape=[jax.ShapeDtypeStruct(shape, f32) for shape in shapes],
         compiler_params=pltpu.CompilerParams(vmem_limit_bytes=40 * 2**20),
@@ -488,7 +493,7 @@
             lead((TOGETHER * win, d)),
             lead((TOGETHER * win, 1)),
             whole(table.shape),
-            whole((1, d)),
+            whole((2, d)),
             whole((3 * d, d)),
             whole((d, 3 * d)),
             whole((d, d)),
@@ -512,7 +517,7 @@
         x,
         relief_col,
         table,
-        gain[None],
+        gain,
         wt,
         w_qkv,
         w_proj,
@@ -524,7 +529,7 @@
     return pl.CostEstimate(flops=flops, bytes_accessed=moved, transcendentals=trans)
 
 
-def tail_both(me, scale, stream2, targ, relief_col, lev, base, att, gain, w_up, w_down, w_out, group):
+def tail_both(me, wsum, stream2, targ, relief_col, base, att, gains, w_up, w_down, w_out, group, lvls, lats):
     t, d = stream2.shape
     win = att.shape[-1]
     m = group * win
@@ -533,18 +538,17 @@
     pieces += -pieces % 8
     sds = jax.ShapeDtypeStruct
     return pl.pallas_call(
-        functools.partial(tail_kernel, block_f=256),
+        functools.partial(tail_kernel, block_f=256, lvls=lvls, lats=lats),
         grid=(t // m,),
         in_specs=[
             pl.BlockSpec(memory_space=pltpu.SMEM),
-            pl.BlockSpec(memory_space=pltpu.SMEM),
+            whole((1, 1)),
             lead((m, d)),
             lead((m, out)),
             lead((m, 1)),
-            pl.BlockSpec(memory_space=pltpu.SMEM),
             whole(base.shape),
             lead((group, d, win)),
-            whole((1, d)),
+            whole((2, d)),
             whole((d, ff)),
             whole((ff, d)),
             whole((out, d)),
@@ -564,17 +568,16 @@
         scratch_shapes=[
             pltpu.VMEM((win, out), jnp.int32),
             pltpu.VMEM((win, out), f32),
-            pltpu.VMEM((d, d), f32),
+            pltpu.VMEM((d // 128, d, 128), f32),
+            pltpu.VMEM((ff // 128, d, 128), f32),
             pltpu.VMEM((d, ff), f32),
-            pltpu.VMEM((d, ff), f32),
-            pltpu.VMEM((d, 256), f32),
-            pltpu.VMEM((ff // 128, d, 128), f32),
+            pltpu.VMEM((2, d, 128), f32),
             pltpu.VMEM((d // 128, ff, 128), f32),
             pltpu.VMEM((DEVS * pieces, 128), f32),
         ],
         compiler_params=params_of(),
         name="tail_both",
-    )(me, scale, stream2, targ, relief_col, lev, base, att, gain[None], w_up, w_down, w_out.T)
+    )(me, wsum, stream2, targ, relief_col, base, att, gains, w_up, w_down, w_out.T)
 
 
 def attention_back(me, num, x, relief_col, table, gain, w_qkv, wt, w_proj, qt, probs, att, gs2):
@@ -589,7 +592,7 @@
             lead((TOGETHER * win, d)),
             lead((TOGETHER * win, 1)),
             whole(table.shape),
-            whole((1, d)),
+            whole((2, d)),
             whole((d, 3 * d)),
             whole((3 * d, d)),
             whole((d, d)),
@@ -601,12 +604,14 @@
         ],
         out_specs=[
             whole((HEADS, win, WIDE)),
-            whole((DEVS * 32, 128)),
+            whole((DEVS * 16, 128)),
+            whole((DEVS * 16, 128)),
             whole((8, 3 * d)),
         ],
         out_shape=[
             sds((HEADS, win, WIDE), f32),
-            sds((DEVS * 32, 128), bf16),
+            sds((DEVS * 16, 128), bf16),
+            sds((DEVS * 16, 128), bf16),
             sds((8, 3 * d), f32),
         ],
         scratch_shapes=[
@@ -619,22 +624,7 @@
         compiler_params=params_of(),
         cost_estimate=cost(10 * 2**30, 20 * 2**20, 0),
         name="attention_back",
-    )(me, x, relief_col, table, gain[None], w_qkv, wt, w_proj, qt, probs, att, gs2, num)
-
-
-def lat_weights(row_ids, lat_rows):
-    fine_rows = 4 * row_ids[:, None] + jnp.arange(4, dtype=jnp.int32)[None, :]
-    angle_rad = (90.0 - 180.0 * (fine_rows.astype(f32) + 0.5) / (4.0 * lat_rows)) * (
-        math.pi / 180.0
-    )
-    return jnp.cos(angle_rad)
-
-
-def weight_total(relief, var_weight, level_count):
-    lat_rows = relief.shape[0]
-    lat_weight = jnp.sum(lat_weights(jnp.arange(lat_rows, dtype=jnp.int32), lat_rows), 1)
-    live_levels = (2 * level_count - relief).astype(f32)
-    return jnp.sum(var_weight) * 4.0 * jnp.sum(lat_weight[:, None] * live_levels)
+    )(me, x, relief_col, table, gain, w_qkv, wt, w_proj, qt, probs, att, gs2, num)
 
 
 def from_next(value, axes):
@@ -657,23 +647,27 @@
     return up, side, both
 
 
-def summed_by_chips(send):
-    lvls, lats = lax.axis_size("lvl"), lax.axis_size("lat")
-    odd = lax.axis_index("lvl") % 2
-    halves = send.reshape(lvls // 2, 2, lats, *send.shape[1:])
-    keep = lax.dynamic_index_in_dim(halves, odd, 1, False)
-    give = lax.dynamic_index_in_dim(halves, 1 - odd, 1, False)
-    got = lax.ppermute(give, "lvl", [(i, i ^ 1) for i in range(lvls)])
-    pair = (keep.astype(f32) + got.astype(f32)).astype(bf16)
-    groups = [
-        [lvl * lats + lat for lvl in range(c, lvls, 2) for lat in range(lats)] for c in range(2)
-    ]
-    return lax.all_to_all(
-        pair.reshape(-1, *send.shape[1:]), ("lvl", "lat"), 0, 0, axis_index_groups=groups, tiled=True
-    )
-
-
-def prepare_kernel(me_ref, bias_ref, relief_ref, wqkv_ref, bias_t_ref, col_ref, wt_ref, lane_ref, *, lvls, lats):
+def cos_latitude(fine_rows, lat_rows):
+    angle = 90.0 - 180.0 * (fine_rows.astype(f32) + 0.5) / (4.0 * lat_rows)
+    return jnp.cos(angle * (math.pi / 180.0))
+
+
+def prepare_kernel(
+    me_ref,
+    var_ref,
+    bias_ref,
+    relief_ref,
+    wqkv_ref,
+    bias_t_ref,
+    col_ref,
+    wt_ref,
+    base_ref,
+    wsum_ref,
+    lane_ref,
+    *,
+    lvls,
+    lats,
+):
     me = me_ref[0]
     heads, win, _ = bias_ref.shape
     slots, rows, lon = SLOTS, win // (SLOTS * WIN_LON), relief_ref.shape[0]
@@ -701,10 +695,27 @@
                 at = w * win + (s * rows + r) * WIN_LON
                 lane_ref[at : at + WIN_LON] = col[w * WIN_LON : (w + 1) * WIN_LON]
     col_ref[...] = lane_ref[...].astype(jnp.int32)
+    lat_rows = rows * lats
+    vars_n = var_ref.shape[0]
+    shape = base_ref.shape
+    chan = lax.broadcasted_iota(jnp.int32, shape, 1)
+    row = (first + lax.broadcasted_iota(jnp.int32, shape, 0)) % lat_rows
+    var = jnp.zeros(shape, f32)
+    var_sum = var_ref[0]
+    for v in range(vars_n):
+        var = jnp.where(chan // 32 == v, var_ref[v], var)
+        var_sum = var_sum + var_ref[v] if v else var_sum
+    base_ref[...] = var * cos_latitude(4 * row + (chan // 4) % 4, lat_rows)
+    shape = (8, lat_rows)
+    part = lax.broadcasted_iota(jnp.int32, shape, 0)
+    fine = 4 * lax.broadcasted_iota(jnp.int32, shape, 1) + part
+    lat_weight = jnp.sum(jnp.where(part < 4, cos_latitude(fine, lat_rows), 0.0), 0, keepdims=True)
+    live = jnp.sum(2.0 * slots * lvls - grid, 0, keepdims=True)
+    wsum_ref[...] = jnp.sum(lat_weight * live, 1, keepdims=True) * (4.0 * var_sum)
     wt_ref[...] = wqkv_ref[...].T
 
 
-def prepare(me, earth_bias, relief, w_qkv, lvls, lats):
+def prepare(me, var_weight, earth_bias, relief, w_qkv, lvls, lats):
     heads, win, _ = earth_bias.shape
     rows = win // (SLOTS * WIN_LON)
     tokens = SLOTS * rows * relief.shape[1]
@@ -712,37 +723,19 @@
     vmem = pl.BlockSpec(memory_space=pltpu.VMEM)
     return pl.pallas_call(
         functools.partial(prepare_kernel, lvls=lvls, lats=lats),
-        in_specs=[pl.BlockSpec(memory_space=pltpu.SMEM)] + [vmem] * 3,
-        out_specs=[vmem] * 3,
+        in_specs=[pl.BlockSpec(memory_space=pltpu.SMEM)] * 2 + [vmem] * 3,
+        out_specs=[vmem] * 5,
         out_shape=[
             sds((heads, win, WIDE), f32),
             sds((tokens, 1), jnp.int32),
             sds(w_qkv.shape[::-1], bf16),
+            sds((8, var_weight.shape[0] * 32), f32),
+            sds((1, 1), f32),
         ],
         scratch_shapes=[pltpu.VMEM((tokens, 1), f32)],
         compiler_params=pltpu.CompilerParams(vmem_limit_bytes=40 * 2**20),
         name="prepare_inputs",
-    )(me, earth_bias, relief.T, w_qkv)
-
-
-def local_inputs(tokens_shape, var_weight):
-    slots_dev, rows_dev, _, _ = tokens_shape
-    lvl_count, lat_count = lax.axis_size("lvl"), lax.axis_size("lat")
-    lvl_id, lat_id = lax.axis_index("lvl"), lax.axis_index("lat")
-    level_total, lat_rows = slots_dev * lvl_count, rows_dev * lat_count
-    level_ids = (
-        lvl_id * slots_dev + jnp.arange(slots_dev, dtype=jnp.int32) + slots_dev // 2
-    ) % level_total
-    row_ids = (
-        lat_id * rows_dev + jnp.arange(rows_dev, dtype=jnp.int32) + rows_dev // 2
-    ) % lat_rows
-    vars_n = var_weight.shape[0]
-    base = jnp.broadcast_to(
-        var_weight[None, :, None, None, None]
-        * lat_weights(row_ids, lat_rows)[:, None, None, :, None],
-        (rows_dev, vars_n, 2, 4, 4),
-    ).reshape(rows_dev, vars_n * 32)
-    return level_ids, base
+    )(me, var_weight, earth_bias, relief.T, w_qkv)
 
 
 def body(
@@ -762,34 +755,39 @@
 ):
     axes = ("lvl", "lat")
     devs = lax.axis_size("lvl") * lax.axis_size("lat")
-    level_total = tokens.shape[0] * lax.axis_size("lvl")
-    weight_sum = weight_total(relief, var_weight, level_total)
     token_halo = halo_of(tokens)
     me = lax.axis_index(axes)
-    bias_t, relief_col, wt = prepare(
-        me.reshape(1), earth_bias[0, 0], relief, w_qkv, lax.axis_size("lvl"), lax.axis_size("lat")
-    )
-    lev, base = local_inputs(tokens.shape, var_weight)
-    scale = (loss_scale / weight_sum).reshape(1)
-    tokens, targets, relief_col, bias_t, base, lev, scale, wt = lax.optimization_barrier(
-        (tokens, targets, relief_col, bias_t, base, lev, scale, wt)
+    lvls, lats = lax.axis_size("lvl"), lax.axis_size("lat")
+    bias_t, relief_col, wt, base, wsum = prepare(
+        me.reshape(1), var_weight, earth_bias[0, 0], relief, w_qkv, lvls, lats
+    )
+    gains = jnp.stack([gain_attn, gain_mlp])
+    tokens, targets, relief_col, bias_t, base, wsum, wt, gains = lax.optimization_barrier(
+        (tokens, targets, relief_col, bias_t, base, wsum, wt, gains)
     )
     targ_halo = halo_of(targets)
     x = assemble(tokens, *token_halo)
     stream2, qt, probs, att = attention_forward(
-        x, relief_col, relief_table, gain_attn, w_qkv, wt, w_proj, bias_t
+        x, relief_col, relief_table, gains, w_qkv, wt, w_proj, bias_t
     )
     stream2, targets = lax.optimization_barrier((stream2, targets))
     targ = assemble(targets, *targ_halo)
     num, gs2, send_t, up_rows = tail_both(
-        me.reshape(1), scale, stream2, targ, relief_col, lev, base, att, gain_mlp, w_up, w_down, w_out, GROUP
+        me.reshape(1), wsum, stream2, targ, relief_col, base, att, gains, w_up, w_down, w_out, GROUP, lvls, lats
     )
     got_t = lax.all_to_all(send_t.reshape(devs, -1, 128), axes, 0, 0, tiled=True)
-    gbias_t, send_q, qkv_rows = attention_back(
-        me.reshape(1), num, x, relief_col, relief_table, gain_attn, w_qkv, wt, w_proj, qt, probs, att, gs2
-    )
-    send_q, got_t = lax.optimization_barrier((send_q.reshape(devs, -1, 128), got_t))
-    got_q = summed_by_chips(send_q)
+    gbias_t, keep, give, qkv_rows = attention_back(
+        me.reshape(1), num, x, relief_col, relief_table, gains, w_qkv, wt, w_proj, qt, probs, att, gs2
+    )
+    got = lax.ppermute(give, "lvl", [(i, i ^ 1) for i in range(lvls)])
+    pair = (keep.astype(f32) + got.astype(f32)).astype(bf16)
+    pair, got_t = lax.optimization_barrier((pair, got_t))
+    groups = [
+        [lvl * lats + lat for lvl in range(c, lvls, 2) for lat in range(lats)] for c in range(2)
+    ]
+    got_q = lax.all_to_all(
+        pair.reshape(devs // 2, -1, 128), axes, 0, 0, axis_index_groups=groups, tiled=True
+    )
     d = tokens.shape[-1]
     share = d // devs
 
@@ -808,7 +806,7 @@
         (share, relief_table.shape[0]),
     )
     sums = finish(
-        weight_sum.reshape(1), got_t, got_q, up_rows, qkv_rows, mine(gain_mlp), mine(gain_attn), shapes
+        wsum, got_t, got_q, up_rows, qkv_rows, mine(gain_mlp), mine(gain_attn), shapes
     )
     return (
         sums[0][0, 0],

time: 163 us -> 162 us (level)
  starting transfers between devices: 28.8 us -> 34 us
  local copies, waits for them, and re-layouts: 17.6 us -> 13.8 us
    all_to_all x1, waiting for transfers between devices: 3.42 us -> 0.01 us  [body(): lax.all_to_all(send_t.reshape(devs, -1, 128), axes, 0, 0, tiled=True)]
    all_to_all x1, starting transfers between devices: 6.71 us -> 10.1 us  [body(): lax.all_to_all(pair.reshape(devs // 2, -1, 128), axes, 0, 0, axis_index_g...]
    ppermute x6, waiting for transfers between devices: 1.19 us -> 4.31 us  [from_next(): return lax.ppermute(value, ('lvl', 'lat'), pairs)]
    squeeze x1 -> x0, local copies, waits for them, and re-layouts: 1.88 us -> none  [summed_by_chips(): give = lax.dynamic_index_in_dim(halves, 1 - odd, 1, False)]
    ppermute x6, starting transfers between devices: 12.4 us -> 14.1 us  [from_next(): return lax.ppermute(value, ('lvl', 'lat'), pairs)]
    unnamed x31 -> x33, local copies, waits for them, and re-layouts: 8.61 us -> 8.63 us
  transfers between devices with their start and end apart: 9 -> 9, of which waited for: 4 -> 3; matrix products, arithmetic and copies ran while one was open for 6% -> 5% of each run, Pallas kernels for 38% -> 38%
where the time goes in v4:
time: 162 us
  Pallas kernels  97.1 us (60%)
  starting transfers between devices  34 us (21%)
  local copies, waits for them, and re-layouts  13.8 us (9%)
  waiting for transfers between devices  13.8 us (9%)
  other arithmetic  2.61 us (2%)
    pallas_call x1, Pallas kernels, attention_back(): pl.pallas_call(back_kernel, grid=(count // TOGETHER,), in_specs=[pl.Block...  35.1 us
    pallas_call x1, Pallas kernels, tail_both(): pl.pallas_call(functools.partial(tail_kernel, block_f=256, lvls=lvls, lat...  33.8 us
    pallas_call x1, Pallas kernels, attention_forward(): pl.pallas_call(att_kernel, grid=(count // TOGETHER,), in_specs=[lead((TOG...  23.5 us
    ppermute x6, starting transfers between devices, from_next(): return lax.ppermute(value, ('lvl', 'lat'), pairs)  14.1 us
    all_to_all x1, starting transfers between devices, body(): lax.all_to_all(pair.reshape(devs // 2, -1, 128), axes, 0, 0, axis_index_g...  10.1 us
    all_to_all x1, starting transfers between devices, body(): lax.all_to_all(send_t.reshape(devs, -1, 128), axes, 0, 0, tiled=True)  9.71 us
    unnamed x33, local copies, waits for them, and re-layouts  8.63 us
    all_to_all x1, waiting for transfers between devices, body(): lax.all_to_all(pair.reshape(devs // 2, -1, 128), axes, 0, 0, axis_index_g...  7.35 us
  transfers between devices with their start and end apart: 9, of which 3 were waited for; matrix products, arithmetic and copies ran while one was open for 5% of the time, Pallas kernels for 38%

profile of v4, /device:TPU:0, one launch (start us, length us, event | category | flops | bytes accessed | tf_op | source)
XLA Modules:
  0.0 162.0 jit_solution(4401082880625760085)
XLA Ops:
  0.7 2.2 %fusion = (bf16[1,3,144,384]{3,2,1,0:T(8,128)(2,1)S(1)}, bf16[1,3,144,384]{3,2,1,0:T(8,128)(2,1)}, bf16[1,3,144,384]{3,2,1,0:T(8,128)(2,1)}) fusion(bf16[2,6,144,384]{3,2,1,0:T(8,128)(2,1)} %own_ref), kind=kLoop, calls=%fused_computation.5 | loop fusion | bytes 1990656 | tf_op jit(solution)/shard_map/slice | solution.py:646
  2.9 2.7 %collective-permute-start = (bf16[1,3,144,384]{3,2,1,0:T(8,128)(2,1)}, bf16[1,3,144,384]{3,2,1,0:T(8,128)(2,1)S(1)}, u32[]{:S(2)}, u32[]{:S(2)}) collective-permute-start(bf16[1,3,144,384]{3,2,1,0:T(8,128)(2,1)} %get-tuple-element.97), channel_id=1, source_target_pairs={{32,0},{33,1},{34,2},{35,3},{36,4},{37,5},{38,6},{39,7},{40,8},{41... | collective-permute-start | bytes 995336 | tf_op jit(solution)/shard_map/ppermute | solution.py:638
  5.6 6.3 %collective-permute-start.1 = (bf16[1,3,144,384]{3,2,1,0:T(8,128)(2,1)}, bf16[1,3,144,384]{3,2,1,0:T(8,128)(2,1)S(1)}, u32[]{:S(2)}, u32[]{:S(2)}) collective-permute-start(bf16[1,3,144,384]{3,2,1,0:T(8,128)(2,1)} %get-tuple-element.98), channel_id=1, source_target_pairs={{1,0},{2,1},{3,2},{4,3},{5,4},{6,5},{7,6},{8,7},{9,8},{10,9},{11,1... | collective-permute-start | bytes 995336 | tf_op jit(solution)/shard_map/ppermute | solution.py:638
  12.3 1.5 copy-done.6
  13.8 2.0 %prepare_inputs.1 = (f32[12,144,256]{2,1,0:T(8,128)S(1)}, s32[1728,1]{1,0:T(8,128)S(1)}, bf16[1152,384]{1,0:T(8,128)(2,1)S(1)}, f32[8,160]{1,0:T(8,128)S(1)}, f32[1,1]{1,0:T(1,128)}) custom-call(s32[1]{0:T(128)} %bitcast.me_ref, f32[5]{0:T(128)S(1)} %copy-done.13, f32[12,144,144]{2,1,0:T(8,128)S(1)} %bitcast.17, s32[144,192]{1,0:T(8,128)S(1)} %bitcast.18, ...), custom_call_target="tpu_custom_call" | custom-call | tf_op jit(solution)/shard_map/prepare_inputs/pallas_call | solution.py:724
  15.8 1.2 copy-done.7
  17.0 0.9 copy-done.8
  18.6 1.4 collective-permute-start.3
  20.0 1.6 collective-permute-start.4
  21.6 1.7 %collective-permute-start.5 = (bf16[1,3,144,160]{3,2,1,0:T(8,128)(2,1)S(1)}, bf16[1,3,144,160]{3,2,1,0:T(8,128)(2,1)S(1)}, u32[]{:S(2)}, u32[]{:S(2)}) collective-permute-start(bf16[1,3,144,160]{3,2,1,0:T(8,128)(2,1)S(1)} %get-tuple-element.99), channel_id=1, source_target_pairs={{33,0},{34,1},{35,2},{36,3},{37,4},{38,5},{39,6},{40,7},{41,8},{42... | collective-permute-start | bytes 414728 | tf_op jit(solution)/shard_map/ppermute | solution.py:638
  23.3 4.3 %collective-permute-done.2.both_ref = bf16[1,3,144,384]{3,2,1,0:T(8,128)(2,1)S(1)} collective-permute-done((bf16[1,3,144,384]{3,2,1,0:T(8,128)(2,1)S(1)}, bf16[1,3,144,384]{3,2,1,0:T(8,128)(2,1)S(1)}, u32[]{:S(2)}, u32[]{:S(2)}) %collective-permute-start.2) | collective-permute-done | bytes 331808 | tf_op jit(solution)/shard_map/ppermute | solution.py:638
  28.1 1.1 copy-done
  29.2 23.5 %attention_forward.1 = (f32[1728,384]{1,0:T(8,128)}, bf16[12,384,256]{2,1,0:T(8,128)(2,1)}, bf16[12,12,144,256]{3,2,1,0:T(8,128)(2,1)}, bf16[12,384,144]{2,1,0:T(8,128)(2,1)}) custom-call(bf16[1728,384]{1,0:T(8,128)(2,1)} %copy-done, s32[1728,1]{1,0:T(8,128)} %copy-done.2, bf16[4,384]{1,0:T(4,128)(2,1)} %table_ref.3, f32[2,384]{1,0:T(2,128)} %pad_maximum_fusion.gain_ref, ...), custom_call_target="tpu_custom_call" | custom-call | tf_op jit(solution)/shard_map/attention_forward/pallas_call | solution.py:489
  53.1 0.9 copy-done.3
  54.0 33.8 %tail_both.1 = (f32[1,160]{1,0:T(1,128)}, f32[1728,384]{1,0:T(8,128)}, bf16[11264,128]{1,0:T(8,128)(2,1)}, f32[8,1536]{1,0:T(8,128)}) custom-call(s32[1]{0:T(128)} %bitcast.me_ref, f32[1,1]{1,0:T(1,128)} %get-tuple-element.53.wsum_ref.weight_sum_ref, f32[1728,384]{1,0:T(8,128)} %get-tuple-element.64.stream2_ref, bf16[1728,160]{1,0:T(8,128)(2,1)} %copy-done.3, ...), custom_call_target="tpu_custom_call" | custom-call | tf_op jit(solution)/shard_map/tail_both/pallas_call | solution.py:540
  87.7 9.7 %all-to-all-start = ((bf16[128,88,128]{2,1,0:T(8,128)(2,1)}), bf16[128,88,128]{2,1,0:T(8,128)(2,1)S(1)}, u32[]{:S(2)}, u32[]{:S(2)}) async-start(bf16[128,88,128]{2,1,0:T(8,128)(2,1)} %bitcast.19), calls=%async_computation | async-start | bytes 5767168 | tf_op jit(solution)/shard_map/all_to_all | solution.py:778
  97.5 35.1 %attention_back.1 = (f32[12,144,256]{2,1,0:T(8,128)}, bf16[2048,128]{1,0:T(8,128)(2,1)}, bf16[2048,128]{1,0:T(8,128)(2,1)}, f32[8,1152]{1,0:T(8,128)}) custom-call(s32[1]{0:T(128)} %bitcast.me_ref, bf16[1728,384]{1,0:T(8,128)(2,1)} %copy-done, s32[1728,1]{1,0:T(8,128)} %copy-done.2, bf16[4,384]{1,0:T(4,128)(2,1)} %table_ref.3, ...), custom_call_target="tpu_custom_call" | custom-call | flops 10737418240 | bytes 20971520 | tf_op jit(solution)/shard_map/attention_back/pallas_call | solution.py:587
  132.7 2.1 %collective-permute-done.6 = bf16[2048,128]{1,0:T(8,128)(2,1)S(1)} collective-permute-done((bf16[2048,128]{1,0:T(8,128)(2,1)}, bf16[2048,128]{1,0:T(8,128)(2,1)S(1)}, u32[]{:S(2)}, u32[]{:S(2)}) %collective-permute-start.6) | collective-permute-done | bytes 524320 | tf_op jit(solution)/shard_map/ppermute | solution.py:782
  134.8 2.0 %add_convert_fusion = bf16[2048,128]{1,0:T(8,128)(2,1)} fusion(bf16[2048,128]{1,0:T(8,128)(2,1)S(1)} %collective-permute-done.6, bf16[2048,128]{1,0:T(8,128)(2,1)} %get-tuple-element.69), kind=kLoop, calls=%fused_computation.1 | loop fusion | flops 1048576 | bytes 1572864 | tf_op jit(solution)/shard_map/convert_element_type | solution.py:783
  136.8 10.1 %all-to-all-start.1 = ((bf16[64,32,128]{2,1,0:T(8,128)(2,1)}), bf16[64,32,128]{2,1,0:T(8,128)(2,1)S(1)}, u32[]{:S(2)}, u32[]{:S(2)}) async-start(bf16[64,32,128]{2,1,0:T(8,128)(2,1)} %bitcast.20), calls=%async_computation.1 | async-start | bytes 1048576 | tf_op jit(solution)/shard_map/all_to_all | solution.py:788
  147.0 2.8 %slice_bitcast_fusion = f32[1,1,12,144,144]{3,4,2,1,0:T(8,128)} fusion(f32[12,144,256]{2,1,0:T(8,128)} %get-tuple-element.85), kind=kLoop, calls=%fused_computation | loop fusion | bytes 1990656 | tf_op jit(solution)/shard_map/broadcast_in_dim | solution.py:817
  149.8 3.0 %copy.23 = f32[1,1,12,144,144]{4,3,2,1,0:T(8,128)} copy(f32[1,1,12,144,144]{3,4,2,1,0:T(8,128)} %slice_bitcast_fusion) | data formatting | bytes 1990656
  152.8 7.3 %all-to-all-done.1.gotq_ref = bf16[64,32,128]{2,1,0:T(8,128)(2,1)S(1)} async-done(((bf16[64,32,128]{2,1,0:T(8,128)(2,1)}), bf16[64,32,128]{2,1,0:T(8,128)(2,1)S(1)}, u32[]{:S(2)}, u32[]{:S(2)}) %all-to-all-start.1) | async-done | bytes 524320 | tf_op jit(solution)/shard_map/all_to_all | solution.py:788
  160.2 1.9 %finish_sums.1 = (f32[1,1]{1,0:T(1,128)}, f32[3,1152]{1,0:T(4,128)}, f32[3,384]{1,0:T(4,128)}, f32[3,1536]{1,0:T(4,128)}, f32[12,384]{1,0:T(8,128)}, /*index=5*/...) custom-call(f32[1,1]{1,0:T(1,128)} %get-tuple-element.53.wsum_ref.weight_sum_ref, ...), custom_call_target="tpu_custom_call" | custom-call | tf_op jit(solution)/shard_map/finish_sums/pallas_call | solution.py:460
  (42 shorter events, 2.0 us)
Async XLA Ops:
  0.6 11.6 %copy-start.14 = (f32[384]{0:T(512)S(1)}, f32[384]{0:T(512)}, u32[]{:S(2)}) copy-start(f32[384]{0:T(512)} %param.19) | copy-start | bytes 4612
  0.7 11.6 %copy-start.15 = (f32[384]{0:T(512)S(1)}, f32[384]{0:T(512)}, u32[]{:S(2)}) copy-start(f32[384]{0:T(512)} %param.18) | copy-start | bytes 4612
  0.7 11.6 %copy-start.13 = (f32[5]{0:T(128)S(1)}, f32[5]{0:T(128)}, u32[]{:S(2)}) copy-start(f32[5]{0:T(128)} %var_ref.1) | copy-start | bytes 64
  0.7 11.6 %copy-start.9 = (s32[192,144]{0,1:T(8,128)S(1)}, s32[192,144]{0,1:T(8,128)}, u32[]{:S(2)}) copy-start(s32[192,144]{0,1:T(8,128)} %param.15) | copy-start | bytes 331780
  0.7 11.6 %copy-start.4 = (bf16[384,1152]{1,0:T(8,128)(2,1)S(1)}, bf16[384,1152]{1,0:T(8,128)(2,1)}, u32[]{:S(2)}) copy-start(bf16[384,1152]{1,0:T(8,128)(2,1)} %wqkv_ref.5) | copy-start | bytes 2654212
  2.9 15.6 %copy-start.5 = (bf16[2,6,144,160]{3,2,1,0:T(8,128)(2,1)S(1)}, bf16[2,6,144,160]{3,2,1,0:T(8,128)(2,1)}, u32[]{:S(2)}) copy-start(bf16[2,6,144,160]{3,2,1,0:T(8,128)(2,1)} %own_ref.1) | copy-start | bytes 1658884
  2.9 18.7 %collective-permute-start = (bf16[1,3,144,384]{3,2,1,0:T(8,128)(2,1)}, bf16[1,3,144,384]{3,2,1,0:T(8,128)(2,1)S(1)}, u32[]{:S(2)}, u32[]{:S(2)}) collective-permute-start(bf16[1,3,144,384]{3,2,1,0:T(8,128)(2,1)} %get-tuple-element.97), channel_id=1, source_target_pairs={{32,0},{33,1},{34,2},{35,3},{36,4},{37,5},{38,6},{39,7},{40,8},{41... | collective-permute-start | bytes 995336 | tf_op jit(solution)/shard_map/ppermute | solution.py:638
  5.6 17.7 %collective-permute-start.1 = (bf16[1,3,144,384]{3,2,1,0:T(8,128)(2,1)}, bf16[1,3,144,384]{3,2,1,0:T(8,128)(2,1)S(1)}, u32[]{:S(2)}, u32[]{:S(2)}) collective-permute-start(bf16[1,3,144,384]{3,2,1,0:T(8,128)(2,1)} %get-tuple-element.98), channel_id=1, source_target_pairs={{1,0},{2,1},{3,2},{4,3},{5,4},{6,5},{7,6},{8,7},{9,8},{10,9},{11,1... | collective-permute-start | bytes 995336 | tf_op jit(solution)/shard_map/ppermute | solution.py:638
  12.0 15.6 %collective-permute-start.2 = (bf16[1,3,144,384]{3,2,1,0:T(8,128)(2,1)S(1)}, bf16[1,3,144,384]{3,2,1,0:T(8,128)(2,1)S(1)}, u32[]{:S(2)}, u32[]{:S(2)}) collective-permute-start(bf16[1,3,144,384]{3,2,1,0:T(8,128)(2,1)S(1)} %get-tuple-element.96), channel_id=1, source_target_pairs={{33,0},{34,1},{35,2},{36,3},{37,4},{38,5},{39,6},{40,7},{41,8},{42... | collective-permute-start | bytes 995336 | tf_op jit(solution)/shard_map/ppermute | solution.py:638
  12.3 1.5 copy-start.6
  13.8 13.8 %copy-start.1 = (bf16[2,6,144,384]{3,2,1,0:T(8,128)(2,1)S(1)}, bf16[2,6,144,384]{3,2,1,0:T(8,128)(2,1)}, u32[]{:S(2)}) copy-start(bf16[2,6,144,384]{3,2,1,0:T(8,128)(2,1)} %own_ref) | copy-start | bytes 3981316
  15.8 1.2 copy-start.7
  17.9 5.4 %copy-start.2 = (s32[1728,1]{1,0:T(8,128)}, s32[1728,1]{1,0:T(8,128)S(1)}, u32[]{:S(2)}) copy-start(s32[1728,1]{1,0:T(8,128)S(1)} %get-tuple-element.55.relief_ref) | copy-start | bytes 20740
  17.9 9.7 %copy-start.12 = (f32[8,160]{1,0:T(8,128)}, f32[8,160]{1,0:T(8,128)S(1)}, u32[]{:S(2)}) copy-start(f32[8,160]{1,0:T(8,128)S(1)} %get-tuple-element.66.base_ref) | copy-start | bytes 15364
  18.6 34.1 %collective-permute-start.3 = (bf16[1,3,144,160]{3,2,1,0:T(8,128)(2,1)S(1)}, bf16[1,3,144,160]{3,2,1,0:T(8,128)(2,1)S(1)}, u32[]{:S(2)}, u32[]{:S(2)}) collective-permute-start(bf16[1,3,144,160]{3,2,1,0:T(8,128)(2,1)S(1)} %get-tuple-element.101), channel_id=1, source_target_pairs={{32,0},{33,1},{34,2},{35,3},{36,4},{37,5},{38,6},{39,7},{40,8},{41... | collective-permute-start | bytes 414728 | tf_op jit(solution)/shard_map/ppermute | solution.py:638
  20.0 32.7 %collective-permute-start.4 = (bf16[1,3,144,160]{3,2,1,0:T(8,128)(2,1)S(1)}, bf16[1,3,144,160]{3,2,1,0:T(8,128)(2,1)S(1)}, u32[]{:S(2)}, u32[]{:S(2)}) collective-permute-start(bf16[1,3,144,160]{3,2,1,0:T(8,128)(2,1)S(1)} %get-tuple-element.100), channel_id=1, source_target_pairs={{1,0},{2,1},{3,2},{4,3},{5,4},{6,5},{7,6},{8,7},{9,8},{10,9},{11,1... | collective-permute-start | bytes 414728 | tf_op jit(solution)/shard_map/ppermute | solution.py:638
  21.6 31.1 %collective-permute-start.5 = (bf16[1,3,144,160]{3,2,1,0:T(8,128)(2,1)S(1)}, bf16[1,3,144,160]{3,2,1,0:T(8,128)(2,1)S(1)}, u32[]{:S(2)}, u32[]{:S(2)}) collective-permute-start(bf16[1,3,144,160]{3,2,1,0:T(8,128)(2,1)S(1)} %get-tuple-element.99), channel_id=1, source_target_pairs={{33,0},{34,1},{35,2},{36,3},{37,4},{38,5},{39,6},{40,7},{41,8},{42... | collective-permute-start | bytes 414728 | tf_op jit(solution)/shard_map/ppermute | solution.py:638
  28.1 1.1 copy-start
  53.1 0.9 copy-start.3
  87.7 49.0 %all-to-all-start = ((bf16[128,88,128]{2,1,0:T(8,128)(2,1)}), bf16[128,88,128]{2,1,0:T(8,128)(2,1)S(1)}, u32[]{:S(2)}, u32[]{:S(2)}) async-start(bf16[128,88,128]{2,1,0:T(8,128)(2,1)} %bitcast.19), calls=%async_computation | async-start | bytes 5767168 | tf_op jit(solution)/shard_map/all_to_all | solution.py:778
  132.6 2.2 %collective-permute-start.6 = (bf16[2048,128]{1,0:T(8,128)(2,1)}, bf16[2048,128]{1,0:T(8,128)(2,1)S(1)}, u32[]{:S(2)}, u32[]{:S(2)}) collective-permute-start(bf16[2048,128]{1,0:T(8,128)(2,1)} %get-tuple-element.70), channel_id=1, source_target_pairs={{0,32},{32,0},{64,96},{96,64},{1,33},{33,1},{65,97},{97,65},{2,34}... | collective-permute-start | bytes 1572872 | tf_op jit(solution)/shard_map/ppermute | solution.py:782
  136.8 23.4 %all-to-all-start.1 = ((bf16[64,32,128]{2,1,0:T(8,128)(2,1)}), bf16[64,32,128]{2,1,0:T(8,128)(2,1)S(1)}, u32[]{:S(2)}, u32[]{:S(2)}) async-start(bf16[64,32,128]{2,1,0:T(8,128)(2,1)} %bitcast.20), calls=%async_computation.1 | async-start | bytes 1048576 | tf_op jit(solution)/shard_map/all_to_all | solution.py:788
  149.8 10.3 %copy-start.10 = (f32[8,1536]{1,0:T(8,128)S(1)}, f32[8,1536]{1,0:T(8,128)}, u32[]{:S(2)}) copy-start(f32[8,1536]{1,0:T(8,128)} %get-tuple-element.74.wup_ref) | copy-start | bytes 147460
  149.8 10.3 %copy-start.11 = (f32[8,1152]{1,0:T(8,128)S(1)}, f32[8,1152]{1,0:T(8,128)}, u32[]{:S(2)}) copy-start(f32[8,1152]{1,0:T(8,128)} %get-tuple-element.75.wqkv_ref) | copy-start | bytes 110596
  (1 other events, 0.9 us)

commit v5 on v4

--- a/solution.py
+++ b/solution.py
@@ -298,7 +298,6 @@
     give_ref,
     wsel_ref,
     gqkv_ref,
-    gqkv_t_ref,
     grel_ref,
     grel_t_ref,
     pack_ref,
@@ -331,7 +330,7 @@
     for u in range(count):
         filled = jnp.concatenate([normed[u * win : (u + 1) * win], pad], 0)
         kts.append(nt(wt_ref[d : 2 * d], filled).astype(bf16)[:, :win])
-    gshift = []
+    gturned = []
     for u in range(count):
         wrows = slice(u * win, (u + 1) * win)
         gatt_b = gatts[u]
@@ -356,17 +355,17 @@
                 gks.append((nt(qt[rows], gsb) * (1.0 / log2_e)).astype(bf16))
                 gvs.append(nt(gatt_b[rows], prob).astype(bf16))
         gheads = jnp.concatenate(gqs + gks + gvs, 0)
-        gqkv_ref[...] += nn(gheads, normed[wrows])
-        gshift.append(nn(wqkv_ref[...], gheads).astype(bf16).T.astype(f32))
-    gshift = jnp.concatenate(gshift, 0)
+        gturned.append(gheads.T)
+    gturned = jnp.concatenate(gturned, 0)
+    gshift = nn(gturned, wt_ref[...]).astype(bf16).astype(f32)
+    add_pieces(gqkv_ref, 0, nn(normed.T, gturned))
     gstream = gs2 + norm_back(gshift * gain, hat, rstd)
     grel_ref[...] += tn(one_hot, gstream.astype(bf16))
 
     @pl.when(step == pl.num_programs(0) - 1)
     def _():
         wsel_ref[...] = own_rows(me_ref[0], wqkv_ref)
-        turn_pieces(gqkv_t_ref, gqkv_ref)
-        at = pack_rows(pack_ref, 0, gqkv_t_ref)
+        at = pack_rows(pack_ref, 0, gqkv_ref)
         classes = grel_ref.shape[0]
         wide = jnp.concatenate([grel_ref[...], jnp.zeros((128 - classes, d), f32)], 0)
         grel_t_ref[...] = wide.T
@@ -615,7 +614,6 @@
             sds((8, 3 * d), f32),
         ],
         scratch_shapes=[
-            pltpu.VMEM((3 * d, d), f32),
             pltpu.VMEM((3 * d // 128, d, 128), f32),
             pltpu.VMEM((table.shape[0], d), f32),
             pltpu.VMEM((d, 128), f32),

time: 162 us -> 158 us (0.975)
  Pallas kernels: 97.1 us -> 92.9 us
  starting transfers between devices: 34 us -> 30.6 us
  waiting for transfers between devices: 13.8 us -> 17.2 us
    pallas_call x1, Pallas kernels: 35.1 us -> 31 us  [attention_back(): pl.pallas_call(back_kernel, grid=(count // TOGETHER,), in_specs=[pl.Block...]
    all_to_all x1, waiting for transfers between devices: 0.01 us -> 3.42 us  [body(): lax.all_to_all(send_t.reshape(devs, -1, 128), axes, 0, 0, tiled=True)]
    all_to_all x1, starting transfers between devices: 10.1 us -> 6.76 us  [body(): lax.all_to_all(pair.reshape(devs // 2, -1, 128), axes, 0, 0, axis_index_g...]
  transfers between devices with their start and end apart: 9 -> 9, of which waited for: 3 -> 4; matrix products, arithmetic and copies ran while one was open for 5% -> 5% of each run, Pallas kernels for 38% -> 36%
where the time goes in v5:
time: 158 us
  Pallas kernels  92.9 us (59%)
  starting transfers between devices  30.6 us (19%)
  waiting for transfers between devices  17.2 us (11%)
  local copies, waits for them, and re-layouts  13.8 us (9%)
  other arithmetic  2.61 us (2%)
    pallas_call x1, Pallas kernels, tail_both(): pl.pallas_call(functools.partial(tail_kernel, block_f=256, lvls=lvls, lat...  33.8 us
    pallas_call x1, Pallas kernels, attention_back(): pl.pallas_call(back_kernel, grid=(count // TOGETHER,), in_specs=[pl.Block...  31 us
    pallas_call x1, Pallas kernels, attention_forward(): pl.pallas_call(att_kernel, grid=(count // TOGETHER,), in_specs=[lead((TOG...  23.5 us
    ppermute x6, starting transfers between devices, from_next(): return lax.ppermute(value, ('lvl', 'lat'), pairs)  14.1 us
    all_to_all x1, starting transfers between devices, body(): lax.all_to_all(send_t.reshape(devs, -1, 128), axes, 0, 0, tiled=True)  9.71 us
    unnamed x33, local copies, waits for them, and re-layouts  8.63 us
    all_to_all x1, waiting for transfers between devices, body(): lax.all_to_all(pair.reshape(devs // 2, -1, 128), axes, 0, 0, axis_index_g...  7.34 us
    all_to_all x1, starting transfers between devices, body(): lax.all_to_all(pair.reshape(devs // 2, -1, 128), axes, 0, 0, axis_index_g...  6.76 us
  transfers between devices with their start and end apart: 9, of which 4 were waited for; matrix products, arithmetic and copies ran while one was open for 5% of the time, Pallas kernels for 36%

profile of v5, /device:TPU:0, one launch (start us, length us, event | category | flops | bytes accessed | tf_op | source)
XLA Modules:
  0.0 157.9 jit_solution(7167639843248877089)
XLA Ops:
  0.7 2.2 %fusion = (bf16[1,3,144,384]{3,2,1,0:T(8,128)(2,1)S(1)}, bf16[1,3,144,384]{3,2,1,0:T(8,128)(2,1)}, bf16[1,3,144,384]{3,2,1,0:T(8,128)(2,1)}) fusion(bf16[2,6,144,384]{3,2,1,0:T(8,128)(2,1)} %own_ref), kind=kLoop, calls=%fused_computation.5 | loop fusion | bytes 1990656 | tf_op jit(solution)/shard_map/slice | solution.py:644
  2.9 2.7 %collective-permute-start = (bf16[1,3,144,384]{3,2,1,0:T(8,128)(2,1)}, bf16[1,3,144,384]{3,2,1,0:T(8,128)(2,1)S(1)}, u32[]{:S(2)}, u32[]{:S(2)}) collective-permute-start(bf16[1,3,144,384]{3,2,1,0:T(8,128)(2,1)} %get-tuple-element.97), channel_id=1, source_target_pairs={{32,0},{33,1},{34,2},{35,3},{36,4},{37,5},{38,6},{39,7},{40,8},{41... | collective-permute-start | bytes 995336 | tf_op jit(solution)/shard_map/ppermute | solution.py:636
  5.6 6.3 %collective-permute-start.1 = (bf16[1,3,144,384]{3,2,1,0:T(8,128)(2,1)}, bf16[1,3,144,384]{3,2,1,0:T(8,128)(2,1)S(1)}, u32[]{:S(2)}, u32[]{:S(2)}) collective-permute-start(bf16[1,3,144,384]{3,2,1,0:T(8,128)(2,1)} %get-tuple-element.98), channel_id=1, source_target_pairs={{1,0},{2,1},{3,2},{4,3},{5,4},{6,5},{7,6},{8,7},{9,8},{10,9},{11,1... | collective-permute-start | bytes 995336 | tf_op jit(solution)/shard_map/ppermute | solution.py:636
  12.3 1.5 copy-done.6
  13.8 2.0 %prepare_inputs.1 = (f32[12,144,256]{2,1,0:T(8,128)S(1)}, s32[1728,1]{1,0:T(8,128)S(1)}, bf16[1152,384]{1,0:T(8,128)(2,1)S(1)}, f32[8,160]{1,0:T(8,128)S(1)}, f32[1,1]{1,0:T(1,128)}) custom-call(s32[1]{0:T(128)} %bitcast.me_ref, f32[5]{0:T(128)S(1)} %copy-done.13, f32[12,144,144]{2,1,0:T(8,128)S(1)} %bitcast.17, s32[144,192]{1,0:T(8,128)S(1)} %bitcast.18, ...), custom_call_target="tpu_custom_call" | custom-call | tf_op jit(solution)/shard_map/prepare_inputs/pallas_call | solution.py:722
  15.8 1.2 copy-done.7
  17.0 0.9 copy-done.8
  18.6 1.4 collective-permute-start.3
  20.0 1.6 %collective-permute-start.4 = (bf16[1,3,144,160]{3,2,1,0:T(8,128)(2,1)S(1)}, bf16[1,3,144,160]{3,2,1,0:T(8,128)(2,1)S(1)}, u32[]{:S(2)}, u32[]{:S(2)}) collective-permute-start(bf16[1,3,144,160]{3,2,1,0:T(8,128)(2,1)S(1)} %get-tuple-element.100), channel_id=1, source_target_pairs={{1,0},{2,1},{3,2},{4,3},{5,4},{6,5},{7,6},{8,7},{9,8},{10,9},{11,1... | collective-permute-start | bytes 414728 | tf_op jit(solution)/shard_map/ppermute | solution.py:636
  21.6 1.7 %collective-permute-start.5 = (bf16[1,3,144,160]{3,2,1,0:T(8,128)(2,1)S(1)}, bf16[1,3,144,160]{3,2,1,0:T(8,128)(2,1)S(1)}, u32[]{:S(2)}, u32[]{:S(2)}) collective-permute-start(bf16[1,3,144,160]{3,2,1,0:T(8,128)(2,1)S(1)} %get-tuple-element.99), channel_id=1, source_target_pairs={{33,0},{34,1},{35,2},{36,3},{37,4},{38,5},{39,6},{40,7},{41,8},{42... | collective-permute-start | bytes 414728 | tf_op jit(solution)/shard_map/ppermute | solution.py:636
  23.3 4.3 %collective-permute-done.2.both_ref = bf16[1,3,144,384]{3,2,1,0:T(8,128)(2,1)S(1)} collective-permute-done((bf16[1,3,144,384]{3,2,1,0:T(8,128)(2,1)S(1)}, bf16[1,3,144,384]{3,2,1,0:T(8,128)(2,1)S(1)}, u32[]{:S(2)}, u32[]{:S(2)}) %collective-permute-start.2) | collective-permute-done | bytes 331808 | tf_op jit(solution)/shard_map/ppermute | solution.py:636
  28.1 1.1 copy-done
  29.2 23.5 %attention_forward.1 = (f32[1728,384]{1,0:T(8,128)}, bf16[12,384,256]{2,1,0:T(8,128)(2,1)}, bf16[12,12,144,256]{3,2,1,0:T(8,128)(2,1)}, bf16[12,384,144]{2,1,0:T(8,128)(2,1)}) custom-call(bf16[1728,384]{1,0:T(8,128)(2,1)} %copy-done, s32[1728,1]{1,0:T(8,128)} %copy-done.2, bf16[4,384]{1,0:T(4,128)(2,1)} %table_ref.3, f32[2,384]{1,0:T(2,128)} %pad_maximum_fusion.gain_ref, ...), custom_call_target="tpu_custom_call" | custom-call | tf_op jit(solution)/shard_map/attention_forward/pallas_call | solution.py:488
  54.0 33.8 %tail_both.1 = (f32[1,160]{1,0:T(1,128)}, f32[1728,384]{1,0:T(8,128)}, bf16[11264,128]{1,0:T(8,128)(2,1)}, f32[8,1536]{1,0:T(8,128)}) custom-call(s32[1]{0:T(128)} %bitcast.me_ref, f32[1,1]{1,0:T(1,128)} %get-tuple-element.53.wsum_ref.weight_sum_ref, f32[1728,384]{1,0:T(8,128)} %get-tuple-element.64.stream2_ref, bf16[1728,160]{1,0:T(8,128)(2,1)} %copy-done.3, ...), custom_call_target="tpu_custom_call" | custom-call | tf_op jit(solution)/shard_map/tail_both/pallas_call | solution.py:539
  87.7 9.7 %all-to-all-start = ((bf16[128,88,128]{2,1,0:T(8,128)(2,1)}), bf16[128,88,128]{2,1,0:T(8,128)(2,1)S(1)}, u32[]{:S(2)}, u32[]{:S(2)}) async-start(bf16[128,88,128]{2,1,0:T(8,128)(2,1)} %bitcast.19), calls=%async_computation | async-start | bytes 5767168 | tf_op jit(solution)/shard_map/all_to_all | solution.py:776
  97.5 31.0 %attention_back.1 = (f32[12,144,256]{2,1,0:T(8,128)}, bf16[2048,128]{1,0:T(8,128)(2,1)}, bf16[2048,128]{1,0:T(8,128)(2,1)}, f32[8,1152]{1,0:T(8,128)}) custom-call(s32[1]{0:T(128)} %bitcast.me_ref, bf16[1728,384]{1,0:T(8,128)(2,1)} %copy-done, s32[1728,1]{1,0:T(8,128)} %copy-done.2, bf16[4,384]{1,0:T(4,128)(2,1)} %table_ref.3, ...), custom_call_target="tpu_custom_call" | custom-call | flops 10737418240 | bytes 20971520 | tf_op jit(solution)/shard_map/attention_back/pallas_call | solution.py:586
  128.5 2.1 %collective-permute-done.6 = bf16[2048,128]{1,0:T(8,128)(2,1)S(1)} collective-permute-done((bf16[2048,128]{1,0:T(8,128)(2,1)}, bf16[2048,128]{1,0:T(8,128)(2,1)S(1)}, u32[]{:S(2)}, u32[]{:S(2)}) %collective-permute-start.6) | collective-permute-done | bytes 524320 | tf_op jit(solution)/shard_map/ppermute | solution.py:780
  130.6 2.0 %add_convert_fusion = bf16[2048,128]{1,0:T(8,128)(2,1)} fusion(bf16[2048,128]{1,0:T(8,128)(2,1)S(1)} %collective-permute-done.6, bf16[2048,128]{1,0:T(8,128)(2,1)} %get-tuple-element.69), kind=kLoop, calls=%fused_computation.1 | loop fusion | flops 1048576 | bytes 1572864 | tf_op jit(solution)/shard_map/convert_element_type | solution.py:781
  132.6 3.4 %all-to-all-done.gott_ref = bf16[128,88,128]{2,1,0:T(8,128)(2,1)S(1)} async-done(((bf16[128,88,128]{2,1,0:T(8,128)(2,1)}), bf16[128,88,128]{2,1,0:T(8,128)(2,1)S(1)}, u32[]{:S(2)}, u32[]{:S(2)}) %all-to-all-start) | async-done | bytes 2883616 | tf_op jit(solution)/shard_map/all_to_all | solution.py:776
  136.0 6.8 %all-to-all-start.1 = ((bf16[64,32,128]{2,1,0:T(8,128)(2,1)}), bf16[64,32,128]{2,1,0:T(8,128)(2,1)S(1)}, u32[]{:S(2)}, u32[]{:S(2)}) async-start(bf16[64,32,128]{2,1,0:T(8,128)(2,1)} %bitcast.20), calls=%async_computation.1 | async-start | bytes 1048576 | tf_op jit(solution)/shard_map/all_to_all | solution.py:786
  142.9 2.8 %slice_bitcast_fusion = f32[1,1,12,144,144]{3,4,2,1,0:T(8,128)} fusion(f32[12,144,256]{2,1,0:T(8,128)} %get-tuple-element.85), kind=kLoop, calls=%fused_computation | loop fusion | bytes 1990656 | tf_op jit(solution)/shard_map/broadcast_in_dim | solution.py:815
  145.7 3.0 %copy.23 = f32[1,1,12,144,144]{4,3,2,1,0:T(8,128)} copy(f32[1,1,12,144,144]{3,4,2,1,0:T(8,128)} %slice_bitcast_fusion) | data formatting | bytes 1990656
  148.7 7.3 %all-to-all-done.1.gotq_ref = bf16[64,32,128]{2,1,0:T(8,128)(2,1)S(1)} async-done(((bf16[64,32,128]{2,1,0:T(8,128)(2,1)}), bf16[64,32,128]{2,1,0:T(8,128)(2,1)S(1)}, u32[]{:S(2)}, u32[]{:S(2)}) %all-to-all-start.1) | async-done | bytes 524320 | tf_op jit(solution)/shard_map/all_to_all | solution.py:786
  156.0 1.9 %finish_sums.1 = (f32[1,1]{1,0:T(1,128)}, f32[3,1152]{1,0:T(4,128)}, f32[3,384]{1,0:T(4,128)}, f32[3,1536]{1,0:T(4,128)}, f32[12,384]{1,0:T(8,128)}, /*index=5*/...) custom-call(f32[1,1]{1,0:T(1,128)} %get-tuple-element.53.wsum_ref.weight_sum_ref, ...), custom_call_target="tpu_custom_call" | custom-call | tf_op jit(solution)/shard_map/finish_sums/pallas_call | solution.py:459
  (42 shorter events, 2.9 us)
Async XLA Ops:
  0.6 11.6 %copy-start.14 = (f32[384]{0:T(512)S(1)}, f32[384]{0:T(512)}, u32[]{:S(2)}) copy-start(f32[384]{0:T(512)} %param.19) | copy-start | bytes 4612
  0.7 11.6 %copy-start.15 = (f32[384]{0:T(512)S(1)}, f32[384]{0:T(512)}, u32[]{:S(2)}) copy-start(f32[384]{0:T(512)} %param.18) | copy-start | bytes 4612
  0.7 11.6 %copy-start.13 = (f32[5]{0:T(128)S(1)}, f32[5]{0:T(128)}, u32[]{:S(2)}) copy-start(f32[5]{0:T(128)} %var_ref.1) | copy-start | bytes 64
  0.7 11.6 %copy-start.9 = (s32[192,144]{0,1:T(8,128)S(1)}, s32[192,144]{0,1:T(8,128)}, u32[]{:S(2)}) copy-start(s32[192,144]{0,1:T(8,128)} %param.15) | copy-start | bytes 331780
  0.7 11.6 %copy-start.4 = (bf16[384,1152]{1,0:T(8,128)(2,1)S(1)}, bf16[384,1152]{1,0:T(8,128)(2,1)}, u32[]{:S(2)}) copy-start(bf16[384,1152]{1,0:T(8,128)(2,1)} %wqkv_ref.5) | copy-start | bytes 2654212
  2.9 15.6 %copy-start.5 = (bf16[2,6,144,160]{3,2,1,0:T(8,128)(2,1)S(1)}, bf16[2,6,144,160]{3,2,1,0:T(8,128)(2,1)}, u32[]{:S(2)}) copy-start(bf16[2,6,144,160]{3,2,1,0:T(8,128)(2,1)} %own_ref.1) | copy-start | bytes 1658884
  2.9 18.7 %collective-permute-start = (bf16[1,3,144,384]{3,2,1,0:T(8,128)(2,1)}, bf16[1,3,144,384]{3,2,1,0:T(8,128)(2,1)S(1)}, u32[]{:S(2)}, u32[]{:S(2)}) collective-permute-start(bf16[1,3,144,384]{3,2,1,0:T(8,128)(2,1)} %get-tuple-element.97), channel_id=1, source_target_pairs={{32,0},{33,1},{34,2},{35,3},{36,4},{37,5},{38,6},{39,7},{40,8},{41... | collective-permute-start | bytes 995336 | tf_op jit(solution)/shard_map/ppermute | solution.py:636
  5.6 17.7 %collective-permute-start.1 = (bf16[1,3,144,384]{3,2,1,0:T(8,128)(2,1)}, bf16[1,3,144,384]{3,2,1,0:T(8,128)(2,1)S(1)}, u32[]{:S(2)}, u32[]{:S(2)}) collective-permute-start(bf16[1,3,144,384]{3,2,1,0:T(8,128)(2,1)} %get-tuple-element.98), channel_id=1, source_target_pairs={{1,0},{2,1},{3,2},{4,3},{5,4},{6,5},{7,6},{8,7},{9,8},{10,9},{11,1... | collective-permute-start | bytes 995336 | tf_op jit(solution)/shard_map/ppermute | solution.py:636
  12.0 15.6 %collective-permute-start.2 = (bf16[1,3,144,384]{3,2,1,0:T(8,128)(2,1)S(1)}, bf16[1,3,144,384]{3,2,1,0:T(8,128)(2,1)S(1)}, u32[]{:S(2)}, u32[]{:S(2)}) collective-permute-start(bf16[1,3,144,384]{3,2,1,0:T(8,128)(2,1)S(1)} %get-tuple-element.96), channel_id=1, source_target_pairs={{33,0},{34,1},{35,2},{36,3},{37,4},{38,5},{39,6},{40,7},{41,8},{42... | collective-permute-start | bytes 995336 | tf_op jit(solution)/shard_map/ppermute | solution.py:636
  12.3 1.5 copy-start.6
  13.8 13.8 %copy-start.1 = (bf16[2,6,144,384]{3,2,1,0:T(8,128)(2,1)S(1)}, bf16[2,6,144,384]{3,2,1,0:T(8,128)(2,1)}, u32[]{:S(2)}) copy-start(bf16[2,6,144,384]{3,2,1,0:T(8,128)(2,1)} %own_ref) | copy-start | bytes 3981316
  15.8 1.2 copy-start.7
  17.9 5.4 %copy-start.2 = (s32[1728,1]{1,0:T(8,128)}, s32[1728,1]{1,0:T(8,128)S(1)}, u32[]{:S(2)}) copy-start(s32[1728,1]{1,0:T(8,128)S(1)} %get-tuple-element.55.relief_ref) | copy-start | bytes 20740
  17.9 9.7 %copy-start.12 = (f32[8,160]{1,0:T(8,128)}, f32[8,160]{1,0:T(8,128)S(1)}, u32[]{:S(2)}) copy-start(f32[8,160]{1,0:T(8,128)S(1)} %get-tuple-element.66.base_ref) | copy-start | bytes 15364
  18.6 34.1 %collective-permute-start.3 = (bf16[1,3,144,160]{3,2,1,0:T(8,128)(2,1)S(1)}, bf16[1,3,144,160]{3,2,1,0:T(8,128)(2,1)S(1)}, u32[]{:S(2)}, u32[]{:S(2)}) collective-permute-start(bf16[1,3,144,160]{3,2,1,0:T(8,128)(2,1)S(1)} %get-tuple-element.101), channel_id=1, source_target_pairs={{32,0},{33,1},{34,2},{35,3},{36,4},{37,5},{38,6},{39,7},{40,8},{41... | collective-permute-start | bytes 414728 | tf_op jit(solution)/shard_map/ppermute | solution.py:636
  20.0 32.7 %collective-permute-start.4 = (bf16[1,3,144,160]{3,2,1,0:T(8,128)(2,1)S(1)}, bf16[1,3,144,160]{3,2,1,0:T(8,128)(2,1)S(1)}, u32[]{:S(2)}, u32[]{:S(2)}) collective-permute-start(bf16[1,3,144,160]{3,2,1,0:T(8,128)(2,1)S(1)} %get-tuple-element.100), channel_id=1, source_target_pairs={{1,0},{2,1},{3,2},{4,3},{5,4},{6,5},{7,6},{8,7},{9,8},{10,9},{11,1... | collective-permute-start | bytes 414728 | tf_op jit(solution)/shard_map/ppermute | solution.py:636
  21.6 31.1 %collective-permute-start.5 = (bf16[1,3,144,160]{3,2,1,0:T(8,128)(2,1)S(1)}, bf16[1,3,144,160]{3,2,1,0:T(8,128)(2,1)S(1)}, u32[]{:S(2)}, u32[]{:S(2)}) collective-permute-start(bf16[1,3,144,160]{3,2,1,0:T(8,128)(2,1)S(1)} %get-tuple-element.99), channel_id=1, source_target_pairs={{33,0},{34,1},{35,2},{36,3},{37,4},{38,5},{39,6},{40,7},{41,8},{42... | collective-permute-start | bytes 414728 | tf_op jit(solution)/shard_map/ppermute | solution.py:636
  28.1 1.1 copy-start
  53.1 0.9 copy-start.3
  87.7 48.3 %all-to-all-start = ((bf16[128,88,128]{2,1,0:T(8,128)(2,1)}), bf16[128,88,128]{2,1,0:T(8,128)(2,1)S(1)}, u32[]{:S(2)}, u32[]{:S(2)}) async-start(bf16[128,88,128]{2,1,0:T(8,128)(2,1)} %bitcast.19), calls=%async_computation | async-start | bytes 5767168 | tf_op jit(solution)/shard_map/all_to_all | solution.py:776
  128.4 2.2 %collective-permute-start.6 = (bf16[2048,128]{1,0:T(8,128)(2,1)}, bf16[2048,128]{1,0:T(8,128)(2,1)S(1)}, u32[]{:S(2)}, u32[]{:S(2)}) collective-permute-start(bf16[2048,128]{1,0:T(8,128)(2,1)} %get-tuple-element.70), channel_id=1, source_target_pairs={{0,32},{32,0},{64,96},{96,64},{1,33},{33,1},{65,97},{97,65},{2,34}... | collective-permute-start | bytes 1572872 | tf_op jit(solution)/shard_map/ppermute | solution.py:780
  136.0 20.0 %all-to-all-start.1 = ((bf16[64,32,128]{2,1,0:T(8,128)(2,1)}), bf16[64,32,128]{2,1,0:T(8,128)(2,1)S(1)}, u32[]{:S(2)}, u32[]{:S(2)}) async-start(bf16[64,32,128]{2,1,0:T(8,128)(2,1)} %bitcast.20), calls=%async_computation.1 | async-start | bytes 1048576 | tf_op jit(solution)/shard_map/all_to_all | solution.py:786
  145.7 10.3 %copy-start.10 = (f32[8,1536]{1,0:T(8,128)S(1)}, f32[8,1536]{1,0:T(8,128)}, u32[]{:S(2)}) copy-start(f32[8,1536]{1,0:T(8,128)} %get-tuple-element.74.wup_ref) | copy-start | bytes 147460
  145.7 10.3 %copy-start.11 = (f32[8,1152]{1,0:T(8,128)S(1)}, f32[8,1152]{1,0:T(8,128)}, u32[]{:S(2)}) copy-start(f32[8,1152]{1,0:T(8,128)} %get-tuple-element.75.wqkv_ref) | copy-start | bytes 110596
  (1 other events, 0.9 us)

commit v6 on v5

--- a/solution.py
+++ b/solution.py
@@ -14,7 +14,7 @@
 DEVS = 128
 WIDE = 256
 SLOTS = 2
-TOGETHER = 3
+TOGETHER = 4
 norm_eps = 1e-05
 loss_scale = 32768.0
 smooth_sq = 0.01

time: 158 us -> 157 us (level)
  Pallas kernels: 92.9 us -> 91.1 us
    pallas_call x1, Pallas kernels: 23.5 us -> 21.6 us  [attention_forward(): pl.pallas_call(att_kernel, grid=(count // TOGETHER,), in_specs=[lead((TOG...]
  transfers between devices with their start and end apart: 9 -> 9, of which waited for: 4 -> 4; matrix products, arithmetic and copies ran while one was open for 5% -> 5% of each run, Pallas kernels for 36% -> 35%
where the time goes in v6:
time: 157 us; the launch traced here: 156 us
  Pallas kernels  91.1 us (58%)
  starting transfers between devices  30.7 us (20%)
  waiting for transfers between devices  17 us (11%)
  local copies, waits for them, and re-layouts  13.8 us (9%)
  other arithmetic  2.61 us (2%)
    pallas_call x1, Pallas kernels, tail_both(): pl.pallas_call(functools.partial(tail_kernel, block_f=256, lvls=lvls, lat...  33.8 us
    pallas_call x1, Pallas kernels, attention_back(): pl.pallas_call(back_kernel, grid=(count // TOGETHER,), in_specs=[pl.Block...  31.1 us
    pallas_call x1, Pallas kernels, attention_forward(): pl.pallas_call(att_kernel, grid=(count // TOGETHER,), in_specs=[lead((TOG...  21.6 us
    ppermute x6, starting transfers between devices, from_next(): return lax.ppermute(value, ('lvl', 'lat'), pairs)  14.1 us
    all_to_all x1, starting transfers between devices, body(): lax.all_to_all(send_t.reshape(devs, -1, 128), axes, 0, 0, tiled=True)  9.7 us
    unnamed x33, local copies, waits for them, and re-layouts  8.63 us
    all_to_all x1, waiting for transfers between devices, body(): lax.all_to_all(pair.reshape(devs // 2, -1, 128), axes, 0, 0, axis_index_g...  7.35 us
    all_to_all x1, starting transfers between devices, body(): lax.all_to_all(pair.reshape(devs // 2, -1, 128), axes, 0, 0, axis_index_g...  6.86 us
  transfers between devices with their start and end apart: 9, of which 4 were waited for; matrix products, arithmetic and copies ran while one was open for 5% of the time, Pallas kernels for 35%

profile of v6, /device:TPU:0, one launch (start us, length us, event | category | flops | bytes accessed | tf_op | source)
XLA Modules:
  0.0 156.1 jit_solution(15567321622217279248)
XLA Ops:
  0.7 2.2 %fusion = (bf16[1,3,144,384]{3,2,1,0:T(8,128)(2,1)S(1)}, bf16[1,3,144,384]{3,2,1,0:T(8,128)(2,1)}, bf16[1,3,144,384]{3,2,1,0:T(8,128)(2,1)}) fusion(bf16[2,6,144,384]{3,2,1,0:T(8,128)(2,1)} %own_ref), kind=kLoop, calls=%fused_computation.5 | loop fusion | bytes 1990656 | tf_op jit(solution)/shard_map/slice | solution.py:644
  2.9 2.7 %collective-permute-start = (bf16[1,3,144,384]{3,2,1,0:T(8,128)(2,1)}, bf16[1,3,144,384]{3,2,1,0:T(8,128)(2,1)S(1)}, u32[]{:S(2)}, u32[]{:S(2)}) collective-permute-start(bf16[1,3,144,384]{3,2,1,0:T(8,128)(2,1)} %get-tuple-element.97), channel_id=1, source_target_pairs={{32,0},{33,1},{34,2},{35,3},{36,4},{37,5},{38,6},{39,7},{40,8},{41... | collective-permute-start | bytes 995336 | tf_op jit(solution)/shard_map/ppermute | solution.py:636
  5.6 6.3 %collective-permute-start.1 = (bf16[1,3,144,384]{3,2,1,0:T(8,128)(2,1)}, bf16[1,3,144,384]{3,2,1,0:T(8,128)(2,1)S(1)}, u32[]{:S(2)}, u32[]{:S(2)}) collective-permute-start(bf16[1,3,144,384]{3,2,1,0:T(8,128)(2,1)} %get-tuple-element.98), channel_id=1, source_target_pairs={{1,0},{2,1},{3,2},{4,3},{5,4},{6,5},{7,6},{8,7},{9,8},{10,9},{11,1... | collective-permute-start | bytes 995336 | tf_op jit(solution)/shard_map/ppermute | solution.py:636
  12.3 1.5 copy-done.6
  13.8 2.0 %prepare_inputs.1 = (f32[12,144,256]{2,1,0:T(8,128)S(1)}, s32[1728,1]{1,0:T(8,128)S(1)}, bf16[1152,384]{1,0:T(8,128)(2,1)S(1)}, f32[8,160]{1,0:T(8,128)S(1)}, f32[1,1]{1,0:T(1,128)}) custom-call(s32[1]{0:T(128)} %bitcast.me_ref, f32[5]{0:T(128)S(1)} %copy-done.13, f32[12,144,144]{2,1,0:T(8,128)S(1)} %bitcast.17, s32[144,192]{1,0:T(8,128)S(1)} %bitcast.18, ...), custom_call_target="tpu_custom_call" | custom-call | tf_op jit(solution)/shard_map/prepare_inputs/pallas_call | solution.py:722
  15.8 1.2 copy-done.7
  17.0 0.9 copy-done.8
  18.6 1.4 collective-permute-start.3
  20.0 1.6 %collective-permute-start.4 = (bf16[1,3,144,160]{3,2,1,0:T(8,128)(2,1)S(1)}, bf16[1,3,144,160]{3,2,1,0:T(8,128)(2,1)S(1)}, u32[]{:S(2)}, u32[]{:S(2)}) collective-permute-start(bf16[1,3,144,160]{3,2,1,0:T(8,128)(2,1)S(1)} %get-tuple-element.100), channel_id=1, source_target_pairs={{1,0},{2,1},{3,2},{4,3},{5,4},{6,5},{7,6},{8,7},{9,8},{10,9},{11,1... | collective-permute-start | bytes 414728 | tf_op jit(solution)/shard_map/ppermute | solution.py:636
  21.6 1.7 %collective-permute-start.5 = (bf16[1,3,144,160]{3,2,1,0:T(8,128)(2,1)S(1)}, bf16[1,3,144,160]{3,2,1,0:T(8,128)(2,1)S(1)}, u32[]{:S(2)}, u32[]{:S(2)}) collective-permute-start(bf16[1,3,144,160]{3,2,1,0:T(8,128)(2,1)S(1)} %get-tuple-element.99), channel_id=1, source_target_pairs={{33,0},{34,1},{35,2},{36,3},{37,4},{38,5},{39,6},{40,7},{41,8},{42... | collective-permute-start | bytes 414728 | tf_op jit(solution)/shard_map/ppermute | solution.py:636
  23.3 4.3 %collective-permute-done.2.both_ref = bf16[1,3,144,384]{3,2,1,0:T(8,128)(2,1)S(1)} collective-permute-done((bf16[1,3,144,384]{3,2,1,0:T(8,128)(2,1)S(1)}, bf16[1,3,144,384]{3,2,1,0:T(8,128)(2,1)S(1)}, u32[]{:S(2)}, u32[]{:S(2)}) %collective-permute-start.2) | collective-permute-done | bytes 331808 | tf_op jit(solution)/shard_map/ppermute | solution.py:636
  28.1 1.1 copy-done
  29.2 21.6 %attention_forward.1 = (f32[1728,384]{1,0:T(8,128)}, bf16[12,384,256]{2,1,0:T(8,128)(2,1)}, bf16[12,12,144,256]{3,2,1,0:T(8,128)(2,1)}, bf16[12,384,144]{2,1,0:T(8,128)(2,1)}) custom-call(bf16[1728,384]{1,0:T(8,128)(2,1)} %copy-done, s32[1728,1]{1,0:T(8,128)} %copy-done.2, bf16[4,384]{1,0:T(4,128)(2,1)} %table_ref.3, f32[2,384]{1,0:T(2,128)} %pad_maximum_fusion.gain_ref, ...), custom_call_target="tpu_custom_call" | custom-call | tf_op jit(solution)/shard_map/attention_forward/pallas_call | solution.py:488
  52.1 33.8 %tail_both.1 = (f32[1,160]{1,0:T(1,128)}, f32[1728,384]{1,0:T(8,128)}, bf16[11264,128]{1,0:T(8,128)(2,1)}, f32[8,1536]{1,0:T(8,128)}) custom-call(s32[1]{0:T(128)} %bitcast.me_ref, f32[1,1]{1,0:T(1,128)} %get-tuple-element.53.wsum_ref.weight_sum_ref, f32[1728,384]{1,0:T(8,128)} %get-tuple-element.64.stream2_ref, bf16[1728,160]{1,0:T(8,128)(2,1)} %copy-done.3, ...), custom_call_target="tpu_custom_call" | custom-call | tf_op jit(solution)/shard_map/tail_both/pallas_call | solution.py:539
  85.8 9.7 %all-to-all-start = ((bf16[128,88,128]{2,1,0:T(8,128)(2,1)}), bf16[128,88,128]{2,1,0:T(8,128)(2,1)S(1)}, u32[]{:S(2)}, u32[]{:S(2)}) async-start(bf16[128,88,128]{2,1,0:T(8,128)(2,1)} %bitcast.19), calls=%async_computation | async-start | bytes 5767168 | tf_op jit(solution)/shard_map/all_to_all | solution.py:776
  95.5 31.1 %attention_back.1 = (f32[12,144,256]{2,1,0:T(8,128)}, bf16[2048,128]{1,0:T(8,128)(2,1)}, bf16[2048,128]{1,0:T(8,128)(2,1)}, f32[8,1152]{1,0:T(8,128)}) custom-call(s32[1]{0:T(128)} %bitcast.me_ref, bf16[1728,384]{1,0:T(8,128)(2,1)} %copy-done, s32[1728,1]{1,0:T(8,128)} %copy-done.2, bf16[4,384]{1,0:T(4,128)(2,1)} %table_ref.3, ...), custom_call_target="tpu_custom_call" | custom-call | flops 10737418240 | bytes 20971520 | tf_op jit(solution)/shard_map/attention_back/pallas_call | solution.py:586
  126.7 2.1 %collective-permute-done.6 = bf16[2048,128]{1,0:T(8,128)(2,1)S(1)} collective-permute-done((bf16[2048,128]{1,0:T(8,128)(2,1)}, bf16[2048,128]{1,0:T(8,128)(2,1)S(1)}, u32[]{:S(2)}, u32[]{:S(2)}) %collective-permute-start.6) | collective-permute-done | bytes 524320 | tf_op jit(solution)/shard_map/ppermute | solution.py:780
  128.8 2.0 %add_convert_fusion = bf16[2048,128]{1,0:T(8,128)(2,1)} fusion(bf16[2048,128]{1,0:T(8,128)(2,1)S(1)} %collective-permute-done.6, bf16[2048,128]{1,0:T(8,128)(2,1)} %get-tuple-element.69), kind=kLoop, calls=%fused_computation.1 | loop fusion | flops 1048576 | bytes 1572864 | tf_op jit(solution)/shard_map/convert_element_type | solution.py:781
  130.8 3.3 %all-to-all-done.gott_ref = bf16[128,88,128]{2,1,0:T(8,128)(2,1)S(1)} async-done(((bf16[128,88,128]{2,1,0:T(8,128)(2,1)}), bf16[128,88,128]{2,1,0:T(8,128)(2,1)S(1)}, u32[]{:S(2)}, u32[]{:S(2)}) %all-to-all-start) | async-done | bytes 2883616 | tf_op jit(solution)/shard_map/all_to_all | solution.py:776
  134.1 6.9 %all-to-all-start.1 = ((bf16[64,32,128]{2,1,0:T(8,128)(2,1)}), bf16[64,32,128]{2,1,0:T(8,128)(2,1)S(1)}, u32[]{:S(2)}, u32[]{:S(2)}) async-start(bf16[64,32,128]{2,1,0:T(8,128)(2,1)} %bitcast.20), calls=%async_computation.1 | async-start | bytes 1048576 | tf_op jit(solution)/shard_map/all_to_all | solution.py:786
  141.0 2.8 %slice_bitcast_fusion = f32[1,1,12,144,144]{3,4,2,1,0:T(8,128)} fusion(f32[12,144,256]{2,1,0:T(8,128)} %get-tuple-element.85), kind=kLoop, calls=%fused_computation | loop fusion | bytes 1990656 | tf_op jit(solution)/shard_map/broadcast_in_dim | solution.py:815
  143.9 3.0 %copy.23 = f32[1,1,12,144,144]{4,3,2,1,0:T(8,128)} copy(f32[1,1,12,144,144]{3,4,2,1,0:T(8,128)} %slice_bitcast_fusion) | data formatting | bytes 1990656
  146.8 7.3 %all-to-all-done.1.gotq_ref = bf16[64,32,128]{2,1,0:T(8,128)(2,1)S(1)} async-done(((bf16[64,32,128]{2,1,0:T(8,128)(2,1)}), bf16[64,32,128]{2,1,0:T(8,128)(2,1)S(1)}, u32[]{:S(2)}, u32[]{:S(2)}) %all-to-all-start.1) | async-done | bytes 524320 | tf_op jit(solution)/shard_map/all_to_all | solution.py:786
  154.2 1.9 %finish_sums.1 = (f32[1,1]{1,0:T(1,128)}, f32[3,1152]{1,0:T(4,128)}, f32[3,384]{1,0:T(4,128)}, f32[3,1536]{1,0:T(4,128)}, f32[12,384]{1,0:T(8,128)}, /*index=5*/...) custom-call(f32[1,1]{1,0:T(1,128)} %get-tuple-element.53.wsum_ref.weight_sum_ref, ...), custom_call_target="tpu_custom_call" | custom-call | tf_op jit(solution)/shard_map/finish_sums/pallas_call | solution.py:459
  (42 shorter events, 2.9 us)
Async XLA Ops:
  0.6 11.6 %copy-start.14 = (f32[384]{0:T(512)S(1)}, f32[384]{0:T(512)}, u32[]{:S(2)}) copy-start(f32[384]{0:T(512)} %param.19) | copy-start | bytes 4612
  0.7 11.6 %copy-start.15 = (f32[384]{0:T(512)S(1)}, f32[384]{0:T(512)}, u32[]{:S(2)}) copy-start(f32[384]{0:T(512)} %param.18) | copy-start | bytes 4612
  0.7 11.6 %copy-start.13 = (f32[5]{0:T(128)S(1)}, f32[5]{0:T(128)}, u32[]{:S(2)}) copy-start(f32[5]{0:T(128)} %var_ref.1) | copy-start | bytes 64
  0.7 11.6 %copy-start.9 = (s32[192,144]{0,1:T(8,128)S(1)}, s32[192,144]{0,1:T(8,128)}, u32[]{:S(2)}) copy-start(s32[192,144]{0,1:T(8,128)} %param.15) | copy-start | bytes 331780
  0.7 11.6 %copy-start.4 = (bf16[384,1152]{1,0:T(8,128)(2,1)S(1)}, bf16[384,1152]{1,0:T(8,128)(2,1)}, u32[]{:S(2)}) copy-start(bf16[384,1152]{1,0:T(8,128)(2,1)} %wqkv_ref.5) | copy-start | bytes 2654212
  2.9 15.6 %copy-start.5 = (bf16[2,6,144,160]{3,2,1,0:T(8,128)(2,1)S(1)}, bf16[2,6,144,160]{3,2,1,0:T(8,128)(2,1)}, u32[]{:S(2)}) copy-start(bf16[2,6,144,160]{3,2,1,0:T(8,128)(2,1)} %own_ref.1) | copy-start | bytes 1658884
  2.9 18.7 %collective-permute-start = (bf16[1,3,144,384]{3,2,1,0:T(8,128)(2,1)}, bf16[1,3,144,384]{3,2,1,0:T(8,128)(2,1)S(1)}, u32[]{:S(2)}, u32[]{:S(2)}) collective-permute-start(bf16[1,3,144,384]{3,2,1,0:T(8,128)(2,1)} %get-tuple-element.97), channel_id=1, source_target_pairs={{32,0},{33,1},{34,2},{35,3},{36,4},{37,5},{38,6},{39,7},{40,8},{41... | collective-permute-start | bytes 995336 | tf_op jit(solution)/shard_map/ppermute | solution.py:636
  5.6 17.7 %collective-permute-start.1 = (bf16[1,3,144,384]{3,2,1,0:T(8,128)(2,1)}, bf16[1,3,144,384]{3,2,1,0:T(8,128)(2,1)S(1)}, u32[]{:S(2)}, u32[]{:S(2)}) collective-permute-start(bf16[1,3,144,384]{3,2,1,0:T(8,128)(2,1)} %get-tuple-element.98), channel_id=1, source_target_pairs={{1,0},{2,1},{3,2},{4,3},{5,4},{6,5},{7,6},{8,7},{9,8},{10,9},{11,1... | collective-permute-start | bytes 995336 | tf_op jit(solution)/shard_map/ppermute | solution.py:636
  12.0 15.6 %collective-permute-start.2 = (bf16[1,3,144,384]{3,2,1,0:T(8,128)(2,1)S(1)}, bf16[1,3,144,384]{3,2,1,0:T(8,128)(2,1)S(1)}, u32[]{:S(2)}, u32[]{:S(2)}) collective-permute-start(bf16[1,3,144,384]{3,2,1,0:T(8,128)(2,1)S(1)} %get-tuple-element.96), channel_id=1, source_target_pairs={{33,0},{34,1},{35,2},{36,3},{37,4},{38,5},{39,6},{40,7},{41,8},{42... | collective-permute-start | bytes 995336 | tf_op jit(solution)/shard_map/ppermute | solution.py:636
  12.3 1.5 copy-start.6
  13.8 13.8 %copy-start.1 = (bf16[2,6,144,384]{3,2,1,0:T(8,128)(2,1)S(1)}, bf16[2,6,144,384]{3,2,1,0:T(8,128)(2,1)}, u32[]{:S(2)}) copy-start(bf16[2,6,144,384]{3,2,1,0:T(8,128)(2,1)} %own_ref) | copy-start | bytes 3981316
  15.8 1.2 copy-start.7
  17.9 5.4 %copy-start.2 = (s32[1728,1]{1,0:T(8,128)}, s32[1728,1]{1,0:T(8,128)S(1)}, u32[]{:S(2)}) copy-start(s32[1728,1]{1,0:T(8,128)S(1)} %get-tuple-element.55.relief_ref) | copy-start | bytes 20740
  17.9 9.7 %copy-start.12 = (f32[8,160]{1,0:T(8,128)}, f32[8,160]{1,0:T(8,128)S(1)}, u32[]{:S(2)}) copy-start(f32[8,160]{1,0:T(8,128)S(1)} %get-tuple-element.66.base_ref) | copy-start | bytes 15364
  18.6 32.2 %collective-permute-start.3 = (bf16[1,3,144,160]{3,2,1,0:T(8,128)(2,1)S(1)}, bf16[1,3,144,160]{3,2,1,0:T(8,128)(2,1)S(1)}, u32[]{:S(2)}, u32[]{:S(2)}) collective-permute-start(bf16[1,3,144,160]{3,2,1,0:T(8,128)(2,1)S(1)} %get-tuple-element.101), channel_id=1, source_target_pairs={{32,0},{33,1},{34,2},{35,3},{36,4},{37,5},{38,6},{39,7},{40,8},{41... | collective-permute-start | bytes 414728 | tf_op jit(solution)/shard_map/ppermute | solution.py:636
  20.0 30.8 %collective-permute-start.4 = (bf16[1,3,144,160]{3,2,1,0:T(8,128)(2,1)S(1)}, bf16[1,3,144,160]{3,2,1,0:T(8,128)(2,1)S(1)}, u32[]{:S(2)}, u32[]{:S(2)}) collective-permute-start(bf16[1,3,144,160]{3,2,1,0:T(8,128)(2,1)S(1)} %get-tuple-element.100), channel_id=1, source_target_pairs={{1,0},{2,1},{3,2},{4,3},{5,4},{6,5},{7,6},{8,7},{9,8},{10,9},{11,1... | collective-permute-start | bytes 414728 | tf_op jit(solution)/shard_map/ppermute | solution.py:636
  21.6 29.2 %collective-permute-start.5 = (bf16[1,3,144,160]{3,2,1,0:T(8,128)(2,1)S(1)}, bf16[1,3,144,160]{3,2,1,0:T(8,128)(2,1)S(1)}, u32[]{:S(2)}, u32[]{:S(2)}) collective-permute-start(bf16[1,3,144,160]{3,2,1,0:T(8,128)(2,1)S(1)} %get-tuple-element.99), channel_id=1, source_target_pairs={{33,0},{34,1},{35,2},{36,3},{37,4},{38,5},{39,6},{40,7},{41,8},{42... | collective-permute-start | bytes 414728 | tf_op jit(solution)/shard_map/ppermute | solution.py:636
  28.1 1.1 copy-start
  51.1 0.9 copy-start.3
  85.8 48.3 %all-to-all-start = ((bf16[128,88,128]{2,1,0:T(8,128)(2,1)}), bf16[128,88,128]{2,1,0:T(8,128)(2,1)S(1)}, u32[]{:S(2)}, u32[]{:S(2)}) async-start(bf16[128,88,128]{2,1,0:T(8,128)(2,1)} %bitcast.19), calls=%async_computation | async-start | bytes 5767168 | tf_op jit(solution)/shard_map/all_to_all | solution.py:776
  126.6 2.2 %collective-permute-start.6 = (bf16[2048,128]{1,0:T(8,128)(2,1)}, bf16[2048,128]{1,0:T(8,128)(2,1)S(1)}, u32[]{:S(2)}, u32[]{:S(2)}) collective-permute-start(bf16[2048,128]{1,0:T(8,128)(2,1)} %get-tuple-element.70), channel_id=1, source_target_pairs={{0,32},{32,0},{64,96},{96,64},{1,33},{33,1},{65,97},{97,65},{2,34}... | collective-permute-start | bytes 1572872 | tf_op jit(solution)/shard_map/ppermute | solution.py:780
  134.1 20.1 %all-to-all-start.1 = ((bf16[64,32,128]{2,1,0:T(8,128)(2,1)}), bf16[64,32,128]{2,1,0:T(8,128)(2,1)S(1)}, u32[]{:S(2)}, u32[]{:S(2)}) async-start(bf16[64,32,128]{2,1,0:T(8,128)(2,1)} %bitcast.20), calls=%async_computation.1 | async-start | bytes 1048576 | tf_op jit(solution)/shard_map/all_to_all | solution.py:786
  143.9 10.3 %copy-start.10 = (f32[8,1536]{1,0:T(8,128)S(1)}, f32[8,1536]{1,0:T(8,128)}, u32[]{:S(2)}) copy-start(f32[8,1536]{1,0:T(8,128)} %get-tuple-element.74.wup_ref) | copy-start | bytes 147460
  143.9 10.3 %copy-start.11 = (f32[8,1152]{1,0:T(8,128)S(1)}, f32[8,1152]{1,0:T(8,128)}, u32[]{:S(2)}) copy-start(f32[8,1152]{1,0:T(8,128)} %get-tuple-element.75.wqkv_ref) | copy-start | bytes 110596
  (1 other events, 0.9 us)
